TPU v7x, 128 devices: a whole 4x4x4 slice. The times are simulated.
128 devices in a mesh: dp: 32 (over y, z, x_hi), sp: 4 (over x_lo, core).
Axes of the slice: x: 4 (x_hi: 2, x_lo: 2; x = x_hi * 2 + x_lo), y: 4, z: 4, core: 2. Of those that a mesh axis runs over, the one named last changes fastest.
Arguments:
- queries: bfloat16 [16384, 2560], P(('dp', 'sp')), may hold values from -80 to 80
- key_rows: bfloat16 [16384, 2560], P(('dp', 'sp')), may hold values from -5 to 5
- value_rows: bfloat16 [16384, 2560], P(('dp', 'sp')), may hold values from -6 to 6
- cotangent: bfloat16 [16384, 2560], P(('dp', 'sp')), may hold values from -6 to 6
- lengths: int32 [32], replicated, may hold values from 1 to 512, 10240 in all
- sample_plan: int32 [32], replicated, may hold values from 0 to 31, each once
- guide_bins: int32 [32], replicated, may hold values from 0 to 7
- guide_table: float32 [8, 20], replicated, may hold values from 0.5 to 2
- block_source: int32 [16384], replicated, may hold values from 0 to 16383, as said below
Outputs:
- attn_out: bfloat16 [16384, 2560], P(('dp', 'sp'))
- grad_queries: bfloat16 [16384, 2560], P(('dp', 'sp'))
- grad_keys: bfloat16 [16384, 2560], P(('dp', 'sp'))
- grad_values: bfloat16 [16384, 2560], P(('dp', 'sp'))
Inputs may be any that keep to these rules, and one draw needn't show every extreme that they name: `lengths`: the longest sample has exactly 512 tokens. `sample_plan`: every group takes exactly one sample. `block_source`: a permutation; the 128 row blocks of the group order that one device holds come one from each device's loader rows, and each device's 128 loader row blocks go one to each device.
All inputs are finite; a program needn't handle non-finite values.
Results may differ from a plain program's by a relative error of at most 0.009.
Values may be sent and summed in bfloat16 or wider, within the bound.
No kernel may reach another device: no remote copies, remote signals or barrier semaphores. Data moves between devices by JAX's collectives and lax.ppermute only.
A program may use at most 64 MiB of HBM per device.

v0:
```python
import jax
import jax.numpy as jnp
from jax import lax
from jax.sharding import PartitionSpec as P

HEADS = 20
HD = 128


def head_pass(query_head, key_head, value_head, grad_head, query_live, key_live):
    scores = jnp.dot(query_head, key_head.T, preferred_element_type=jnp.float32) * HD ** (-0.5)
    masked = jnp.where(key_live[None, :], scores, -1e30)
    top_score = jnp.max(masked, axis=1, keepdims=True)
    shifted_exp = jnp.where(key_live[None, :], jnp.exp(masked - top_score), 0.0)
    row_total = jnp.sum(shifted_exp, axis=1, keepdims=True)
    attend = jnp.where(query_live[:, None], shifted_exp / row_total, 0.0)
    attend_bf = attend.astype(jnp.bfloat16)
    output = jnp.dot(attend_bf, value_head, preferred_element_type=jnp.float32)
    grad_attend = jnp.dot(grad_head, value_head.T, preferred_element_type=jnp.float32)
    row_dot = jnp.sum(grad_head.astype(jnp.float32) * output, axis=1, keepdims=True)
    grad_scores = (attend * (grad_attend - row_dot) * HD ** (-0.5)).astype(jnp.bfloat16)
    grad_query = jnp.dot(grad_scores, key_head, preferred_element_type=jnp.float32)
    grad_key = jnp.dot(grad_scores.T, query_head, preferred_element_type=jnp.float32)
    grad_value = jnp.dot(attend_bf.T, grad_head, preferred_element_type=jnp.float32)
    return (output, grad_query, grad_key, grad_value)


def head_stack(query_part, key_part, value_part, grad_part, query_live, key_live):

    def one_head(head_items):
        return head_pass(
            head_items[0], head_items[1], head_items[2], head_items[3], query_live, key_live
        )

    stacked = tuple(
        (jnp.moveaxis(source, 1, 0) for source in (query_part, key_part, value_part, grad_part))
    )
    return lax.map(one_head, stacked)


def dispatch(first, second, third):
    return (
        lax.all_to_all(first, ("dp", "sp"), split_axis=0, concat_axis=0, tiled=True),
        lax.all_to_all(second, ("dp", "sp"), split_axis=0, concat_axis=0, tiled=True),
        lax.all_to_all(third, ("dp", "sp"), split_axis=0, concat_axis=0, tiled=True),
    )


def send_back(first, second, third):
    return (
        lax.all_to_all(first, ("dp", "sp"), split_axis=0, concat_axis=0, tiled=True),
        lax.all_to_all(second, ("dp", "sp"), split_axis=0, concat_axis=0, tiled=True),
        lax.all_to_all(third, ("dp", "sp"), split_axis=0, concat_axis=0, tiled=True),
    )


def per_device(
    queries,
    key_rows,
    value_rows,
    cotangent,
    lengths,
    sample_plan,
    guide_bins,
    guide_table,
    block_source,
):
    n_dp = lax.axis_size("dp")
    n_sp = lax.axis_size("sp")
    loaders = n_dp * n_sp
    tok_rows = queries.shape[0]
    row_width = queries.shape[1]
    block_rows = tok_rows // loaders
    device_index = lax.axis_index("dp") * n_sp + lax.axis_index("sp")
    table = block_source.reshape(loaders, loaders)
    sources = table[device_index] // loaders
    send_slot = jnp.sum(jnp.where(table // loaders == device_index, table % loaders, 0), axis=1)
    slot_index = jnp.arange(loaders, dtype=jnp.int32)
    back_slot = jnp.sum(
        jnp.where(sources[None, :] == slot_index[:, None], slot_index[None, :], 0), axis=1
    )
    loader_slot = jnp.sum(
        jnp.where(send_slot[None, :] == slot_index[:, None], slot_index[None, :], 0), axis=1
    )

    def as_blocks(source, order):
        return source.reshape(loaders, block_rows, row_width)[order]

    recv_query, recv_key, recv_value = dispatch(
        as_blocks(queries, send_slot),
        as_blocks(key_rows, send_slot),
        as_blocks(value_rows, send_slot),
    )
    query_own = recv_query[sources].reshape(tok_rows, HEADS, HD)
    key_own = recv_key[sources].reshape(tok_rows, HEADS, HD)
    value_own = recv_value[sources].reshape(tok_rows, HEADS, HD)
    group_index = lax.axis_index("dp")
    picked = sample_plan == group_index
    group_len = jnp.sum(jnp.where(picked, lengths, 0))
    group_bin = jnp.sum(jnp.where(picked, guide_bins, 0))
    bin_match = jnp.arange(guide_table.shape[0], dtype=jnp.int32) == group_bin
    head_gate = jnp.sum(jnp.where(bin_match[:, None], guide_table, 0.0), axis=0)
    grad_own = (
        head_gate[None, :, None] * cotangent.reshape(tok_rows, HEADS, HD).astype(jnp.float32)
    ).astype(jnp.bfloat16)
    heads_dev = HEADS // n_sp
    split_shape = (tok_rows, n_sp, heads_dev, HD)
    group_items = (
        lax.all_to_all(
            query_own.reshape(split_shape), "sp", split_axis=1, concat_axis=0, tiled=True
        ),
        lax.all_to_all(key_own.reshape(split_shape), "sp", split_axis=1, concat_axis=0, tiled=True),
        lax.all_to_all(
            value_own.reshape(split_shape), "sp", split_axis=1, concat_axis=0, tiled=True
        ),
        lax.all_to_all(
            grad_own.reshape(split_shape), "sp", split_axis=1, concat_axis=0, tiled=True
        ),
    )
    flat_items = tuple((item[:, 0] for item in group_items))
    live_rows = jnp.arange(flat_items[0].shape[0], dtype=jnp.int32) < group_len
    results = head_stack(
        flat_items[0], flat_items[1], flat_items[2], flat_items[3], live_rows, live_rows
    )
    out_heads, gq_heads, gk_heads, gv_heads = tuple(
        (jnp.moveaxis(result, 0, 1)[:, None].astype(jnp.bfloat16) for result in results)
    )
    back_rows = (
        lax.all_to_all(out_heads, "sp", split_axis=0, concat_axis=1, tiled=True),
        lax.all_to_all(gq_heads, "sp", split_axis=0, concat_axis=1, tiled=True),
        lax.all_to_all(gk_heads, "sp", split_axis=0, concat_axis=1, tiled=True),
        lax.all_to_all(gv_heads, "sp", split_axis=0, concat_axis=1, tiled=True),
    )
    out_bf, grad_q_own, grad_k_own, grad_v_own = tuple(
        (part.reshape(tok_rows, HEADS, HD) for part in back_rows)
    )
    attn_out = (
        (head_gate[None, :, None] * lax.optimization_barrier(out_bf).astype(jnp.float32))
        .astype(jnp.bfloat16)
        .reshape(tok_rows, row_width)
    )
    back_query, back_key, back_value = send_back(
        as_blocks(grad_q_own, back_slot),
        as_blocks(grad_k_own, back_slot),
        as_blocks(grad_v_own, back_slot),
    )
    grad_queries = back_query[loader_slot].reshape(tok_rows, row_width)
    grad_keys = back_key[loader_slot].reshape(tok_rows, row_width)
    grad_values = back_value[loader_slot].reshape(tok_rows, row_width)
    return (attn_out, grad_queries, grad_keys, grad_values)


def solution(mesh):
    placed = (
        P(("dp", "sp"), None),
        P(("dp", "sp"), None),
        P(("dp", "sp"), None),
        P(("dp", "sp"), None),
        P(),
        P(),
        P(),
        P(),
        P(),
    )
    return jax.shard_map(
        per_device,
        mesh=mesh,
        in_specs=placed,
        out_specs=(
            P(("dp", "sp"), None),
            P(("dp", "sp"), None),
            P(("dp", "sp"), None),
            P(("dp", "sp"), None),
        ),
        check_vma=False,
    )
```

profile of v0, /device:TPU:1, one launch (start us, length us, event | category | flops | bytes accessed | tf_op | source)
XLA Modules:
  0.0 320.8 jit_solution(7268872180652038923)
XLA Ops:
  6.0 4.9 %all-to-all-start.6 = ((bf16[128,4,5,128]{0,3,2,1:T(8,128)(2,1)}), bf16[128,4,5,128]{0,3,2,1:T(8,128)(2,1)S(1)}, u32[]{:S(2)}, u32[]{:S(2)}) async-start(bf16[128,4,5,128]{0,3,2,1:T(8,128)(2,1)} %fusion.32), calls=%async_computation.6 | async-start | bytes 1310720 | tf_op jit(solution)/shard_map/all_to_all | solution.py:116
  14.6 5.6 %all-to-all-done.6 = bf16[128,4,5,128]{0,3,2,1:T(8,128)(2,1)S(1)} async-done(((bf16[128,4,5,128]{0,3,2,1:T(8,128)(2,1)}), bf16[128,4,5,128]{0,3,2,1:T(8,128)(2,1)S(1)}, u32[]{:S(2)}, u32[]{:S(2)}) %all-to-all-start.6) | async-done | bytes 655392 | tf_op jit(solution)/shard_map/all_to_all | solution.py:116
  20.3 11.3 %all-to-all-start = ((bf16[128,2,1280]{2,1,0:T(2,128)(2,1)}), bf16[128,2,1280]{2,1,0:T(2,128)(2,1)}, u32[]{:S(2)}, u32[]{:S(2)}) async-start(bf16[128,2,1280]{2,1,0:T(2,128)(2,1)} %reshape.324), calls=%async_computation | async-start | bytes 1310720 | tf_op jit(solution)/shard_map/all_to_all | solution.py:43
  34.7 11.8 %all-to-all-done = bf16[128,2,1280]{2,1,0:T(2,128)(2,1)} async-done(((bf16[128,2,1280]{2,1,0:T(2,128)(2,1)}), bf16[128,2,1280]{2,1,0:T(2,128)(2,1)}, u32[]{:S(2)}, u32[]{:S(2)}) %all-to-all-start) | async-done | bytes 655392 | tf_op jit(solution)/shard_map/all_to_all | solution.py:43
  46.5 4.5 %all-to-all-start.2 = ((bf16[128,2,1280]{2,1,0:T(2,128)(2,1)}), bf16[128,2,1280]{2,1,0:T(2,128)(2,1)S(1)}, u32[]{:S(2)}, u32[]{:S(2)}) async-start(bf16[128,2,1280]{2,1,0:T(2,128)(2,1)} %reshape.326), calls=%async_computation.2 | async-start | bytes 1310720 | tf_op jit(solution)/shard_map/all_to_all | solution.py:44
  54.0 12.1 %all-to-all-done.2 = bf16[128,2,1280]{2,1,0:T(2,128)(2,1)S(1)} async-done(((bf16[128,2,1280]{2,1,0:T(2,128)(2,1)}), bf16[128,2,1280]{2,1,0:T(2,128)(2,1)S(1)}, u32[]{:S(2)}, u32[]{:S(2)}) %all-to-all-start.2) | async-done | bytes 655392 | tf_op jit(solution)/shard_map/all_to_all | solution.py:44
  66.1 5.3 %all-to-all-start.4 = ((bf16[128,2,1280]{2,1,0:T(2,128)(2,1)}), bf16[128,2,1280]{2,1,0:T(2,128)(2,1)}, u32[]{:S(2)}, u32[]{:S(2)}) async-start(bf16[128,2,1280]{2,1,0:T(2,128)(2,1)} %reshape.328), calls=%async_computation.4 | async-start | bytes 1310720 | tf_op jit(solution)/shard_map/all_to_all | solution.py:45
  77.7 8.7 %all-to-all-done.4 = bf16[128,2,1280]{2,1,0:T(2,128)(2,1)} async-done(((bf16[128,2,1280]{2,1,0:T(2,128)(2,1)}), bf16[128,2,1280]{2,1,0:T(2,128)(2,1)}, u32[]{:S(2)}, u32[]{:S(2)}) %all-to-all-start.4) | async-done | bytes 655392 | tf_op jit(solution)/shard_map/all_to_all | solution.py:45
  86.3 5.0 %all-to-all-start.1 = ((bf16[128,4,5,128]{0,3,2,1:T(8,128)(2,1)}), bf16[128,4,5,128]{0,3,2,1:T(8,128)(2,1)}, u32[]{:S(2)}, u32[]{:S(2)}) async-start(bf16[128,4,5,128]{0,3,2,1:T(8,128)(2,1)} %bitcast.6), calls=%async_computation.1 | async-start | bytes 1310720 | tf_op jit(solution)/shard_map/all_to_all | solution.py:109
  94.0 6.8 %all-to-all-done.1 = bf16[128,4,5,128]{0,3,2,1:T(8,128)(2,1)} async-done(((bf16[128,4,5,128]{0,3,2,1:T(8,128)(2,1)}), bf16[128,4,5,128]{0,3,2,1:T(8,128)(2,1)}, u32[]{:S(2)}, u32[]{:S(2)}) %all-to-all-start.1) | async-done | bytes 655392 | tf_op jit(solution)/shard_map/all_to_all | solution.py:109
  100.8 5.0 %all-to-all-start.3 = ((bf16[128,4,5,128]{0,3,2,1:T(8,128)(2,1)}), bf16[128,4,5,128]{0,3,2,1:T(8,128)(2,1)}, u32[]{:S(2)}, u32[]{:S(2)}) async-start(bf16[128,4,5,128]{0,3,2,1:T(8,128)(2,1)} %bitcast.12), calls=%async_computation.3 | async-start | bytes 1310720 | tf_op jit(solution)/shard_map/all_to_all | solution.py:112
  123.6 5.5 %all-to-all-done.5 = bf16[128,4,5,128]{0,3,2,1:T(8,128)(2,1)S(1)} async-done(((bf16[128,4,5,128]{0,3,2,1:T(8,128)(2,1)}), bf16[128,4,5,128]{0,3,2,1:T(8,128)(2,1)S(1)}, u32[]{:S(2)}, u32[]{:S(2)}) %all-to-all-start.5) | async-done | bytes 655392 | tf_op jit(solution)/shard_map/all_to_all | solution.py:113
  130.1 48.1 %while.17 = (s32[]{:T(128)}, bf16[5,512,128]{2,1,0:T(8,128)(2,1)}, bf16[5,512,128]{2,1,0:T(8,128)(2,1)}, bf16[5,512,128]{2,1,0:T(8,128)(2,1)}, bf16[5,512,128]{2...) while((s32[]{:T(128)}, bf16[5,512,128]{2,1,0:T(8,128)(2,1)}, ...), condition=%wide.region_8.9_spmd.clone, body=%wide.region_4.8_spmd.clone.sunk | while | flops 409205760 | bytes 9994869 | solution.py:38
  180.8 4.5 %all-to-all-start.12 = ((bf16[512,1,5,128]{3,2,1,0:T(8,128)(2,1)}), bf16[512,1,5,128]{3,2,1,0:T(8,128)(2,1)S(1)}, u32[]{:S(2)}, u32[]{:S(2)}) async-start(bf16[512,1,5,128]{3,2,1,0:T(8,128)(2,1)} %copy.165), calls=%async_computation.12 | async-start | bytes 2097152 | tf_op jit(solution)/shard_map/all_to_all | solution.py:132
  186.8 12.1 %all-to-all-done.12 = bf16[512,1,5,128]{3,2,1,0:T(8,128)(2,1)S(1)} async-done(((bf16[512,1,5,128]{3,2,1,0:T(8,128)(2,1)}), bf16[512,1,5,128]{3,2,1,0:T(8,128)(2,1)S(1)}, u32[]{:S(2)}, u32[]{:S(2)}) %all-to-all-start.12) | async-done | bytes 655392 | tf_op jit(solution)/shard_map/all_to_all | solution.py:132
  205.7 12.1 %all-to-all-done.8 = bf16[512,1,5,128]{3,2,1,0:T(8,128)(2,1)S(1)} async-done(((bf16[512,1,5,128]{3,2,1,0:T(8,128)(2,1)}), bf16[512,1,5,128]{3,2,1,0:T(8,128)(2,1)S(1)}, u32[]{:S(2)}, u32[]{:S(2)}) %all-to-all-start.8) | async-done | bytes 655392 | tf_op jit(solution)/shard_map/all_to_all | solution.py:130
  217.9 4.4 %all-to-all-start.10 = ((bf16[512,1,5,128]{3,2,1,0:T(8,128)(2,1)}), bf16[512,1,5,128]{3,2,1,0:T(8,128)(2,1)S(1)}, u32[]{:S(2)}, u32[]{:S(2)}) async-start(bf16[512,1,5,128]{3,2,1,0:T(8,128)(2,1)} %copy.160), calls=%async_computation.10 | async-start | bytes 2097152 | tf_op jit(solution)/shard_map/all_to_all | solution.py:131
  223.7 12.1 %all-to-all-done.10 = bf16[512,1,5,128]{3,2,1,0:T(8,128)(2,1)S(1)} async-done(((bf16[512,1,5,128]{3,2,1,0:T(8,128)(2,1)}), bf16[512,1,5,128]{3,2,1,0:T(8,128)(2,1)S(1)}, u32[]{:S(2)}, u32[]{:S(2)}) %all-to-all-start.10) | async-done | bytes 655392 | tf_op jit(solution)/shard_map/all_to_all | solution.py:131
  249.0 4.8 %all-to-all-done.7 = bf16[512,1,5,128]{3,2,1,0:T(8,128)(2,1)S(1)} async-done(((bf16[512,1,5,128]{3,2,1,0:T(8,128)(2,1)}), bf16[512,1,5,128]{3,2,1,0:T(8,128)(2,1)S(1)}, u32[]{:S(2)}, u32[]{:S(2)}) %all-to-all-start.7) | async-done | bytes 655392 | tf_op jit(solution)/shard_map/all_to_all | solution.py:129
  253.8 5.3 %all-to-all-start.13 = ((bf16[128,2,1280]{2,1,0:T(2,128)(2,1)}), bf16[128,2,1280]{2,1,0:T(2,128)(2,1)}, u32[]{:S(2)}, u32[]{:S(2)}) async-start(bf16[128,2,1280]{2,1,0:T(2,128)(2,1)} %reshape.334), calls=%async_computation.13 | async-start | bytes 1310720 | tf_op jit(solution)/shard_map/all_to_all | solution.py:53
  267.8 6.3 %all-to-all-done.13 = bf16[128,2,1280]{2,1,0:T(2,128)(2,1)} async-done(((bf16[128,2,1280]{2,1,0:T(2,128)(2,1)}), bf16[128,2,1280]{2,1,0:T(2,128)(2,1)}, u32[]{:S(2)}, u32[]{:S(2)}) %all-to-all-start.13) | async-done | bytes 655392 | tf_op jit(solution)/shard_map/all_to_all | solution.py:53
  274.0 5.3 %all-to-all-start.9 = ((bf16[128,2,1280]{2,1,0:T(2,128)(2,1)}), bf16[128,2,1280]{2,1,0:T(2,128)(2,1)}, u32[]{:S(2)}, u32[]{:S(2)}) async-start(bf16[128,2,1280]{2,1,0:T(2,128)(2,1)} %reshape.330), calls=%async_computation.9 | async-start | bytes 1310720 | tf_op jit(solution)/shard_map/all_to_all | solution.py:51
  284.9 9.4 %all-to-all-done.9 = bf16[128,2,1280]{2,1,0:T(2,128)(2,1)} async-done(((bf16[128,2,1280]{2,1,0:T(2,128)(2,1)}), bf16[128,2,1280]{2,1,0:T(2,128)(2,1)}, u32[]{:S(2)}, u32[]{:S(2)}) %all-to-all-start.9) | async-done | bytes 655392 | tf_op jit(solution)/shard_map/all_to_all | solution.py:51
  294.3 5.5 %all-to-all-start.11 = ((bf16[128,2,1280]{2,1,0:T(2,128)(2,1)}), bf16[128,2,1280]{2,1,0:T(2,128)(2,1)}, u32[]{:S(2)}, u32[]{:S(2)}) async-start(bf16[128,2,1280]{2,1,0:T(2,128)(2,1)} %reshape.332), calls=%async_computation.11 | async-start | bytes 1310720 | tf_op jit(solution)/shard_map/all_to_all | solution.py:52
  (171 shorter events, 151.3 us)
Async XLA Ops:
  0.6 10.4 %copy-start = (bf16[128,2560]{1,0:T(8,128)(2,1)S(1)}, bf16[128,2560]{1,0:T(8,128)(2,1)}, u32[]{:S(2)}) copy-start(bf16[128,2560]{1,0:T(8,128)(2,1)} %param.11) | copy-start | bytes 1966084
  5.0 5.9 %copy-start.10 = (s32[16384]{0:T(1024)S(1)}, s32[16384]{0:T(1024)}, u32[]{:S(2)}) copy-start(s32[16384]{0:T(1024)} %param.19) | copy-start | bytes 196612
  6.0 14.3 %all-to-all-start.6 = ((bf16[128,4,5,128]{0,3,2,1:T(8,128)(2,1)}), bf16[128,4,5,128]{0,3,2,1:T(8,128)(2,1)S(1)}, u32[]{:S(2)}, u32[]{:S(2)}) async-start(bf16[128,4,5,128]{0,3,2,1:T(8,128)(2,1)} %fusion.32), calls=%async_computation.6 | async-start | bytes 1310720 | tf_op jit(solution)/shard_map/all_to_all | solution.py:116
  13.6 18.0 %copy-start.1 = (bf16[128,2560]{1,0:T(8,128)(2,1)S(1)}, bf16[128,2560]{1,0:T(8,128)(2,1)}, u32[]{:S(2)}) copy-start(bf16[128,2560]{1,0:T(8,128)(2,1)} %param.12) | copy-start | bytes 1966084
  20.3 26.2 %all-to-all-start = ((bf16[128,2,1280]{2,1,0:T(2,128)(2,1)}), bf16[128,2,1280]{2,1,0:T(2,128)(2,1)}, u32[]{:S(2)}, u32[]{:S(2)}) async-start(bf16[128,2,1280]{2,1,0:T(2,128)(2,1)} %reshape.324), calls=%async_computation | async-start | bytes 1310720 | tf_op jit(solution)/shard_map/all_to_all | solution.py:43
  33.7 17.2 %copy-start.2 = (bf16[128,2560]{1,0:T(8,128)(2,1)S(1)}, bf16[128,2560]{1,0:T(8,128)(2,1)}, u32[]{:S(2)}) copy-start(bf16[128,2560]{1,0:T(8,128)(2,1)} %param.13) | copy-start | bytes 1966084
  46.5 19.6 %all-to-all-start.2 = ((bf16[128,2,1280]{2,1,0:T(2,128)(2,1)}), bf16[128,2,1280]{2,1,0:T(2,128)(2,1)S(1)}, u32[]{:S(2)}, u32[]{:S(2)}) async-start(bf16[128,2,1280]{2,1,0:T(2,128)(2,1)} %reshape.326), calls=%async_computation.2 | async-start | bytes 1310720 | tf_op jit(solution)/shard_map/all_to_all | solution.py:44
  66.1 5.3 %copy-start.5 = (bf16[128,2,1280]{2,1,0:T(2,128)(2,1)}, bf16[128,2,1280]{2,1,0:T(2,128)(2,1)S(1)}, u32[]{:S(2)}) copy-start(bf16[128,2,1280]{2,1,0:T(2,128)(2,1)S(1)} %all-to-all-done.2) | copy-start | bytes 1966084
  66.1 20.3 %all-to-all-start.4 = ((bf16[128,2,1280]{2,1,0:T(2,128)(2,1)}), bf16[128,2,1280]{2,1,0:T(2,128)(2,1)}, u32[]{:S(2)}, u32[]{:S(2)}) async-start(bf16[128,2,1280]{2,1,0:T(2,128)(2,1)} %reshape.328), calls=%async_computation.4 | async-start | bytes 1310720 | tf_op jit(solution)/shard_map/all_to_all | solution.py:45
  76.6 14.8 %copy-start.6 = (bf16[128,2,1280]{2,1,0:T(2,128)(2,1)S(1)}, bf16[128,2,1280]{2,1,0:T(2,128)(2,1)}, u32[]{:S(2)}) copy-start(bf16[128,2,1280]{2,1,0:T(2,128)(2,1)} %copy-done.5) | copy-start | bytes 1966084
  86.3 14.5 %all-to-all-start.1 = ((bf16[128,4,5,128]{0,3,2,1:T(8,128)(2,1)}), bf16[128,4,5,128]{0,3,2,1:T(8,128)(2,1)}, u32[]{:S(2)}, u32[]{:S(2)}) async-start(bf16[128,4,5,128]{0,3,2,1:T(8,128)(2,1)} %bitcast.6), calls=%async_computation.1 | async-start | bytes 1310720 | tf_op jit(solution)/shard_map/all_to_all | solution.py:109
  100.8 14.5 %all-to-all-start.3 = ((bf16[128,4,5,128]{0,3,2,1:T(8,128)(2,1)}), bf16[128,4,5,128]{0,3,2,1:T(8,128)(2,1)}, u32[]{:S(2)}, u32[]{:S(2)}) async-start(bf16[128,4,5,128]{0,3,2,1:T(8,128)(2,1)} %bitcast.12), calls=%async_computation.3 | async-start | bytes 1310720 | tf_op jit(solution)/shard_map/all_to_all | solution.py:112
  115.3 13.7 %all-to-all-start.5 = ((bf16[128,4,5,128]{0,3,2,1:T(8,128)(2,1)}), bf16[128,4,5,128]{0,3,2,1:T(8,128)(2,1)S(1)}, u32[]{:S(2)}, u32[]{:S(2)}) async-start(bf16[128,4,5,128]{0,3,2,1:T(8,128)(2,1)} %bitcast.18), calls=%async_computation.5 | async-start | bytes 1310720 | tf_op jit(solution)/shard_map/all_to_all | solution.py:113
  180.8 4.5 %copy-start.8 = (bf16[5,512,128]{2,1,0:T(8,128)(2,1)S(1)}, bf16[5,512,128]{2,1,0:T(8,128)(2,1)}, u32[]{:S(2)}) copy-start(bf16[5,512,128]{2,1,0:T(8,128)(2,1)} %get-tuple-element.60) | copy-start | bytes 1966084
  180.8 18.1 %all-to-all-start.12 = ((bf16[512,1,5,128]{3,2,1,0:T(8,128)(2,1)}), bf16[512,1,5,128]{3,2,1,0:T(8,128)(2,1)S(1)}, u32[]{:S(2)}, u32[]{:S(2)}) async-start(bf16[512,1,5,128]{3,2,1,0:T(8,128)(2,1)} %copy.165), calls=%async_computation.12 | async-start | bytes 2097152 | tf_op jit(solution)/shard_map/all_to_all | solution.py:132
  186.8 17.5 %copy-start.9 = (bf16[5,512,128]{2,1,0:T(8,128)(2,1)S(1)}, bf16[5,512,128]{2,1,0:T(8,128)(2,1)}, u32[]{:S(2)}) copy-start(bf16[5,512,128]{2,1,0:T(8,128)(2,1)} %get-tuple-element.61) | copy-start | bytes 1966084
  199.9 18.0 %all-to-all-start.8 = ((bf16[512,1,5,128]{3,2,1,0:T(8,128)(2,1)}), bf16[512,1,5,128]{3,2,1,0:T(8,128)(2,1)S(1)}, u32[]{:S(2)}, u32[]{:S(2)}) async-start(bf16[512,1,5,128]{3,2,1,0:T(8,128)(2,1)} %copy.155), calls=%async_computation.8 | async-start | bytes 2097152 | tf_op jit(solution)/shard_map/all_to_all | solution.py:130
  205.7 16.5 %copy-start.7 = (bf16[5,512,128]{2,1,0:T(8,128)(2,1)S(1)}, bf16[5,512,128]{2,1,0:T(8,128)(2,1)}, u32[]{:S(2)}) copy-start(bf16[5,512,128]{2,1,0:T(8,128)(2,1)} %get-tuple-element.59) | copy-start | bytes 1966084
  217.9 5.8 %copy-start.3 = (bf16[512,1,5,128]{3,2,1,0:T(8,128)(2,1)}, bf16[512,1,5,128]{3,2,1,0:T(8,128)(2,1)S(1)}, u32[]{:S(2)}) copy-start(bf16[512,1,5,128]{3,2,1,0:T(8,128)(2,1)S(1)} %all-to-all-done.8) | copy-start | bytes 1966084
  217.9 18.0 %all-to-all-start.10 = ((bf16[512,1,5,128]{3,2,1,0:T(8,128)(2,1)}), bf16[512,1,5,128]{3,2,1,0:T(8,128)(2,1)S(1)}, u32[]{:S(2)}, u32[]{:S(2)}) async-start(bf16[512,1,5,128]{3,2,1,0:T(8,128)(2,1)} %copy.160), calls=%async_computation.10 | async-start | bytes 2097152 | tf_op jit(solution)/shard_map/all_to_all | solution.py:131
  235.8 18.0 %all-to-all-start.7 = ((bf16[512,1,5,128]{3,2,1,0:T(8,128)(2,1)}), bf16[512,1,5,128]{3,2,1,0:T(8,128)(2,1)S(1)}, u32[]{:S(2)}, u32[]{:S(2)}) async-start(bf16[512,1,5,128]{3,2,1,0:T(8,128)(2,1)} %copy.151), calls=%async_computation.7 | async-start | bytes 2097152 | tf_op jit(solution)/shard_map/all_to_all | solution.py:129
  253.8 20.3 %all-to-all-start.13 = ((bf16[128,2,1280]{2,1,0:T(2,128)(2,1)}), bf16[128,2,1280]{2,1,0:T(2,128)(2,1)}, u32[]{:S(2)}, u32[]{:S(2)}) async-start(bf16[128,2,1280]{2,1,0:T(2,128)(2,1)} %reshape.334), calls=%async_computation.13 | async-start | bytes 1310720 | tf_op jit(solution)/shard_map/all_to_all | solution.py:53
  274.0 20.3 %all-to-all-start.9 = ((bf16[128,2,1280]{2,1,0:T(2,128)(2,1)}), bf16[128,2,1280]{2,1,0:T(2,128)(2,1)}, u32[]{:S(2)}, u32[]{:S(2)}) async-start(bf16[128,2,1280]{2,1,0:T(2,128)(2,1)} %reshape.330), calls=%async_computation.9 | async-start | bytes 1310720 | tf_op jit(solution)/shard_map/all_to_all | solution.py:51
  294.3 20.5 %all-to-all-start.11 = ((bf16[128,2,1280]{2,1,0:T(2,128)(2,1)}), bf16[128,2,1280]{2,1,0:T(2,128)(2,1)}, u32[]{:S(2)}, u32[]{:S(2)}) async-start(bf16[128,2,1280]{2,1,0:T(2,128)(2,1)} %reshape.332), calls=%async_computation.11 | async-start | bytes 1310720 | tf_op jit(solution)/shard_map/all_to_all | solution.py:52
  (1 other events, 1.0 us)
where the time goes:
time: 323 us; the launch traced here: 321 us
  waiting for transfers between devices  112 us (35%)
  local copies, waits for them, and re-layouts  82.1 us (25%)
  starting transfers between devices  73.9 us (23%)
  matrix products  34.7 us (11%)
  other arithmetic  17.2 us (5%)
    unnamed x42, local copies, waits for them, and re-layouts  30.9 us
    all_to_all x1, waiting for transfers between devices, per_device(): lax.all_to_all(gk_heads, 'sp', split_axis=0, concat_axis=1, tiled=True)  12.1 us
    all_to_all x1, waiting for transfers between devices, per_device(): lax.all_to_all(gq_heads, 'sp', split_axis=0, concat_axis=1, tiled=True)  12.1 us
    all_to_all x1, waiting for transfers between devices, per_device(): lax.all_to_all(gv_heads, 'sp', split_axis=0, concat_axis=1, tiled=True)  12.1 us
    all_to_all x1, waiting for transfers between devices, dispatch(): lax.all_to_all(second, ('dp', 'sp'), split_axis=0, concat_axis=0, tiled=T...  12.1 us
    all_to_all x1, waiting for transfers between devices, dispatch(): lax.all_to_all(first, ('dp', 'sp'), split_axis=0, concat_axis=0, tiled=True)  11.8 us
    all_to_all x1, starting transfers between devices, dispatch(): lax.all_to_all(first, ('dp', 'sp'), split_axis=0, concat_axis=0, tiled=True)  11.3 us
    dot_general x5, matrix products, head_pass(): jnp.dot(attend_bf.T, grad_head, preferred_element_type=jnp.float32)  9.67 us
  transfers between devices with their start and end apart: 14, of which 14 were waited for; matrix products, arithmetic and copies ran while one was open for 22% of the time, Pallas kernels for 0%

commit v1 on v0

v1 whole, which is shorter than its diff:
```python
import functools

import jax
import jax.numpy as jnp
from jax import lax
from jax.experimental import pallas as pl
from jax.experimental.pallas import tpu as pltpu
from jax.sharding import PartitionSpec as P

HEADS = 20
HD = 128
N_DP = 32
N_SP = 4
LOADERS = N_DP * N_SP
ROWS = 128
GROUP = 512
HEADS_DEV = HEADS // N_SP
WIDTH = HEADS * HD
PART = HEADS_DEV * HD
SCALE = HD ** (-0.5)
LOG2E = 1.4426950408889634
BF = jnp.bfloat16
F32 = jnp.float32
UNITS = 4
CHUNK = 16 * UNITS
VMEM_LIMIT = 48 * 1024 * 1024


def dot(a, b):
    return jnp.dot(a, b, preferred_element_type=F32)


def dot_nt(a, b):
    return lax.dot_general(a, b, (((1,), (1,)), ((), ())), preferred_element_type=F32)


def dot_tn(a, b):
    return lax.dot_general(a, b, (((0,), (0,)), ((), ())), preferred_element_type=F32)


def swap16():
    row = lax.broadcasted_iota(jnp.int32, (256, 256), 0)
    col = lax.broadcasted_iota(jnp.int32, (256, 256), 1)
    return jnp.where(col == (row % 16) * 16 + row // 16, 1.0, 0.0).astype(BF)


def combos(unit):
    for place in range(4):
        index = unit * 4 + place
        if index < 3 * HEADS_DEV:
            yield place, index // HEADS_DEV, index % HEADS_DEV


def row_picker(table_ref, me):
    table = table_ref[...]
    slot = jnp.sum(jnp.where(table // ROWS == me, table % ROWS, 0), axis=1, keepdims=True)
    lane = lax.broadcasted_iota(jnp.int32, (LOADERS, ROWS), 1)
    row = lax.broadcasted_iota(jnp.int32, (LOADERS, ROWS), 0)
    pick = jnp.where(slot == lane, 1.0, 0.0).astype(BF)
    order = jnp.where(lane == (row % N_DP) * N_SP + row // N_DP, 1.0, 0.0).astype(BF)
    return dot(order, pick).astype(BF)


def source_onehot(table_row):
    loader = lax.broadcasted_iota(jnp.int32, (LOADERS, ROWS), 0)
    return jnp.where(table_row // ROWS == loader, 1.0, 0.0).astype(BF)


def pack_kernel(me_ref, table_ref, q_ref, k_ref, v_ref, send_ref, rows_ref):
    pick = row_picker(table_ref, me_ref[0])
    for array, ref in enumerate((q_ref, k_ref, v_ref)):
        rows_ref[array] = dot(pick, ref[...]).astype(BF)
    swap = swap16()
    for part in range(N_SP):
        for half in range(2):
            blocks = []
            for unit in range(UNITS):
                pieces = []
                for _, array, head in combos(unit):
                    lanes = pl.ds((part * HEADS_DEV + head) * HD, HD)
                    for quarter in range(4):
                        pieces.append(rows_ref[array, pl.ds(quarter * N_DP + half * 16, 16), lanes])
                if len(pieces) < 16:
                    pieces.append(jnp.zeros((256 - 16 * len(pieces), HD), BF))
                blocks.append(jnp.concatenate(pieces, axis=0))
            for pair in range(UNITS // 2):
                both = jnp.concatenate(blocks[2 * pair : 2 * pair + 2], axis=1)
                swapped = dot(swap, both).astype(BF)
                for side in range(2):
                    unit = 2 * pair + side
                    for group in range(16):
                        send_ref[(half * 16 + group) * N_SP + part, pl.ds(unit * 16, 16), :] = swapped[
                            group * 16 : (group + 1) * 16, side * HD : (side + 1) * HD
                        ]


def unpack_kernel(me_ref, table_ref, recv_ref, q_ref, k_ref, v_ref, rows_ref):
    pick = row_picker(table_ref, me_ref[0])
    swap = swap16()
    for part in range(N_SP):
        for half in range(2):
            for pair in range(UNITS // 2):
                blocks = []
                for side in range(2):
                    unit = 2 * pair + side
                    blocks.append(
                        jnp.concatenate(
                            [
                                recv_ref[(half * 16 + group) * N_SP + part, pl.ds(unit * 16, 16), :]
                                for group in range(16)
                            ],
                            axis=0,
                        )
                    )
                swapped = dot(swap, jnp.concatenate(blocks, axis=1)).astype(BF)
                for side in range(2):
                    for place, array, head in combos(2 * pair + side):
                        lanes = pl.ds((part * HEADS_DEV + head) * HD, HD)
                        for quarter in range(4):
                            at = (place * 4 + quarter) * 16
                            rows_ref[array, pl.ds(quarter * N_DP + half * 16, 16), lanes] = swapped[
                                at : at + 16, side * HD : (side + 1) * HD
                            ]
    for array, ref in enumerate((q_ref, k_ref, v_ref)):
        ref[...] = dot_tn(pick, rows_ref[array]).astype(BF)


def part_lanes(index):
    return pl.ds(pl.multiple_of(index * PART, HD), PART)


def spread_kernel(me_ref, table_ref, cot_ref, *out_refs):
    me = me_ref[0]
    onehot = source_onehot(table_ref[pl.ds(me, 1), :])
    for step in range(N_SP):
        other = jnp.bitwise_xor(me % N_SP, step)
        out_refs[step][...] = dot(onehot, cot_ref[:, part_lanes(other)]).astype(BF)


def collect_kernel(me_ref, table_ref, *refs):
    in_refs, out_ref = refs[:-1], refs[-1]
    me = me_ref[0]
    onehot = source_onehot(table_ref[pl.ds(me, 1), :])
    for step in range(N_SP):
        other = jnp.bitwise_xor(me % N_SP, step)
        out_ref[:, part_lanes(other)] = dot_tn(onehot, in_refs[step][...]).astype(BF)


def attend_kernel(
    me_ref,
    lengths_ref,
    plan_ref,
    bins_ref,
    guide_ref,
    table_ref,
    recv_ref,
    d0_ref,
    d1_ref,
    d2_ref,
    d3_ref,
    ret_ref,
    o0_ref,
    o1_ref,
    o2_ref,
    o3_ref,
    items_ref,
    cot_ref,
    out_ref,
    bias_ref,
    live_ref,
):
    me = me_ref[0]
    group = me // N_SP
    mine = me % N_SP
    group_len = jnp.int32(0)
    group_bin = jnp.int32(0)
    for sample in range(N_DP):
        hit = plan_ref[sample] == group
        group_len = jnp.where(hit, lengths_ref[sample], group_len)
        group_bin = jnp.where(hit, bins_ref[sample], group_bin)
    for quarter in range(4):
        onehot = source_onehot(table_ref[pl.ds(group * N_SP + quarter, 1), :])
        lane = lax.broadcasted_iota(jnp.int32, (LOADERS, ROWS), 1).astype(F32)
        limit = (group_len - quarter * ROWS).astype(F32)
        where_col = jnp.sum(onehot.astype(F32) * lane, axis=1, keepdims=True)
        where_row = dot_nt(lane[:8].astype(BF), onehot)
        bias_ref[pl.ds(quarter * ROWS, ROWS), :] = jnp.broadcast_to(
            jnp.where(where_col < limit, 0.0, -1e30), (ROWS, HD)
        )
        live_ref[:, pl.ds(quarter * ROWS, ROWS)] = jnp.where(where_row < limit, 1.0, 0.0)
    for step, ref in enumerate((d0_ref, d1_ref, d2_ref, d3_ref)):
        source = jnp.bitwise_xor(mine, step)
        cot_ref[pl.ds(pl.multiple_of(source * ROWS, ROWS), ROWS), :] = ref[...]
    swap = swap16()
    for block in range(8):
        for pair in range(UNITS // 2):
            both = jnp.concatenate(
                [
                    recv_ref[pl.ds(block * 16, 16), pl.ds((2 * pair + side) * 16, 16), :].reshape(256, HD)
                    for side in range(2)
                ],
                axis=1,
            )
            swapped = dot(swap, both).astype(BF)
            for side in range(2):
                unit = 2 * pair + side
                for place in range(4):
                    for quarter in range(4):
                        at = (place * 4 + quarter) * 16
                        items_ref[unit * 4 + place, pl.ds(quarter * ROWS + block * 16, 16), :] = swapped[
                            at : at + 16, side * HD : (side + 1) * HD
                        ]
    live = live_ref[0:1, :]
    bias = bias_ref[:, 0:1]
    for head in range(HEADS_DEV):
        gate = guide_ref[group_bin, mine * HEADS_DEV + head]
        query = items_ref[head]
        key = items_ref[HEADS_DEV + head]
        value = items_ref[2 * HEADS_DEV + head]
        lanes = pl.ds(head * HD, HD)
        grad = (gate * cot_ref[:, lanes].astype(F32)).astype(BF)
        scores = dot_nt(key, query) + bias
        top = jnp.max(scores, axis=0, keepdims=True)
        raised = jnp.exp2((scores - top) * (SCALE * LOG2E))
        attend = raised * (live / jnp.sum(raised, axis=0, keepdims=True))
        attend_bf = attend.astype(BF)
        output = dot_tn(attend_bf, value)
        grad_attend = dot_nt(value, grad)
        row_dot = jnp.sum((grad.astype(F32) * output).T, axis=0, keepdims=True)
        grad_scores = (attend * (grad_attend - row_dot) * SCALE).astype(BF)
        out_ref[:, lanes] = (gate * output.astype(BF).astype(F32)).astype(BF)
        items_ref[2 * HEADS_DEV + head] = dot(attend_bf, grad).astype(BF)
        items_ref[head] = dot_tn(grad_scores, key).astype(BF)
        items_ref[HEADS_DEV + head] = dot(grad_scores, query).astype(BF)
    for step, ref in enumerate((o0_ref, o1_ref, o2_ref, o3_ref)):
        target = jnp.bitwise_xor(mine, step)
        ref[...] = out_ref[pl.ds(pl.multiple_of(target * ROWS, ROWS), ROWS), :]
    for block in range(8):
        for pair in range(UNITS // 2):
            both = jnp.concatenate(
                [
                    jnp.concatenate(
                        [
                            items_ref[
                                (2 * pair + side) * 4 + place, pl.ds(quarter * ROWS + block * 16, 16), :
                            ]
                            for place in range(4)
                            for quarter in range(4)
                        ],
                        axis=0,
                    )
                    for side in range(2)
                ],
                axis=1,
            )
            swapped = dot(swap, both).astype(BF)
            for side in range(2):
                ret_ref[pl.ds(block * 16, 16), pl.ds((2 * pair + side) * 16, 16), :] = swapped[
                    :, side * HD : (side + 1) * HD
                ].reshape(16, 16, HD)


SMEM = pl.BlockSpec(memory_space=pltpu.SMEM)
VMEM = pl.BlockSpec(memory_space=pltpu.VMEM)
PARAMS = pltpu.CompilerParams(vmem_limit_bytes=VMEM_LIMIT)
CHUNKS = jax.ShapeDtypeStruct((LOADERS, CHUNK, HD), BF)
PIECE = jax.ShapeDtypeStruct((ROWS, PART), BF)
WHOLE = jax.ShapeDtypeStruct((ROWS, WIDTH), BF)


def pack(me, table, queries, keys, values):
    return pl.pallas_call(
        pack_kernel,
        out_shape=CHUNKS,
        in_specs=[SMEM] + [VMEM] * 4,
        out_specs=VMEM,
        scratch_shapes=[pltpu.VMEM((3, ROWS, WIDTH), BF)],
        compiler_params=PARAMS,
        name="pack",
    )(me, table, queries, keys, values)


def unpack(me, table, chunks):
    return pl.pallas_call(
        unpack_kernel,
        out_shape=(WHOLE,) * 3,
        in_specs=[SMEM] + [VMEM] * 2,
        out_specs=(VMEM,) * 3,
        scratch_shapes=[pltpu.VMEM((3, ROWS, WIDTH), BF)],
        compiler_params=PARAMS,
        name="unpack",
    )(me, table, chunks)


def spread(me, table, cotangent):
    return pl.pallas_call(
        spread_kernel,
        out_shape=(PIECE,) * N_SP,
        in_specs=[SMEM] + [VMEM] * 2,
        out_specs=(VMEM,) * N_SP,
        compiler_params=PARAMS,
        name="spread",
    )(me, table, cotangent)


def collect(me, table, pieces):
    return pl.pallas_call(
        collect_kernel,
        out_shape=WHOLE,
        in_specs=[SMEM] + [VMEM] * (1 + N_SP),
        out_specs=VMEM,
        compiler_params=PARAMS,
        name="collect",
    )(me, table, *pieces)


def attend(me, lengths, plan, bins, guide, table, chunks, pieces):
    return pl.pallas_call(
        attend_kernel,
        out_shape=(CHUNKS,) + (PIECE,) * N_SP,
        in_specs=[SMEM] * 5 + [VMEM] * (2 + N_SP),
        out_specs=(VMEM,) * (1 + N_SP),
        scratch_shapes=[
            pltpu.VMEM((16, GROUP, HD), BF),
            pltpu.VMEM((GROUP, PART), BF),
            pltpu.VMEM((GROUP, PART), BF),
            pltpu.VMEM((GROUP, HD), F32),
            pltpu.VMEM((8, GROUP), F32),
        ],
        compiler_params=PARAMS,
        name="attend",
    )(me, lengths, plan, bins, guide, table, chunks, *pieces)


def exchange(chunks):
    return lax.all_to_all(chunks, ("dp", "sp"), split_axis=0, concat_axis=0, tiled=True)


def swap_pieces(pieces):
    moved = [pieces[0]]
    for step in range(1, N_SP):
        moved.append(lax.ppermute(pieces[step], "sp", [(i, i ^ step) for i in range(N_SP)]))
    return moved


def per_device(
    queries,
    key_rows,
    value_rows,
    cotangent,
    lengths,
    sample_plan,
    guide_bins,
    guide_table,
    block_source,
):
    me = (lax.axis_index("dp") * N_SP + lax.axis_index("sp")).astype(jnp.int32).reshape(1)
    table = block_source.reshape(LOADERS, ROWS)
    grad_pieces = swap_pieces(spread(me, table, cotangent))
    chunks = exchange(pack(me, table, queries, key_rows, value_rows))
    results = attend(
        me, lengths, sample_plan, guide_bins, guide_table, table, chunks, grad_pieces
    )
    out_pieces = swap_pieces(results[1:])
    back = exchange(results[0])
    grad_queries, grad_keys, grad_values = unpack(me, table, back)
    attn_out = collect(me, table, out_pieces)
    return attn_out, grad_queries, grad_keys, grad_values


def solution(mesh):
    rows = P(("dp", "sp"), None)
    return jax.shard_map(
        per_device,
        mesh=mesh,
        in_specs=(rows,) * 4 + (P(),) * 5,
        out_specs=(rows,) * 4,
        check_vma=False,
    )
```

time: 323 us -> 106 us (0.33)
  local copies, waits for them, and re-layouts: 82.1 us -> 6.79 us
  waiting for transfers between devices: 112 us -> 56.8 us
  starting transfers between devices: 73.9 us -> 26.1 us
  matrix products: 34.7 us -> 0 us
  other arithmetic: 17.2 us -> 0 us
  Pallas kernels: 0 us -> 15.1 us
    all_to_all x14 -> x2, waiting for transfers between devices: 112 us -> 0.01 us  [exchange(): lax.all_to_all(chunks, ('dp', 'sp'), split_axis=0, concat_axis=0, tiled=T...]
    ppermute x0 -> x6, waiting for transfers between devices: none -> 56.8 us  [swap_pieces(): lax.ppermute(pieces[step], 'sp', [(i, i ^ step) for i in range(N_SP)])]
    all_to_all x14 -> x2, starting transfers between devices: 73.9 us -> 20.3 us  [exchange(): lax.all_to_all(chunks, ('dp', 'sp'), split_axis=0, concat_axis=0, tiled=T...]
    dot_general x30 -> x0, matrix products: 34.7 us -> none  [the longest x5 9.67 us: head_pass(): jnp.dot(attend_bf.T, grad_head, preferred_element_type=jnp.float32)]
    unnamed x42 -> x24, local copies, waits for them, and re-layouts: 30.9 us -> 6.79 us
    gather x16 -> x0, local copies, waits for them, and re-layouts: 19.6 us -> none  [the longest x7 8.04 us: as_blocks(): return source.reshape(loaders, block_rows, row_width)[order]]
    pallas_call x0 -> x5, Pallas kernels: none -> 15.1 us  [the longest x1 9.76 us: attend(): pl.pallas_call(attend_kernel, out_shape=(CHUNKS,) + (PIECE,) * N_SP, in_s...]
    all_to_all x12 -> x0, local copies, waits for them, and re-layouts: 11.1 us -> none  [the longest x2 2.4 us: per_device(): lax.all_to_all(gq_heads, 'sp', split_axis=0, concat_axis=1, tiled=True)]
  transfers between devices with their start and end apart: 14 -> 8, of which waited for: 14 -> 4; matrix products, arithmetic and copies ran while one was open for 22% -> 0% of each run, Pallas kernels for 0% -> 1%
where the time goes in v1:
time: 106 us
  waiting for transfers between devices  56.8 us (54%)
  starting transfers between devices  26.1 us (25%)
  Pallas kernels  15.1 us (14%)
  local copies, waits for them, and re-layouts  6.79 us (6%)
    ppermute x6, waiting for transfers between devices, swap_pieces(): lax.ppermute(pieces[step], 'sp', [(i, i ^ step) for i in range(N_SP)])  56.8 us
    all_to_all x2, starting transfers between devices, exchange(): lax.all_to_all(chunks, ('dp', 'sp'), split_axis=0, concat_axis=0, tiled=T...  20.3 us
    pallas_call x1, Pallas kernels, attend(): pl.pallas_call(attend_kernel, out_shape=(CHUNKS,) + (PIECE,) * N_SP, in_s...  9.76 us
    unnamed x24, local copies, waits for them, and re-layouts  6.79 us
    ppermute x6, starting transfers between devices, swap_pieces(): lax.ppermute(pieces[step], 'sp', [(i, i ^ step) for i in range(N_SP)])  5.74 us
    pallas_call x1, Pallas kernels, unpack(): pl.pallas_call(unpack_kernel, out_shape=(WHOLE,) * 3, in_specs=[SMEM] + [...  2.29 us
  transfers between devices with their start and end apart: 8, of which 4 were waited for; matrix products, arithmetic and copies ran while one was open for 0% of the time, Pallas kernels for 1%

profile of v1, /device:TPU:1, one launch (start us, length us, event | category | flops | bytes accessed | tf_op | source)
XLA Modules:
  0.0 105.5 jit_solution(2771008822684047435)
XLA Ops:
  0.6 0.0 copy-start.2
  0.6 0.8 copy-done.2
  1.5 1.1 %copy-done.4 = bf16[128,2560]{1,0:T(8,128)(2,1)S(1)} copy-done((bf16[128,2560]{1,0:T(8,128)(2,1)S(1)}, bf16[128,2560]{1,0:T(8,128)(2,1)}, u32[]{:S(2)}) %copy-start.4) | copy-done | bytes 655384
  2.6 1.1 %copy-done.5 = bf16[128,2560]{1,0:T(8,128)(2,1)S(1)} copy-done((bf16[128,2560]{1,0:T(8,128)(2,1)S(1)}, bf16[128,2560]{1,0:T(8,128)(2,1)}, u32[]{:S(2)}) %copy-start.5) | copy-done | bytes 655384
  3.7 1.1 %copy-done.6 = bf16[128,2560]{1,0:T(8,128)(2,1)S(1)} copy-done((bf16[128,2560]{1,0:T(8,128)(2,1)S(1)}, bf16[128,2560]{1,0:T(8,128)(2,1)}, u32[]{:S(2)}) %copy-start.6) | copy-done | bytes 655384
  4.7 1.5 %pack.1 = bf16[128,64,128]{2,1,0:T(8,128)(2,1)S(1)} custom-call(s32[1]{0:T(128)} %bitcast.me_ref, s32[128,128]{1,0:T(8,128)S(1)} %bitcast.2, bf16[128,2560]{1,0:T(8,128)(2,1)S(1)} %copy-done.4, bf16[128,2560]{1,0:T(8,128)(2,1)S(1)} %copy-done.5, bf16[128,2560]{1,0:T(8,128)(2,1)S(1)} %copy-done.6), custom_call_target="tpu_custom_call" | custom-call | tf_op jit(solution)/shard_map/pack/pallas_call | solution.py:272
  6.2 1.3 %copy-done = bf16[128,64,128]{2,1,0:T(8,128)(2,1)} copy-done((bf16[128,64,128]{2,1,0:T(8,128)(2,1)}, bf16[128,64,128]{2,1,0:T(8,128)(2,1)S(1)}, u32[]{:S(2)}) %copy-start) | copy-done | bytes 2097176
  7.6 11.5 %all-to-all-start = ((bf16[128,64,128]{2,1,0:T(8,128)(2,1)}), bf16[128,64,128]{2,1,0:T(8,128)(2,1)S(1)}, u32[]{:S(2)}, u32[]{:S(2)}) async-start(bf16[128,64,128]{2,1,0:T(8,128)(2,1)} %copy-done), calls=%async_computation | async-start | bytes 4194304 | tf_op jit(solution)/shard_map/all_to_all | solution.py:336
  19.1 0.3 spread.1
  19.5 1.1 %collective-permute-start = (bf16[128,640]{1,0:T(8,128)(2,1)S(1)}, bf16[128,640]{1,0:T(8,128)(2,1)S(1)}, u32[]{:S(2)}, u32[]{:S(2)}) collective-permute-start(bf16[128,640]{1,0:T(8,128)(2,1)S(1)} %get-tuple-element.17), channel_id=1, source_target_pairs={{0,1},{1,0},{2,3},{3,2},{4,5},{5,4},{6,7},{7,6},{8,9},{9,8},{10,11... | collective-permute-start | bytes 491528 | tf_op jit(solution)/shard_map/ppermute | solution.py:342
  20.6 0.7 collective-permute-start.1
  21.3 1.0 collective-permute-start.2
  22.4 24.2 %collective-permute-done.1.d2_ref = bf16[128,640]{1,0:T(8,128)(2,1)S(1)} collective-permute-done((bf16[128,640]{1,0:T(8,128)(2,1)S(1)}, bf16[128,640]{1,0:T(8,128)(2,1)S(1)}, u32[]{:S(2)}, u32[]{:S(2)}) %collective-permute-start.1) | collective-permute-done | bytes 163872 | tf_op jit(solution)/shard_map/ppermute | solution.py:342
  46.6 4.0 %collective-permute-done.2.d3_ref = bf16[128,640]{1,0:T(8,128)(2,1)S(1)} collective-permute-done((bf16[128,640]{1,0:T(8,128)(2,1)S(1)}, bf16[128,640]{1,0:T(8,128)(2,1)S(1)}, u32[]{:S(2)}, u32[]{:S(2)}) %collective-permute-start.2) | collective-permute-done | bytes 163872 | tf_op jit(solution)/shard_map/ppermute | solution.py:342
  50.6 9.8 %attend.1 = (bf16[128,64,128]{2,1,0:T(8,128)(2,1)S(1)}, bf16[128,640]{1,0:T(8,128)(2,1)S(1)}, bf16[128,640]{1,0:T(8,128)(2,1)S(1)}, bf16[128,640]{1,0:T(8,128)(2,1)S(1)}, bf16[128,640]{1,0:T(8,128)(2,1)S(1)}) custom-call(s32[1]{0:T(128)} %bitcast.me_ref, s32[32]{0:T(128)S(1)} %copy-done.9, s32[32]{0:T(128)S(1)} %copy-done.10, s32[32]{0:T(128)S(1)} %copy-done.11, ...), custom_call_target="tpu_custom_call" | custom-call | tf_op jit(solution)/shard_map/attend/pallas_call | solution.py:318
  60.4 1.3 %copy-done.1 = bf16[128,64,128]{2,1,0:T(8,128)(2,1)} copy-done((bf16[128,64,128]{2,1,0:T(8,128)(2,1)}, bf16[128,64,128]{2,1,0:T(8,128)(2,1)S(1)}, u32[]{:S(2)}) %copy-start.1) | copy-done | bytes 2097176
  61.7 8.8 %all-to-all-start.1 = ((bf16[128,64,128]{2,1,0:T(8,128)(2,1)}), bf16[128,64,128]{2,1,0:T(8,128)(2,1)S(1)}, u32[]{:S(2)}, u32[]{:S(2)}) async-start(bf16[128,64,128]{2,1,0:T(8,128)(2,1)} %copy-done.1), calls=%async_computation.1 | async-start | bytes 4194304 | tf_op jit(solution)/shard_map/all_to_all | solution.py:336
  70.6 1.1 %collective-permute-start.3 = (bf16[128,640]{1,0:T(8,128)(2,1)S(1)}, bf16[128,640]{1,0:T(8,128)(2,1)S(1)}, u32[]{:S(2)}, u32[]{:S(2)}) collective-permute-start(bf16[128,640]{1,0:T(8,128)(2,1)S(1)} %get-tuple-element.21), channel_id=1, source_target_pairs={{0,1},{1,0},{2,3},{3,2},{4,5},{5,4},{6,7},{7,6},{8,9},{9,8},{10,11... | collective-permute-start | bytes 491528 | tf_op jit(solution)/shard_map/ppermute | solution.py:342
  71.7 0.7 collective-permute-start.4
  72.4 1.0 collective-permute-start.5
  73.4 24.6 %collective-permute-done.4.refs_2_ = bf16[128,640]{1,0:T(8,128)(2,1)S(1)} collective-permute-done((bf16[128,640]{1,0:T(8,128)(2,1)S(1)}, bf16[128,640]{1,0:T(8,128)(2,1)S(1)}, u32[]{:S(2)}, u32[]{:S(2)}) %collective-permute-start.4) | collective-permute-done | bytes 163872 | tf_op jit(solution)/shard_map/ppermute | solution.py:342
  98.0 4.0 %collective-permute-done.5.refs_3_ = bf16[128,640]{1,0:T(8,128)(2,1)S(1)} collective-permute-done((bf16[128,640]{1,0:T(8,128)(2,1)S(1)}, bf16[128,640]{1,0:T(8,128)(2,1)S(1)}, u32[]{:S(2)}, u32[]{:S(2)}) %collective-permute-start.5) | collective-permute-done | bytes 163872 | tf_op jit(solution)/shard_map/ppermute | solution.py:342
  102.0 1.2 %collect.1 = bf16[128,2560]{1,0:T(8,128)(2,1)} custom-call(s32[1]{0:T(128)} %bitcast.me_ref, s32[128,128]{1,0:T(8,128)S(1)} %bitcast.5, bf16[128,640]{1,0:T(8,128)(2,1)S(1)} %get-tuple-element.20.refs_0_, bf16[128,640]{1,0:T(8,128)(2,1)S(1)} %collective-permute-done.3.refs_1_, bf16[128,640]{1,0:T(8,128)(2,1)S(1)} %collective-permute-done.4.refs_2_, ...), custom_call_target="tpu_custom_call" | custom-call | tf_op jit(solution)/shard_map/collect/pallas_call | solution.py:307
  103.2 2.3 %unpack.1 = (bf16[128,2560]{1,0:T(8,128)(2,1)}, bf16[128,2560]{1,0:T(8,128)(2,1)}, bf16[128,2560]{1,0:T(8,128)(2,1)}) custom-call(s32[1]{0:T(128)} %bitcast.me_ref, s32[128,128]{1,0:T(8,128)S(1)} %bitcast.6, bf16[128,64,128]{2,1,0:T(8,128)(2,1)S(1)} %all-to-all-done.1.recv_ref), custom_call_target="tpu_custom_call" | custom-call | tf_op jit(solution)/shard_map/unpack/pallas_call | solution.py:284
  (21 shorter events, 0.0 us)
Async XLA Ops:
  0.6 0.8 copy-start.2
  1.5 1.1 %copy-start.4 = (bf16[128,2560]{1,0:T(8,128)(2,1)S(1)}, bf16[128,2560]{1,0:T(8,128)(2,1)}, u32[]{:S(2)}) copy-start(bf16[128,2560]{1,0:T(8,128)(2,1)} %q_ref.1) | copy-start | bytes 1966084
  2.6 1.1 %copy-start.5 = (bf16[128,2560]{1,0:T(8,128)(2,1)S(1)}, bf16[128,2560]{1,0:T(8,128)(2,1)}, u32[]{:S(2)}) copy-start(bf16[128,2560]{1,0:T(8,128)(2,1)} %k_ref.1) | copy-start | bytes 1966084
  3.7 1.1 %copy-start.6 = (bf16[128,2560]{1,0:T(8,128)(2,1)S(1)}, bf16[128,2560]{1,0:T(8,128)(2,1)}, u32[]{:S(2)}) copy-start(bf16[128,2560]{1,0:T(8,128)(2,1)} %v_ref.1) | copy-start | bytes 1966084
  6.2 1.3 %copy-start = (bf16[128,64,128]{2,1,0:T(8,128)(2,1)}, bf16[128,64,128]{2,1,0:T(8,128)(2,1)S(1)}, u32[]{:S(2)}) copy-start(bf16[128,64,128]{2,1,0:T(8,128)(2,1)S(1)} %pack.1) | copy-start | bytes 6291460
  7.6 11.6 %copy-start.3 = (s32[16384]{0:T(1024)S(1)}, s32[16384]{0:T(1024)}, u32[]{:S(2)}) copy-start(s32[16384]{0:T(1024)} %param.17) | copy-start | bytes 196612
  7.6 11.6 %copy-start.7 = (bf16[128,2560]{1,0:T(8,128)(2,1)S(1)}, bf16[128,2560]{1,0:T(8,128)(2,1)}, u32[]{:S(2)}) copy-start(bf16[128,2560]{1,0:T(8,128)(2,1)} %cot_ref.1) | copy-start | bytes 1966084
  7.6 43.0 %copy-start.8 = (f32[8,20]{1,0:T(8,128)S(1)}, f32[8,20]{1,0:T(8,128)}, u32[]{:S(2)}) copy-start(f32[8,20]{1,0:T(8,128)} %guide_ref.1) | copy-start | bytes 1924
  7.6 43.0 %copy-start.9 = (s32[32]{0:T(128)S(1)}, s32[32]{0:T(128)}, u32[]{:S(2)}) copy-start(s32[32]{0:T(128)} %lengths_ref.1) | copy-start | bytes 388
  7.6 43.0 %copy-start.10 = (s32[32]{0:T(128)S(1)}, s32[32]{0:T(128)}, u32[]{:S(2)}) copy-start(s32[32]{0:T(128)} %plan_ref.1) | copy-start | bytes 388
  7.6 43.0 %copy-start.11 = (s32[32]{0:T(128)S(1)}, s32[32]{0:T(128)}, u32[]{:S(2)}) copy-start(s32[32]{0:T(128)} %bins_ref.1) | copy-start | bytes 388
  7.6 43.0 %all-to-all-start = ((bf16[128,64,128]{2,1,0:T(8,128)(2,1)}), bf16[128,64,128]{2,1,0:T(8,128)(2,1)S(1)}, u32[]{:S(2)}, u32[]{:S(2)}) async-start(bf16[128,64,128]{2,1,0:T(8,128)(2,1)} %copy-done), calls=%async_computation | async-start | bytes 4194304 | tf_op jit(solution)/shard_map/all_to_all | solution.py:336
  19.5 2.9 %collective-permute-start = (bf16[128,640]{1,0:T(8,128)(2,1)S(1)}, bf16[128,640]{1,0:T(8,128)(2,1)S(1)}, u32[]{:S(2)}, u32[]{:S(2)}) collective-permute-start(bf16[128,640]{1,0:T(8,128)(2,1)S(1)} %get-tuple-element.17), channel_id=1, source_target_pairs={{0,1},{1,0},{2,3},{3,2},{4,5},{5,4},{6,7},{7,6},{8,9},{9,8},{10,11... | collective-permute-start | bytes 491528 | tf_op jit(solution)/shard_map/ppermute | solution.py:342
  20.6 26.0 %collective-permute-start.1 = (bf16[128,640]{1,0:T(8,128)(2,1)S(1)}, bf16[128,640]{1,0:T(8,128)(2,1)S(1)}, u32[]{:S(2)}, u32[]{:S(2)}) collective-permute-start(bf16[128,640]{1,0:T(8,128)(2,1)S(1)} %get-tuple-element.18), channel_id=1, source_target_pairs={{0,2},{1,3},{2,0},{3,1},{4,6},{5,7},{6,4},{7,5},{8,10},{9,11},{10,... | collective-permute-start | bytes 491528 | tf_op jit(solution)/shard_map/ppermute | solution.py:342
  21.3 29.3 %collective-permute-start.2 = (bf16[128,640]{1,0:T(8,128)(2,1)S(1)}, bf16[128,640]{1,0:T(8,128)(2,1)S(1)}, u32[]{:S(2)}, u32[]{:S(2)}) collective-permute-start(bf16[128,640]{1,0:T(8,128)(2,1)S(1)} %get-tuple-element.19), channel_id=1, source_target_pairs={{0,3},{1,2},{2,1},{3,0},{4,7},{5,6},{6,5},{7,4},{8,11},{9,10},{10,... | collective-permute-start | bytes 491528 | tf_op jit(solution)/shard_map/ppermute | solution.py:342
  60.4 1.3 %copy-start.1 = (bf16[128,64,128]{2,1,0:T(8,128)(2,1)}, bf16[128,64,128]{2,1,0:T(8,128)(2,1)S(1)}, u32[]{:S(2)}) copy-start(bf16[128,64,128]{2,1,0:T(8,128)(2,1)S(1)} %get-tuple-element.24) | copy-start | bytes 6291460
  61.7 41.5 %all-to-all-start.1 = ((bf16[128,64,128]{2,1,0:T(8,128)(2,1)}), bf16[128,64,128]{2,1,0:T(8,128)(2,1)S(1)}, u32[]{:S(2)}, u32[]{:S(2)}) async-start(bf16[128,64,128]{2,1,0:T(8,128)(2,1)} %copy-done.1), calls=%async_computation.1 | async-start | bytes 4194304 | tf_op jit(solution)/shard_map/all_to_all | solution.py:336
  70.6 2.9 %collective-permute-start.3 = (bf16[128,640]{1,0:T(8,128)(2,1)S(1)}, bf16[128,640]{1,0:T(8,128)(2,1)S(1)}, u32[]{:S(2)}, u32[]{:S(2)}) collective-permute-start(bf16[128,640]{1,0:T(8,128)(2,1)S(1)} %get-tuple-element.21), channel_id=1, source_target_pairs={{0,1},{1,0},{2,3},{3,2},{4,5},{5,4},{6,7},{7,6},{8,9},{9,8},{10,11... | collective-permute-start | bytes 491528 | tf_op jit(solution)/shard_map/ppermute | solution.py:342
  71.7 26.3 %collective-permute-start.4 = (bf16[128,640]{1,0:T(8,128)(2,1)S(1)}, bf16[128,640]{1,0:T(8,128)(2,1)S(1)}, u32[]{:S(2)}, u32[]{:S(2)}) collective-permute-start(bf16[128,640]{1,0:T(8,128)(2,1)S(1)} %get-tuple-element.22), channel_id=1, source_target_pairs={{0,2},{1,3},{2,0},{3,1},{4,6},{5,7},{6,4},{7,5},{8,10},{9,11},{10,... | collective-permute-start | bytes 491528 | tf_op jit(solution)/shard_map/ppermute | solution.py:342
  72.4 29.6 %collective-permute-start.5 = (bf16[128,640]{1,0:T(8,128)(2,1)S(1)}, bf16[128,640]{1,0:T(8,128)(2,1)S(1)}, u32[]{:S(2)}, u32[]{:S(2)}) collective-permute-start(bf16[128,640]{1,0:T(8,128)(2,1)S(1)} %get-tuple-element.23), channel_id=1, source_target_pairs={{0,3},{1,2},{2,1},{3,0},{4,7},{5,6},{6,5},{7,4},{8,11},{9,10},{10,... | collective-permute-start | bytes 491528 | tf_op jit(solution)/shard_map/ppermute | solution.py:342

commit v2 on v0

v2 whole, which is shorter than its diff:
```python
import jax
import jax.numpy as jnp
from jax import lax
from jax.experimental import pallas as pl
from jax.experimental.pallas import tpu as pltpu
from jax.sharding import PartitionSpec as P

HEADS = 20
HD = 128
N_DP = 32
N_SP = 4
LOADERS = N_DP * N_SP
ROWS = 128
GROUP = 512
HEADS_DEV = HEADS // N_SP
WIDTH = HEADS * HD
PART = HEADS_DEV * HD
CHUNK = 3 * PART
SCALE = HD ** (-0.5)
LOG2E = 1.4426950408889634
BF = jnp.bfloat16
F32 = jnp.float32


def dot(a, b):
    return jnp.dot(a, b, preferred_element_type=F32)


def dot_nt(a, b):
    return lax.dot_general(a, b, (((1,), (1,)), ((), ())), preferred_element_type=F32)


def dot_tn(a, b):
    return lax.dot_general(a, b, (((0,), (0,)), ((), ())), preferred_element_type=F32)


def iota(shape, dim):
    return lax.broadcasted_iota(jnp.int32, shape, dim)


def onehot(hit):
    return jnp.where(hit, 1.0, 0.0).astype(BF)


def row_picker(table, me):
    slot = jnp.sum(jnp.where(table // ROWS == me, table % ROWS, 0), axis=1, keepdims=True)
    return onehot(slot == iota((LOADERS, ROWS), 1))


def quarters_first():
    row, col = iota((256, 256), 0), iota((256, 256), 1)
    return onehot(col == (row % 64) * 4 + row // 64)


def columns(head, array):
    return pl.ds((head * 3 + array) * HD, HD)


def part_lanes(index):
    return pl.ds(pl.multiple_of(index * PART, HD), PART)


def sample_of(group, plan_ref, value_ref):
    value = jnp.int32(0)
    for sample in range(N_DP):
        value = jnp.where(plan_ref[sample] == group, value_ref[sample], value)
    return value


def pack_kernel(me_ref, table_ref, q_ref, k_ref, v_ref, out_ref, index_ref, in_ref, send_ref, table_sem, in_sem, out_sem):
    index = pltpu.make_async_copy(table_ref, index_ref, table_sem)
    index.start()
    loads = []
    for part in range(N_SP):
        lanes = pl.ds(part * PART, PART)
        for array, ref in enumerate((q_ref, k_ref, v_ref)):
            load = pltpu.make_async_copy(ref.at[:, lanes], in_ref.at[array, :, lanes], in_sem.at[part, array])
            load.start()
            loads.append(load)
    index.wait()
    pick = row_picker(index_ref[...], me_ref[0])
    stores = []
    for part in range(N_SP):
        for array in range(3):
            loads[part * 3 + array].wait()
            rows = dot(pick, in_ref[array, :, pl.ds(part * PART, PART)]).astype(BF).reshape(N_DP, 4, PART)
            for head in range(HEADS_DEV):
                send_ref[part, :, :, columns(head, array)] = rows[:, :, head * HD : (head + 1) * HD]
        store = pltpu.make_async_copy(send_ref.at[part], out_ref.at[:, part], out_sem.at[part])
        store.start()
        stores.append(store)
    for store in stores:
        store.wait()


def unpack_kernel(pick_ref, recv_ref, q_ref, k_ref, v_ref, out_ref, out_sem):
    pick = pick_ref[...]
    stores = []
    for part in range(N_SP):
        lanes = pl.ds(part * PART, PART)
        for array, ref in enumerate((q_ref, k_ref, v_ref)):
            rows = jnp.concatenate(
                [recv_ref[:, part, :, columns(head, array)].reshape(ROWS, HD) for head in range(HEADS_DEV)],
                axis=1,
            )
            out_ref[array, :, lanes] = dot(pick, rows).astype(BF)
            store = pltpu.make_async_copy(
                out_ref.at[array, :, lanes], ref.at[:, lanes], out_sem.at[array, part]
            )
            store.start()
            stores.append(store)
    for store in stores:
        store.wait()


def spread_kernel(
    me_ref,
    lengths_ref,
    plan_ref,
    bins_ref,
    guide_ref,
    table_ref,
    cot_ref,
    p0_ref,
    p1_ref,
    p2_ref,
    p3_ref,
    bias_ref,
    live_ref,
    pick_ref,
    gated_ref,
):
    me = me_ref[0]
    group, mine = me // N_SP, me % N_SP
    group_len = sample_of(group, plan_ref, lengths_ref)
    group_bin = sample_of(group, plan_ref, bins_ref)
    for head in range(HEADS):
        lanes = pl.ds(head * HD, HD)
        gated_ref[:, lanes] = (guide_ref[group_bin, head] * cot_ref[:, lanes].astype(F32)).astype(BF)
    order = onehot(table_ref[pl.ds(me, 1), :] // ROWS == iota((LOADERS, ROWS), 0))
    for step, ref in enumerate((p0_ref, p1_ref, p2_ref, p3_ref)):
        ref[...] = dot(order, gated_ref[:, part_lanes(jnp.bitwise_xor(mine, step))]).astype(BF)
    pick_ref[...] = row_picker(table_ref[...], me).astype(F32).T.astype(BF)
    row = iota((GROUP, ROWS), 0)
    source = jnp.zeros((GROUP, ROWS), jnp.int32)
    for quarter in range(4):
        own = table_ref[pl.ds(group * N_SP + quarter, 1), :] // ROWS
        source = jnp.where(row % 4 == quarter, own, source)
    place = onehot(source == row // 4)
    count = iota((ROWS, HD), 0).astype(F32).astype(BF)
    place_col = dot(place, count) + (ROWS * (row % 4)).astype(F32)
    bias_ref[...] = jnp.where(place_col < group_len.astype(F32), 0.0, -1e30)
    lane = iota((8, GROUP), 1)
    place_row = dot_nt(iota((8, ROWS), 1).astype(F32).astype(BF), place) + (ROWS * (lane % 4)).astype(F32)
    live_ref[...] = jnp.where(place_row < group_len.astype(F32), 1.0, 0.0)


def collect_kernel(me_ref, plan_ref, bins_ref, guide_ref, table_ref, i0_ref, i1_ref, i2_ref, i3_ref, out_ref):
    me = me_ref[0]
    group, mine = me // N_SP, me % N_SP
    group_bin = sample_of(group, plan_ref, bins_ref)
    order = onehot(table_ref[pl.ds(me, 1), :] // ROWS == iota((LOADERS, ROWS), 0)).astype(F32).T.astype(BF)
    for step, ref in enumerate((i0_ref, i1_ref, i2_ref, i3_ref)):
        out_ref[:, part_lanes(jnp.bitwise_xor(mine, step))] = dot(order, ref[...]).astype(BF)
    for head in range(HEADS):
        lanes = pl.ds(head * HD, HD)
        out_ref[:, lanes] = (guide_ref[group_bin, head] * out_ref[:, lanes].astype(F32)).astype(BF)


def forward_kernel(
    me_ref, bias_ref, live_ref, recv_ref, raised_ref, inverse_ref, o0_ref, o1_ref, o2_ref, o3_ref, out_ref
):
    mine = me_ref[0] % N_SP
    live = live_ref[0:1, :]
    bias = bias_ref[:, 0:1]
    order = quarters_first()
    for head in range(HEADS_DEV):
        query = recv_ref[:, :, columns(head, 0)].reshape(GROUP, HD)
        key = recv_ref[:, :, columns(head, 1)].reshape(GROUP, HD)
        value = recv_ref[:, :, columns(head, 2)].reshape(GROUP, HD)
        scores = dot_nt(key, query) + bias
        top = jnp.max(scores, axis=0, keepdims=True)
        raised = jnp.exp2((scores - top) * (SCALE * LOG2E))
        inverse = live / jnp.sum(raised, axis=0, keepdims=True)
        weights = raised.astype(BF)
        raised_ref[head] = weights
        inverse_ref[head : head + 1, :] = inverse
        output = (dot_tn(value, weights) * inverse).astype(BF)
        for half in range(2):
            rows = dot_nt(order, output[:, half * 256 : (half + 1) * 256]).astype(BF)
            out_ref[:, pl.ds(half * 64, 64), pl.ds(head * HD, HD)] = rows.reshape(4, 64, HD)
    inverse_ref[HEADS_DEV:, :] = jnp.zeros((8 - HEADS_DEV, GROUP), F32)
    for step, ref in enumerate((o0_ref, o1_ref, o2_ref, o3_ref)):
        ref[...] = out_ref[jnp.bitwise_xor(mine, step)]


def backward_kernel(
    me_ref, recv_ref, raised_ref, inverse_ref, d0_ref, d1_ref, d2_ref, d3_ref, ret_ref, cot_ref, grad_ref
):
    mine = me_ref[0] % N_SP
    for step, ref in enumerate((d0_ref, d1_ref, d2_ref, d3_ref)):
        cot_ref[jnp.bitwise_xor(mine, step)] = ref[...]
    order = quarters_first()
    for half in range(2):
        rows = cot_ref[:, pl.ds(half * 64, 64), :].reshape(256, PART)
        grad_ref[pl.ds(half * 256, 256), :] = dot_tn(order, rows).astype(BF)
    inverse_columns = inverse_ref[...].T
    for head in range(HEADS_DEV):
        query = recv_ref[:, :, columns(head, 0)].reshape(GROUP, HD)
        key = recv_ref[:, :, columns(head, 1)].reshape(GROUP, HD)
        value = recv_ref[:, :, columns(head, 2)].reshape(GROUP, HD)
        inverse = inverse_ref[head : head + 1, :]
        scale = inverse_columns[:, head : head + 1] * SCALE
        grad = (grad_ref[:, pl.ds(head * HD, HD)].astype(F32) * scale).astype(BF)
        weights = raised_ref[head]
        wide = weights.astype(F32)
        grad_attend = dot_nt(value, grad)
        row_dot = jnp.sum(wide * grad_attend, axis=0, keepdims=True) * inverse
        grad_scores = (wide * (grad_attend - row_dot)).astype(BF)
        grad_query = dot_tn(key, grad_scores).T.astype(BF)
        grad_key = dot(grad_scores, query).astype(BF)
        grad_value = (dot(weights, grad) * (1.0 / SCALE)).astype(BF)
        ret_ref[:, :, columns(head, 0)] = grad_query.reshape(LOADERS, 4, HD)
        ret_ref[:, :, columns(head, 1)] = grad_key.reshape(LOADERS, 4, HD)
        ret_ref[:, :, columns(head, 2)] = grad_value.reshape(LOADERS, 4, HD)


SMEM = pl.BlockSpec(memory_space=pltpu.SMEM)
VMEM = pl.BlockSpec(memory_space=pltpu.VMEM)
HBM = pl.BlockSpec(memory_space=pltpu.HBM)
PARAMS = pltpu.CompilerParams(vmem_limit_bytes=24 * 1024 * 1024)
PIECE = jax.ShapeDtypeStruct((ROWS, PART), BF)
WHOLE = jax.ShapeDtypeStruct((ROWS, WIDTH), BF)


def in_hbm(array):
    return pltpu.with_memory_space_constraint(array, pltpu.HBM)


def pack(me, table, queries, keys, values):
    chunks = pl.pallas_call(
        pack_kernel,
        out_shape=pltpu.HBM((N_DP, N_SP, 4, CHUNK), BF),
        in_specs=[SMEM] + [HBM] * 4,
        out_specs=HBM,
        scratch_shapes=[
            pltpu.VMEM((LOADERS, ROWS), jnp.int32),
            pltpu.VMEM((3, ROWS, WIDTH), BF),
            pltpu.VMEM((N_SP, N_DP, 4, CHUNK), BF),
            pltpu.SemaphoreType.DMA,
            pltpu.SemaphoreType.DMA((N_SP, 3)),
            pltpu.SemaphoreType.DMA((N_SP,)),
        ],
        compiler_params=PARAMS,
        name="pack",
    )(me, in_hbm(table), in_hbm(queries), in_hbm(keys), in_hbm(values))
    return chunks.reshape(LOADERS, 4, CHUNK)


def unpack(pick, chunks):
    return pl.pallas_call(
        unpack_kernel,
        out_shape=(pltpu.HBM((ROWS, WIDTH), BF),) * 3,
        in_specs=[VMEM] * 2,
        out_specs=(HBM,) * 3,
        scratch_shapes=[
            pltpu.VMEM((3, ROWS, WIDTH), BF),
            pltpu.SemaphoreType.DMA((3, N_SP)),
        ],
        compiler_params=PARAMS,
        name="unpack",
    )(pick, chunks.reshape(N_DP, N_SP, 4, CHUNK))


def spread(me, lengths, plan, bins, guide, table, cotangent):
    return pl.pallas_call(
        spread_kernel,
        out_shape=(PIECE,) * N_SP
        + (
            jax.ShapeDtypeStruct((GROUP, HD), F32),
            jax.ShapeDtypeStruct((8, GROUP), F32),
            jax.ShapeDtypeStruct((ROWS, LOADERS), BF),
        ),
        in_specs=[SMEM] * 5 + [VMEM] * 2,
        out_specs=(VMEM,) * (N_SP + 3),
        scratch_shapes=[pltpu.VMEM((ROWS, WIDTH), BF)],
        compiler_params=PARAMS,
        name="spread",
    )(me, lengths, plan, bins, guide, table, cotangent)


def collect(me, plan, bins, guide, table, pieces):
    return pl.pallas_call(
        collect_kernel,
        out_shape=WHOLE,
        in_specs=[SMEM] * 4 + [VMEM] * (1 + N_SP),
        out_specs=VMEM,
        compiler_params=PARAMS,
        name="collect",
    )(me, plan, bins, guide, table, *pieces)


def forward(me, bias, live, chunks):
    return pl.pallas_call(
        forward_kernel,
        out_shape=(
            jax.ShapeDtypeStruct((HEADS_DEV, GROUP, GROUP), BF),
            jax.ShapeDtypeStruct((8, GROUP), F32),
        )
        + (PIECE,) * N_SP,
        in_specs=[SMEM] + [VMEM] * 3,
        out_specs=(VMEM,) * (2 + N_SP),
        scratch_shapes=[pltpu.VMEM((4, ROWS, PART), BF)],
        compiler_params=PARAMS,
        name="forward",
    )(me, bias, live, chunks)


def backward(me, chunks, raised, inverse, pieces):
    return pl.pallas_call(
        backward_kernel,
        out_shape=jax.ShapeDtypeStruct((LOADERS, 4, CHUNK), BF),
        in_specs=[SMEM] + [VMEM] * (3 + N_SP),
        out_specs=VMEM,
        scratch_shapes=[
            pltpu.VMEM((4, ROWS, PART), BF),
            pltpu.VMEM((GROUP, PART), BF),
        ],
        compiler_params=PARAMS,
        name="backward",
    )(me, chunks, raised, inverse, *pieces)


def exchange(chunks):
    return lax.all_to_all(chunks, ("dp", "sp"), split_axis=0, concat_axis=0, tiled=True)


def swap_pieces(pieces):
    return [pieces[0]] + [
        lax.ppermute(pieces[step], "sp", [(i, i ^ step) for i in range(N_SP)]) for step in range(1, N_SP)
    ]


def per_device(
    queries,
    key_rows,
    value_rows,
    cotangent,
    lengths,
    sample_plan,
    guide_bins,
    guide_table,
    block_source,
):
    me = (lax.axis_index("dp") * N_SP + lax.axis_index("sp")).astype(jnp.int32).reshape(1)
    table = block_source.reshape(LOADERS, ROWS)
    chunks = exchange(pack(me, table, queries, key_rows, value_rows))
    *pieces, bias, live, pick = spread(
        me, lengths, sample_plan, guide_bins, guide_table, table, cotangent
    )
    chunks, pieces = lax.optimization_barrier((chunks, pieces))
    grad_pieces = swap_pieces(pieces)
    raised, inverse, *outs = forward(me, bias, live, chunks)
    out_pieces = swap_pieces(outs)
    grads = backward(me, chunks, raised, inverse, grad_pieces)
    grads, out_pieces[2], out_pieces[3] = lax.optimization_barrier((grads, out_pieces[2], out_pieces[3]))
    back = exchange(grads)
    attn_out = collect(me, sample_plan, guide_bins, guide_table, table, out_pieces)
    return attn_out, *unpack(pick, back)


def solution(mesh):
    rows = P(("dp", "sp"), None)
    return jax.shard_map(
        per_device,
        mesh=mesh,
        in_specs=(rows,) * 4 + (P(),) * 5,
        out_specs=(rows,) * 4,
        check_vma=False,
    )
```

time: 323 us -> 99 us (0.31)
  local copies, waits for them, and re-layouts: 82.1 us -> 2.64 us
  waiting for transfers between devices: 112 us -> 55.8 us
  starting transfers between devices: 73.9 us -> 21 us
  matrix products: 34.7 us -> 0 us
  Pallas kernels: 0 us -> 18.4 us
  other arithmetic: 17.2 us -> 0 us
    all_to_all x14 -> x2, waiting for transfers between devices: 112 us -> 51.5 us  [exchange(): lax.all_to_all(chunks, ('dp', 'sp'), split_axis=0, concat_axis=0, tiled=T...]
    all_to_all x14 -> x2, starting transfers between devices: 73.9 us -> 15.2 us  [exchange(): lax.all_to_all(chunks, ('dp', 'sp'), split_axis=0, concat_axis=0, tiled=T...]
    dot_general x30 -> x0, matrix products: 34.7 us -> none  [the longest x5 9.67 us: head_pass(): jnp.dot(attend_bf.T, grad_head, preferred_element_type=jnp.float32)]
    unnamed x42 -> x18, local copies, waits for them, and re-layouts: 30.9 us -> 2.64 us
    gather x16 -> x0, local copies, waits for them, and re-layouts: 19.6 us -> none  [the longest x7 8.04 us: as_blocks(): return source.reshape(loaders, block_rows, row_width)[order]]
    pallas_call x0 -> x6, Pallas kernels: none -> 18.4 us  [the longest x1 5.07 us: pack(): pl.pallas_call(pack_kernel, out_shape=pltpu.HBM((N_DP, N_SP, 4, CHUNK), B...]
    all_to_all x12 -> x0, local copies, waits for them, and re-layouts: 11.1 us -> none  [the longest x2 2.4 us: per_device(): lax.all_to_all(gq_heads, 'sp', split_axis=0, concat_axis=1, tiled=True)]
    gather x10 -> x0, other arithmetic: 8.57 us -> none  [the longest x8 8.56 us: as_blocks(): return source.reshape(loaders, block_rows, row_width)[order]]
  transfers between devices with their start and end apart: 14 -> 8, of which waited for: 14 -> 5; matrix products, arithmetic and copies ran while one was open for 22% -> 0% of each run, Pallas kernels for 0% -> 12%
where the time goes in v2:
time: 99 us; the launch traced here: 98.6 us
  waiting for transfers between devices  55.8 us (56%)
  starting transfers between devices  21 us (21%)
  Pallas kernels  18.4 us (19%)
  local copies, waits for them, and re-layouts  2.64 us (3%)
    all_to_all x2, waiting for transfers between devices, exchange(): lax.all_to_all(chunks, ('dp', 'sp'), split_axis=0, concat_axis=0, tiled=T...  51.5 us
    all_to_all x2, starting transfers between devices, exchange(): lax.all_to_all(chunks, ('dp', 'sp'), split_axis=0, concat_axis=0, tiled=T...  15.2 us
    ppermute x6, starting transfers between devices, swap_pieces(): lax.ppermute(pieces[step], 'sp', [(i, i ^ step) for i in range(N_SP)])  5.74 us
    pallas_call x1, Pallas kernels, pack(): pl.pallas_call(pack_kernel, out_shape=pltpu.HBM((N_DP, N_SP, 4, CHUNK), B...  5.07 us
    pallas_call x1, Pallas kernels, backward(): pl.pallas_call(backward_kernel, out_shape=jax.ShapeDtypeStruct((LOADERS,...  4.39 us
    ppermute x6, waiting for transfers between devices, swap_pieces(): lax.ppermute(pieces[step], 'sp', [(i, i ^ step) for i in range(N_SP)])  4.29 us
    pallas_call x1, Pallas kernels, forward(): pl.pallas_call(forward_kernel, out_shape=(jax.ShapeDtypeStruct((HEADS_DEV...  4.14 us
    unnamed x18, local copies, waits for them, and re-layouts  2.64 us
  transfers between devices with their start and end apart: 8, of which 5 were waited for; matrix products, arithmetic and copies ran while one was open for 0% of the time, Pallas kernels for 12%

profile of v2, /device:TPU:1, one launch (start us, length us, event | category | flops | bytes accessed | tf_op | source)
XLA Modules:
  0.0 98.6 jit_solution(15087271846241916872)
XLA Ops:
  0.6 5.1 %pack.1 = bf16[32,4,4,1920]{3,2,1,0:T(4,128)(2,1)} custom-call(s32[1]{0:T(128)} %bitcast.me_ref, s32[128,128]{1,0:T(8,128)} %bitcast.5, bf16[128,2560]{1,0:T(8,128)(2,1)} %q_ref.1, bf16[128,2560]{1,0:T(8,128)(2,1)} %k_ref.1, bf16[128,2560]{1,0:T(8,128)(2,1)} %v_ref.1), custom_call_target="tpu_custom_call" | custom-call | tf_op jit(solution)/shard_map/pack/pallas_call | solution.py:241
  5.7 0.0 copy-start.3
  5.7 0.0 copy-start.4
  5.8 11.5 %all-to-all-start = ((bf16[128,4,1920]{2,1,0:T(4,128)(2,1)}), bf16[128,4,1920]{2,1,0:T(4,128)(2,1)S(1)}, u32[]{:S(2)}, u32[]{:S(2)}) async-start(bf16[128,4,1920]{2,1,0:T(4,128)(2,1)} %bitcast.8), calls=%async_computation | async-start | bytes 3932160 | tf_op jit(solution)/shard_map/all_to_all | solution.py:335
  17.4 1.3 %spread.1 = (bf16[128,640]{1,0:T(8,128)(2,1)S(1)}, bf16[128,640]{1,0:T(8,128)(2,1)S(1)}, bf16[128,640]{1,0:T(8,128)(2,1)S(1)}, bf16[128,640]{1,0:T(8,128)(2,1)S(...) custom-call(s32[1]{0:T(128)} %bitcast.me_ref, s32[32]{0:T(128)S(1)} %copy-done.6, ...), custom_call_target="tpu_custom_call" | custom-call | tf_op jit(solution)/shard_map/spread/pallas_call | solution.py:276
  18.6 0.7 copy-done.7
  19.3 0.7 copy-done.8
  20.0 26.5 %all-to-all-done.recv_ref = bf16[128,4,1920]{2,1,0:T(4,128)(2,1)S(1)} async-done(((bf16[128,4,1920]{2,1,0:T(4,128)(2,1)}), bf16[128,4,1920]{2,1,0:T(4,128)(2,1)S(1)}, u32[]{:S(2)}, u32[]{:S(2)}) %all-to-all-start) | async-done | bytes 1966112 | tf_op jit(solution)/shard_map/all_to_all | solution.py:335
  46.5 0.9 collective-permute-start.1
  47.3 0.3 collective-permute-start.2
  47.6 1.3 %collective-permute-start.3 = (bf16[128,640]{1,0:T(8,128)(2,1)S(1)}, bf16[128,640]{1,0:T(8,128)(2,1)S(1)}, u32[]{:S(2)}, u32[]{:S(2)}) collective-permute-start(bf16[128,640]{1,0:T(8,128)(2,1)S(1)} %get-tuple-element.42), channel_id=1, source_target_pairs={{0,3},{1,2},{2,1},{3,0},{4,7},{5,6},{6,5},{7,4},{8,11},{9,10},{10,... | collective-permute-start | bytes 491528 | tf_op jit(solution)/shard_map/ppermute | solution.py:340
  49.0 4.1 %forward.1 = (bf16[5,512,512]{2,1,0:T(8,128)(2,1)S(1)}, f32[8,512]{1,0:T(8,128)S(1)}, bf16[128,640]{1,0:T(8,128)(2,1)S(1)}, bf16[128,640]{1,0:T(8,128)(2,1)S(1)}...) custom-call(s32[1]{0:T(128)} %bitcast.me_ref, f32[512,128]{1,0:T(8,128)S(1)} %get-tuple-element.28.bias_ref, ...), custom_call_target="tpu_custom_call" | custom-call | tf_op jit(solution)/shard_map/forward/pallas_call | solution.py:304
  53.1 0.4 collective-permute-start.4
  53.5 1.6 %collective-permute-start.5 = (bf16[128,640]{1,0:T(8,128)(2,1)S(1)}, bf16[128,640]{1,0:T(8,128)(2,1)S(1)}, u32[]{:S(2)}, u32[]{:S(2)}) collective-permute-start(bf16[128,640]{1,0:T(8,128)(2,1)S(1)} %get-tuple-element.44), channel_id=1, source_target_pairs={{0,3},{1,2},{2,1},{3,0},{4,7},{5,6},{6,5},{7,4},{8,11},{9,10},{10,... | collective-permute-start | bytes 491528 | tf_op jit(solution)/shard_map/ppermute | solution.py:340
  55.1 2.3 %collective-permute-done.3.d3_ref = bf16[128,640]{1,0:T(8,128)(2,1)S(1)} collective-permute-done((bf16[128,640]{1,0:T(8,128)(2,1)S(1)}, bf16[128,640]{1,0:T(8,128)(2,1)S(1)}, u32[]{:S(2)}, u32[]{:S(2)}) %collective-permute-start.3) | collective-permute-done | bytes 163872 | tf_op jit(solution)/shard_map/ppermute | solution.py:340
  57.4 4.4 %backward.1 = bf16[128,4,1920]{2,1,0:T(4,128)(2,1)S(1)} custom-call(s32[1]{0:T(128)} %bitcast.me_ref, bf16[128,4,1920]{2,1,0:T(4,128)(2,1)S(1)} %all-to-all-done.recv_ref, bf16[5,512,512]{2,1,0:T(8,128)(2,1)S(1)} %get-tuple-element.37.raised_ref, f32[8,512]{1,0:T(8,128)S(1)} %get-tuple-element.38.inverse_ref, bf16[128,640]{1,0:T(8,128)(2,1)S(1)} %get-tuple-element.39.d0_ref, ...), custom_call_target="tpu_custom_call" | custom-call | tf_op jit(solution)/shard_map/backward/pallas_call | solution.py:320
  61.8 1.3 %copy-done = bf16[128,4,1920]{2,1,0:T(4,128)(2,1)} copy-done((bf16[128,4,1920]{2,1,0:T(4,128)(2,1)}, bf16[128,4,1920]{2,1,0:T(4,128)(2,1)S(1)}, u32[]{:S(2)}) %copy-start) | copy-done | bytes 1966104
  63.1 1.0 collective-permute-done.5.i3_ref
  64.0 3.7 %all-to-all-start.1 = ((bf16[128,4,1920]{2,1,0:T(4,128)(2,1)}), bf16[128,4,1920]{2,1,0:T(4,128)(2,1)S(1)}, u32[]{:S(2)}, u32[]{:S(2)}) async-start(bf16[128,4,1920]{2,1,0:T(4,128)(2,1)} %copy-done), calls=%async_computation.1 | async-start | bytes 3932160 | tf_op jit(solution)/shard_map/all_to_all | solution.py:335
  67.8 1.3 %collective-permute-start = (bf16[128,640]{1,0:T(8,128)(2,1)S(1)}, bf16[128,640]{1,0:T(8,128)(2,1)S(1)}, u32[]{:S(2)}, u32[]{:S(2)}) collective-permute-start(bf16[128,640]{1,0:T(8,128)(2,1)S(1)} %get-tuple-element.36), channel_id=1, source_target_pairs={{0,1},{1,0},{2,3},{3,2},{4,5},{5,4},{6,7},{7,6},{8,9},{9,8},{10,11... | collective-permute-start | bytes 491528 | tf_op jit(solution)/shard_map/ppermute | solution.py:340
  69.0 1.0 %collective-permute-done.i1_ref = bf16[128,640]{1,0:T(8,128)(2,1)S(1)} collective-permute-done((bf16[128,640]{1,0:T(8,128)(2,1)S(1)}, bf16[128,640]{1,0:T(8,128)(2,1)S(1)}, u32[]{:S(2)}, u32[]{:S(2)}) %collective-permute-start) | collective-permute-done | bytes 163872 | tf_op jit(solution)/shard_map/ppermute | solution.py:340
  70.1 2.0 %collect.1 = bf16[128,2560]{1,0:T(8,128)(2,1)} custom-call(s32[1]{0:T(128)} %bitcast.me_ref, s32[32]{0:T(128)S(1)} %copy-done.4, s32[32]{0:T(128)S(1)} %copy-done.5, f32[8,20]{1,0:T(8,128)S(1)} %copy-done.3, s32[128,128]{1,0:T(8,128)S(1)} %bitcast.7, bf16[128,640]{1,0:T(8,128)(2,1)S(1)} %get-tuple-element.35.i0_ref, ...), custom_call_target="tpu_custom_call" | custom-call | tf_op jit(solution)/shard_map/collect/pallas_call | solution.py:293
  72.0 25.0 %all-to-all-done.1 = bf16[128,4,1920]{2,1,0:T(4,128)(2,1)S(1)} async-done(((bf16[128,4,1920]{2,1,0:T(4,128)(2,1)}), bf16[128,4,1920]{2,1,0:T(4,128)(2,1)S(1)}, u32[]{:S(2)}, u32[]{:S(2)}) %all-to-all-start.1) | async-done | bytes 1966112 | tf_op jit(solution)/shard_map/all_to_all | solution.py:335
  97.1 1.6 %unpack.1 = (bf16[128,2560]{1,0:T(8,128)(2,1)}, bf16[128,2560]{1,0:T(8,128)(2,1)}, bf16[128,2560]{1,0:T(8,128)(2,1)}) custom-call(bf16[128,128]{1,0:T(8,128)(2,1)S(1)} %get-tuple-element.47.pick_ref, bf16[32,4,4,1920]{3,2,1,0:T(4,128)(2,1)S(1)} %bitcast.4), custom_call_target="tpu_custom_call" | custom-call | tf_op jit(solution)/shard_map/unpack/pallas_call | solution.py:261
  (16 shorter events, 0.0 us)
Async XLA Ops:
  5.7 11.6 %copy-start.1 = (bf16[128,2560]{1,0:T(8,128)(2,1)S(1)}, bf16[128,2560]{1,0:T(8,128)(2,1)}, u32[]{:S(2)}) copy-start(bf16[128,2560]{1,0:T(8,128)(2,1)} %cot_ref.1) | copy-start | bytes 1966084
  5.7 11.6 %copy-start.2 = (s32[16384]{0:T(1024)S(1)}, s32[16384]{0:T(1024)}, u32[]{:S(2)}) copy-start(s32[16384]{0:T(1024)} %param.17) | copy-start | bytes 196612
  5.7 11.6 %copy-start.3 = (f32[8,20]{1,0:T(8,128)S(1)}, f32[8,20]{1,0:T(8,128)}, u32[]{:S(2)}) copy-start(f32[8,20]{1,0:T(8,128)} %guide_ref.3) | copy-start | bytes 1924
  5.7 11.6 %copy-start.4 = (s32[32]{0:T(128)S(1)}, s32[32]{0:T(128)}, u32[]{:S(2)}) copy-start(s32[32]{0:T(128)} %plan_ref.3) | copy-start | bytes 388
  5.8 11.6 %copy-start.5 = (s32[32]{0:T(128)S(1)}, s32[32]{0:T(128)}, u32[]{:S(2)}) copy-start(s32[32]{0:T(128)} %bins_ref.3) | copy-start | bytes 388
  5.8 11.6 %copy-start.6 = (s32[32]{0:T(128)S(1)}, s32[32]{0:T(128)}, u32[]{:S(2)}) copy-start(s32[32]{0:T(128)} %lengths_ref.1) | copy-start | bytes 388
  5.8 40.7 %all-to-all-start = ((bf16[128,4,1920]{2,1,0:T(4,128)(2,1)}), bf16[128,4,1920]{2,1,0:T(4,128)(2,1)S(1)}, u32[]{:S(2)}, u32[]{:S(2)}) async-start(bf16[128,4,1920]{2,1,0:T(4,128)(2,1)} %bitcast.8), calls=%async_computation | async-start | bytes 3932160 | tf_op jit(solution)/shard_map/all_to_all | solution.py:335
  18.6 0.7 copy-start.7
  19.3 0.7 copy-start.8
  46.5 8.6 %collective-permute-start.1 = (bf16[128,640]{1,0:T(8,128)(2,1)}, bf16[128,640]{1,0:T(8,128)(2,1)S(1)}, u32[]{:S(2)}, u32[]{:S(2)}) collective-permute-start(bf16[128,640]{1,0:T(8,128)(2,1)} %copy-done.8), channel_id=1, source_target_pairs={{0,1},{1,0},{2,3},{3,2},{4,5},{5,4},{6,7},{7,6},{8,9},{9,8},{10,11... | collective-permute-start | bytes 491528 | tf_op jit(solution)/shard_map/ppermute | solution.py:340
  47.3 7.7 %collective-permute-start.2 = (bf16[128,640]{1,0:T(8,128)(2,1)}, bf16[128,640]{1,0:T(8,128)(2,1)S(1)}, u32[]{:S(2)}, u32[]{:S(2)}) collective-permute-start(bf16[128,640]{1,0:T(8,128)(2,1)} %copy-done.7), channel_id=1, source_target_pairs={{0,2},{1,3},{2,0},{3,1},{4,6},{5,7},{6,4},{7,5},{8,10},{9,11},{10,... | collective-permute-start | bytes 491528 | tf_op jit(solution)/shard_map/ppermute | solution.py:340
  47.6 9.7 %collective-permute-start.3 = (bf16[128,640]{1,0:T(8,128)(2,1)S(1)}, bf16[128,640]{1,0:T(8,128)(2,1)S(1)}, u32[]{:S(2)}, u32[]{:S(2)}) collective-permute-start(bf16[128,640]{1,0:T(8,128)(2,1)S(1)} %get-tuple-element.42), channel_id=1, source_target_pairs={{0,3},{1,2},{2,1},{3,0},{4,7},{5,6},{6,5},{7,4},{8,11},{9,10},{10,... | collective-permute-start | bytes 491528 | tf_op jit(solution)/shard_map/ppermute | solution.py:340
  53.1 9.9 %collective-permute-start.4 = (bf16[128,640]{1,0:T(8,128)(2,1)S(1)}, bf16[128,640]{1,0:T(8,128)(2,1)S(1)}, u32[]{:S(2)}, u32[]{:S(2)}) collective-permute-start(bf16[128,640]{1,0:T(8,128)(2,1)S(1)} %get-tuple-element.43), channel_id=1, source_target_pairs={{0,2},{1,3},{2,0},{3,1},{4,6},{5,7},{6,4},{7,5},{8,10},{9,11},{10,... | collective-permute-start | bytes 491528 | tf_op jit(solution)/shard_map/ppermute | solution.py:340
  53.5 10.5 %collective-permute-start.5 = (bf16[128,640]{1,0:T(8,128)(2,1)S(1)}, bf16[128,640]{1,0:T(8,128)(2,1)S(1)}, u32[]{:S(2)}, u32[]{:S(2)}) collective-permute-start(bf16[128,640]{1,0:T(8,128)(2,1)S(1)} %get-tuple-element.44), channel_id=1, source_target_pairs={{0,3},{1,2},{2,1},{3,0},{4,7},{5,6},{6,5},{7,4},{8,11},{9,10},{10,... | collective-permute-start | bytes 491528 | tf_op jit(solution)/shard_map/ppermute | solution.py:340
  61.8 1.3 %copy-start = (bf16[128,4,1920]{2,1,0:T(4,128)(2,1)}, bf16[128,4,1920]{2,1,0:T(4,128)(2,1)S(1)}, u32[]{:S(2)}) copy-start(bf16[128,4,1920]{2,1,0:T(4,128)(2,1)S(1)} %backward.1) | copy-start | bytes 5898244
  64.0 33.0 %all-to-all-start.1 = ((bf16[128,4,1920]{2,1,0:T(4,128)(2,1)}), bf16[128,4,1920]{2,1,0:T(4,128)(2,1)S(1)}, u32[]{:S(2)}, u32[]{:S(2)}) async-start(bf16[128,4,1920]{2,1,0:T(4,128)(2,1)} %copy-done), calls=%async_computation.1 | async-start | bytes 3932160 | tf_op jit(solution)/shard_map/all_to_all | solution.py:335
  67.8 2.3 %collective-permute-start = (bf16[128,640]{1,0:T(8,128)(2,1)S(1)}, bf16[128,640]{1,0:T(8,128)(2,1)S(1)}, u32[]{:S(2)}, u32[]{:S(2)}) collective-permute-start(bf16[128,640]{1,0:T(8,128)(2,1)S(1)} %get-tuple-element.36), channel_id=1, source_target_pairs={{0,1},{1,0},{2,3},{3,2},{4,5},{5,4},{6,7},{7,6},{8,9},{9,8},{10,11... | collective-permute-start | bytes 491528 | tf_op jit(solution)/shard_map/ppermute | solution.py:340

commit v3 on v2

--- a/solution.py
+++ b/solution.py
@@ -53,7 +53,7 @@
 
 
 def columns(head, array):
-    return pl.ds((head * 3 + array) * HD, HD)
+    return pl.ds((array * HEADS_DEV + head) * HD, HD)
 
 
 def part_lanes(index):
@@ -67,26 +67,26 @@
     return value
 
 
-def pack_kernel(me_ref, table_ref, q_ref, k_ref, v_ref, out_ref, index_ref, in_ref, send_ref, table_sem, in_sem, out_sem):
-    index = pltpu.make_async_copy(table_ref, index_ref, table_sem)
+def pack_kernel(me_ref, table_ref, q_ref, k_ref, v_ref, out_ref, index_ref, in_ref, send_ref, index_sem, in_sem, out_sem):
+    index = pltpu.make_async_copy(table_ref, index_ref, index_sem)
     index.start()
     loads = []
-    for part in range(N_SP):
-        lanes = pl.ds(part * PART, PART)
-        for array, ref in enumerate((q_ref, k_ref, v_ref)):
-            load = pltpu.make_async_copy(ref.at[:, lanes], in_ref.at[array, :, lanes], in_sem.at[part, array])
-            load.start()
-            loads.append(load)
+    for array, ref in enumerate((q_ref, k_ref, v_ref)):
+        load = pltpu.make_async_copy(ref, in_ref.at[array], in_sem.at[array])
+        load.start()
+        loads.append(load)
     index.wait()
     pick = row_picker(index_ref[...], me_ref[0])
     stores = []
-    for part in range(N_SP):
-        for array in range(3):
-            loads[part * 3 + array].wait()
-            rows = dot(pick, in_ref[array, :, pl.ds(part * PART, PART)]).astype(BF).reshape(N_DP, 4, PART)
-            for head in range(HEADS_DEV):
-                send_ref[part, :, :, columns(head, array)] = rows[:, :, head * HD : (head + 1) * HD]
-        store = pltpu.make_async_copy(send_ref.at[part], out_ref.at[:, part], out_sem.at[part])
+    for array in range(3):
+        loads[array].wait()
+        lanes = pl.ds(array * PART, PART)
+        for part in range(N_SP):
+            rows = dot(pick, in_ref[array, :, pl.ds(part * PART, PART)]).astype(BF)
+            send_ref[:, part, :, lanes] = rows.reshape(N_DP, 4, PART)
+        store = pltpu.make_async_copy(
+            send_ref.at[:, :, :, lanes], out_ref.at[:, :, :, lanes], out_sem.at[array]
+        )
         store.start()
         stores.append(store)
     for store in stores:
@@ -96,19 +96,13 @@
 def unpack_kernel(pick_ref, recv_ref, q_ref, k_ref, v_ref, out_ref, out_sem):
     pick = pick_ref[...]
     stores = []
-    for part in range(N_SP):
-        lanes = pl.ds(part * PART, PART)
-        for array, ref in enumerate((q_ref, k_ref, v_ref)):
-            rows = jnp.concatenate(
-                [recv_ref[:, part, :, columns(head, array)].reshape(ROWS, HD) for head in range(HEADS_DEV)],
-                axis=1,
-            )
-            out_ref[array, :, lanes] = dot(pick, rows).astype(BF)
-            store = pltpu.make_async_copy(
-                out_ref.at[array, :, lanes], ref.at[:, lanes], out_sem.at[array, part]
-            )
-            store.start()
-            stores.append(store)
+    for array, ref in enumerate((q_ref, k_ref, v_ref)):
+        for part in range(N_SP):
+            rows = recv_ref[:, part, :, pl.ds(array * PART, PART)].reshape(ROWS, PART)
+            out_ref[array, :, pl.ds(part * PART, PART)] = dot(pick, rows).astype(BF)
+        store = pltpu.make_async_copy(out_ref.at[array], ref, out_sem.at[array])
+        store.start()
+        stores.append(store)
     for store in stores:
         store.wait()
 
@@ -195,7 +189,19 @@
 
 
 def backward_kernel(
-    me_ref, recv_ref, raised_ref, inverse_ref, d0_ref, d1_ref, d2_ref, d3_ref, ret_ref, cot_ref, grad_ref
+    me_ref,
+    recv_ref,
+    raised_ref,
+    inverse_ref,
+    d0_ref,
+    d1_ref,
+    d2_ref,
+    d3_ref,
+    out_ref,
+    cot_ref,
+    grad_ref,
+    ret_ref,
+    out_sem,
 ):
     mine = me_ref[0] % N_SP
     for step, ref in enumerate((d0_ref, d1_ref, d2_ref, d3_ref)):
@@ -205,6 +211,7 @@
         rows = cot_ref[:, pl.ds(half * 64, 64), :].reshape(256, PART)
         grad_ref[pl.ds(half * 256, 256), :] = dot_tn(order, rows).astype(BF)
     inverse_columns = inverse_ref[...].T
+    stores = []
     for head in range(HEADS_DEV):
         query = recv_ref[:, :, columns(head, 0)].reshape(GROUP, HD)
         key = recv_ref[:, :, columns(head, 1)].reshape(GROUP, HD)
@@ -220,15 +227,23 @@
         grad_query = dot_tn(key, grad_scores).T.astype(BF)
         grad_key = dot(grad_scores, query).astype(BF)
         grad_value = (dot(weights, grad) * (1.0 / SCALE)).astype(BF)
-        ret_ref[:, :, columns(head, 0)] = grad_query.reshape(LOADERS, 4, HD)
-        ret_ref[:, :, columns(head, 1)] = grad_key.reshape(LOADERS, 4, HD)
-        ret_ref[:, :, columns(head, 2)] = grad_value.reshape(LOADERS, 4, HD)
+        for array, result in enumerate((grad_query, grad_key, grad_value)):
+            lanes = columns(head, array)
+            ret_ref[:, :, lanes] = result.reshape(LOADERS, 4, HD)
+            store = pltpu.make_async_copy(
+                ret_ref.at[:, :, lanes], out_ref.at[:, :, lanes], out_sem.at[head, array]
+            )
+            store.start()
+            stores.append(store)
+    for store in stores:
+        store.wait()
 
 
 SMEM = pl.BlockSpec(memory_space=pltpu.SMEM)
 VMEM = pl.BlockSpec(memory_space=pltpu.VMEM)
 HBM = pl.BlockSpec(memory_space=pltpu.HBM)
 PARAMS = pltpu.CompilerParams(vmem_limit_bytes=24 * 1024 * 1024)
+AHEAD = pl.CostEstimate(flops=60_000_000_000, bytes_accessed=200_000_000, transcendentals=0)
 PIECE = jax.ShapeDtypeStruct((ROWS, PART), BF)
 WHOLE = jax.ShapeDtypeStruct((ROWS, WIDTH), BF)
 
@@ -246,10 +261,10 @@
         scratch_shapes=[
             pltpu.VMEM((LOADERS, ROWS), jnp.int32),
             pltpu.VMEM((3, ROWS, WIDTH), BF),
-            pltpu.VMEM((N_SP, N_DP, 4, CHUNK), BF),
+            pltpu.VMEM((N_DP, N_SP, 4, CHUNK), BF),
             pltpu.SemaphoreType.DMA,
-            pltpu.SemaphoreType.DMA((N_SP, 3)),
-            pltpu.SemaphoreType.DMA((N_SP,)),
+            pltpu.SemaphoreType.DMA((3,)),
+            pltpu.SemaphoreType.DMA((3,)),
         ],
         compiler_params=PARAMS,
         name="pack",
@@ -265,7 +280,7 @@
         out_specs=(HBM,) * 3,
         scratch_shapes=[
             pltpu.VMEM((3, ROWS, WIDTH), BF),
-            pltpu.SemaphoreType.DMA((3, N_SP)),
+            pltpu.SemaphoreType.DMA((3,)),
         ],
         compiler_params=PARAMS,
         name="unpack",
@@ -296,6 +311,7 @@
         in_specs=[SMEM] * 4 + [VMEM] * (1 + N_SP),
         out_specs=VMEM,
         compiler_params=PARAMS,
+        cost_estimate=AHEAD,
         name="collect",
     )(me, plan, bins, guide, table, *pieces)
 
@@ -319,12 +335,14 @@
 def backward(me, chunks, raised, inverse, pieces):
     return pl.pallas_call(
         backward_kernel,
-        out_shape=jax.ShapeDtypeStruct((LOADERS, 4, CHUNK), BF),
+        out_shape=pltpu.HBM((LOADERS, 4, CHUNK), BF),
         in_specs=[SMEM] + [VMEM] * (3 + N_SP),
-        out_specs=VMEM,
+        out_specs=HBM,
         scratch_shapes=[
             pltpu.VMEM((4, ROWS, PART), BF),
             pltpu.VMEM((GROUP, PART), BF),
+            pltpu.VMEM((LOADERS, 4, CHUNK), BF),
+            pltpu.SemaphoreType.DMA((HEADS_DEV, 3)),
         ],
         compiler_params=PARAMS,
         name="backward",
@@ -363,7 +381,6 @@
     raised, inverse, *outs = forward(me, bias, live, chunks)
     out_pieces = swap_pieces(outs)
     grads = backward(me, chunks, raised, inverse, grad_pieces)
-    grads, out_pieces[2], out_pieces[3] = lax.optimization_barrier((grads, out_pieces[2], out_pieces[3]))
     back = exchange(grads)
     attn_out = collect(me, sample_plan, guide_bins, guide_table, table, out_pieces)
     return attn_out, *unpack(pick, back)

time: 99 us -> 95.4 us (0.964)
  local copies, waits for them, and re-layouts: 2.64 us -> 0.7 us
  starting transfers between devices: 21 us -> 19.9 us
    ppermute x6, waiting for transfers between devices: 4.29 us -> 0.8 us  [swap_pieces(): lax.ppermute(pieces[step], 'sp', [(i, i ^ step) for i in range(N_SP)])]
    all_to_all x2, waiting for transfers between devices: 51.5 us -> 54.1 us  [exchange(): lax.all_to_all(chunks, ('dp', 'sp'), split_axis=0, concat_axis=0, tiled=T...]
    unnamed x18 -> x14, local copies, waits for them, and re-layouts: 2.64 us -> 0.7 us
    pallas_call x1, Pallas kernels: 5.07 us -> 3.3 us  [pack(): pl.pallas_call(pack_kernel, out_shape=pltpu.HBM((N_DP, N_SP, 4, CHUNK), B...]
    ppermute x6, starting transfers between devices: 5.74 us -> 4.66 us  [swap_pieces(): lax.ppermute(pieces[step], 'sp', [(i, i ^ step) for i in range(N_SP)])]
    pallas_call x1, Pallas kernels: 4.39 us -> 5.4 us  [backward(): pl.pallas_call(backward_kernel, out_shape=pltpu.HBM((LOADERS, 4, CHUNK),...]
  transfers between devices with their start and end apart: 8 -> 8, of which waited for: 5 -> 3; matrix products, arithmetic and copies ran while one was open for 0% -> 0% of each run, Pallas kernels for 12% -> 15%
where the time goes in v3:
time: 95.4 us; the launch traced here: 95.1 us
  waiting for transfers between devices  54.9 us (58%)
  starting transfers between devices  19.9 us (21%)
  Pallas kernels  18.8 us (20%)
    all_to_all x2, waiting for transfers between devices, exchange(): lax.all_to_all(chunks, ('dp', 'sp'), split_axis=0, concat_axis=0, tiled=T...  54.1 us
    all_to_all x2, starting transfers between devices, exchange(): lax.all_to_all(chunks, ('dp', 'sp'), split_axis=0, concat_axis=0, tiled=T...  15.3 us
    pallas_call x1, Pallas kernels, backward(): pl.pallas_call(backward_kernel, out_shape=pltpu.HBM((LOADERS, 4, CHUNK),...  5.4 us
    pallas_call x1, Pallas kernels, forward(): pl.pallas_call(forward_kernel, out_shape=(jax.ShapeDtypeStruct((HEADS_DEV...  4.87 us
    ppermute x6, starting transfers between devices, swap_pieces(): lax.ppermute(pieces[step], 'sp', [(i, i ^ step) for i in range(N_SP)])  4.66 us
    pallas_call x1, Pallas kernels, pack(): pl.pallas_call(pack_kernel, out_shape=pltpu.HBM((N_DP, N_SP, 4, CHUNK), B...  3.3 us
    pallas_call x1, Pallas kernels, collect(): pl.pallas_call(collect_kernel, out_shape=WHOLE, in_specs=[SMEM] * 4 + [VM...  2.38 us
  transfers between devices with their start and end apart: 8, of which 3 were waited for; matrix products, arithmetic and copies ran while one was open for 0% of the time, Pallas kernels for 15%

profile of v3, /device:TPU:1, one launch (start us, length us, event | category | flops | bytes accessed | tf_op | source)
XLA Modules:
  0.0 95.1 jit_solution(6074516980846580892)
XLA Ops:
  0.6 3.3 %pack.1 = bf16[32,4,4,1920]{3,2,1,0:T(4,128)(2,1)} custom-call(s32[1]{0:T(128)} %bitcast.me_ref, s32[128,128]{1,0:T(8,128)} %bitcast.5, bf16[128,2560]{1,0:T(8,128)(2,1)} %q_ref.1, bf16[128,2560]{1,0:T(8,128)(2,1)} %k_ref.1, bf16[128,2560]{1,0:T(8,128)(2,1)} %v_ref.1), custom_call_target="tpu_custom_call" | custom-call | tf_op jit(solution)/shard_map/pack/pallas_call | solution.py:256
  3.9 0.0 copy-start
  4.0 0.0 copy-start.1
  4.0 0.0 copy-start.2
  4.0 0.0 copy-start.3
  4.0 0.0 copy-start.4
  4.0 0.0 copy-start.5
  4.0 11.5 %all-to-all-start = ((bf16[128,4,1920]{2,1,0:T(4,128)(2,1)}), bf16[128,4,1920]{2,1,0:T(4,128)(2,1)S(1)}, u32[]{:S(2)}, u32[]{:S(2)}) async-start(bf16[128,4,1920]{2,1,0:T(4,128)(2,1)} %bitcast.8), calls=%async_computation | async-start | bytes 3932160 | tf_op jit(solution)/shard_map/all_to_all | solution.py:353
  15.6 1.3 %spread.1 = (bf16[128,640]{1,0:T(8,128)(2,1)S(1)}, bf16[128,640]{1,0:T(8,128)(2,1)S(1)}, bf16[128,640]{1,0:T(8,128)(2,1)S(1)}, bf16[128,640]{1,0:T(8,128)(2,1)S(...) custom-call(s32[1]{0:T(128)} %bitcast.me_ref, s32[32]{0:T(128)S(1)} %copy-done.3, ...), custom_call_target="tpu_custom_call" | custom-call | tf_op jit(solution)/shard_map/spread/pallas_call | solution.py:291
  16.9 0.7 copy-done.6
  17.5 27.2 %all-to-all-done.recv_ref = bf16[128,4,1920]{2,1,0:T(4,128)(2,1)S(1)} async-done(((bf16[128,4,1920]{2,1,0:T(4,128)(2,1)}), bf16[128,4,1920]{2,1,0:T(4,128)(2,1)S(1)}, u32[]{:S(2)}, u32[]{:S(2)}) %all-to-all-start) | async-done | bytes 1966112 | tf_op jit(solution)/shard_map/all_to_all | solution.py:353
  44.7 0.9 collective-permute-start.3
  45.6 0.3 collective-permute-start.4
  45.9 1.3 %collective-permute-start.5 = (bf16[128,640]{1,0:T(8,128)(2,1)S(1)}, bf16[128,640]{1,0:T(8,128)(2,1)S(1)}, u32[]{:S(2)}, u32[]{:S(2)}) collective-permute-start(bf16[128,640]{1,0:T(8,128)(2,1)S(1)} %get-tuple-element.42), channel_id=1, source_target_pairs={{0,3},{1,2},{2,1},{3,0},{4,7},{5,6},{6,5},{7,4},{8,11},{9,10},{10,... | collective-permute-start | bytes 491528 | tf_op jit(solution)/shard_map/ppermute | solution.py:358
  47.2 4.9 %forward.1 = (bf16[5,512,512]{2,1,0:T(8,128)(2,1)S(1)}, f32[8,512]{1,0:T(8,128)S(1)}, bf16[128,640]{1,0:T(8,128)(2,1)S(1)}, bf16[128,640]{1,0:T(8,128)(2,1)}, bf...) custom-call(s32[1]{0:T(128)} %bitcast.me_ref, f32[512,128]{1,0:T(8,128)S(1)} %get-tuple-element.25.bias_ref, ...), custom_call_target="tpu_custom_call" | custom-call | tf_op jit(solution)/shard_map/forward/pallas_call | solution.py:320
  52.1 0.2 collective-permute-start
  52.3 0.3 collective-permute-start.1
  52.6 1.6 %collective-permute-start.2 = (bf16[128,640]{1,0:T(8,128)(2,1)S(1)}, bf16[128,640]{1,0:T(8,128)(2,1)}, u32[]{:S(2)}, u32[]{:S(2)}) collective-permute-start(bf16[128,640]{1,0:T(8,128)(2,1)S(1)} %get-tuple-element.35), channel_id=1, source_target_pairs={{0,3},{1,2},{2,1},{3,0},{4,7},{5,6},{6,5},{7,4},{8,11},{9,10},{10,... | collective-permute-start | bytes 491528 | tf_op jit(solution)/shard_map/ppermute | solution.py:358
  54.2 0.8 collective-permute-done.5.d3_ref
  55.0 5.4 %backward.1 = bf16[128,4,1920]{2,1,0:T(4,128)(2,1)} custom-call(s32[1]{0:T(128)} %bitcast.me_ref, bf16[128,4,1920]{2,1,0:T(4,128)(2,1)S(1)} %all-to-all-done.recv_ref, bf16[5,512,512]{2,1,0:T(8,128)(2,1)S(1)} %get-tuple-element.37.raised_ref, f32[8,512]{1,0:T(8,128)S(1)} %get-tuple-element.38.inverse_ref, bf16[128,640]{1,0:T(8,128)(2,1)S(1)} %get-tuple-element.39.d0_ref, ...), custom_call_target="tpu_custom_call" | custom-call | tf_op jit(solution)/shard_map/backward/pallas_call | solution.py:336
  60.4 3.8 %all-to-all-start.1 = ((bf16[128,4,1920]{2,1,0:T(4,128)(2,1)}), bf16[128,4,1920]{2,1,0:T(4,128)(2,1)S(1)}, u32[]{:S(2)}, u32[]{:S(2)}) async-start(bf16[128,4,1920]{2,1,0:T(4,128)(2,1)} %backward.1), calls=%async_computation.1 | async-start | bytes 3932160 | tf_op jit(solution)/shard_map/all_to_all | solution.py:353
  64.2 2.4 %collect.1 = bf16[128,2560]{1,0:T(8,128)(2,1)} custom-call(s32[1]{0:T(128)} %bitcast.me_ref, s32[32]{0:T(128)S(1)} %copy-done.4, s32[32]{0:T(128)S(1)} %copy-done.5, f32[8,20]{1,0:T(8,128)S(1)} %copy-done.2, s32[128,128]{1,0:T(8,128)S(1)} %bitcast.7, bf16[128,640]{1,0:T(8,128)(2,1)S(1)} %get-tuple-element.32.i0_ref, ...), custom_call_target="tpu_custom_call" | custom-call | flops 60000002048 | bytes 200000000 | tf_op jit(solution)/shard_map/collect/pallas_call | solution.py:308
  66.6 26.9 %all-to-all-done.1 = bf16[128,4,1920]{2,1,0:T(4,128)(2,1)S(1)} async-done(((bf16[128,4,1920]{2,1,0:T(4,128)(2,1)}), bf16[128,4,1920]{2,1,0:T(4,128)(2,1)S(1)}, u32[]{:S(2)}, u32[]{:S(2)}) %all-to-all-start.1) | async-done | bytes 1966112 | tf_op jit(solution)/shard_map/all_to_all | solution.py:353
  93.5 1.6 %unpack.1 = (bf16[128,2560]{1,0:T(8,128)(2,1)}, bf16[128,2560]{1,0:T(8,128)(2,1)}, bf16[128,2560]{1,0:T(8,128)(2,1)}) custom-call(bf16[128,128]{1,0:T(8,128)(2,1)S(1)} %get-tuple-element.36.pick_ref, bf16[32,4,4,1920]{3,2,1,0:T(4,128)(2,1)S(1)} %bitcast.4), custom_call_target="tpu_custom_call" | custom-call | tf_op jit(solution)/shard_map/unpack/pallas_call | solution.py:276
  (12 shorter events, 0.0 us)
Async XLA Ops:
  3.9 11.6 %copy-start = (bf16[128,2560]{1,0:T(8,128)(2,1)S(1)}, bf16[128,2560]{1,0:T(8,128)(2,1)}, u32[]{:S(2)}) copy-start(bf16[128,2560]{1,0:T(8,128)(2,1)} %cot_ref.1) | copy-start | bytes 1966084
  4.0 11.6 %copy-start.1 = (s32[16384]{0:T(1024)S(1)}, s32[16384]{0:T(1024)}, u32[]{:S(2)}) copy-start(s32[16384]{0:T(1024)} %param.17) | copy-start | bytes 196612
  4.0 11.6 %copy-start.2 = (f32[8,20]{1,0:T(8,128)S(1)}, f32[8,20]{1,0:T(8,128)}, u32[]{:S(2)}) copy-start(f32[8,20]{1,0:T(8,128)} %guide_ref.3) | copy-start | bytes 1924
  4.0 11.6 %copy-start.3 = (s32[32]{0:T(128)S(1)}, s32[32]{0:T(128)}, u32[]{:S(2)}) copy-start(s32[32]{0:T(128)} %lengths_ref.1) | copy-start | bytes 388
  4.0 11.6 %copy-start.4 = (s32[32]{0:T(128)S(1)}, s32[32]{0:T(128)}, u32[]{:S(2)}) copy-start(s32[32]{0:T(128)} %plan_ref.3) | copy-start | bytes 388
  4.0 11.6 %copy-start.5 = (s32[32]{0:T(128)S(1)}, s32[32]{0:T(128)}, u32[]{:S(2)}) copy-start(s32[32]{0:T(128)} %bins_ref.3) | copy-start | bytes 388
  4.0 40.7 %all-to-all-start = ((bf16[128,4,1920]{2,1,0:T(4,128)(2,1)}), bf16[128,4,1920]{2,1,0:T(4,128)(2,1)S(1)}, u32[]{:S(2)}, u32[]{:S(2)}) async-start(bf16[128,4,1920]{2,1,0:T(4,128)(2,1)} %bitcast.8), calls=%async_computation | async-start | bytes 3932160 | tf_op jit(solution)/shard_map/all_to_all | solution.py:353
  16.9 0.7 copy-start.6
  44.7 7.9 %collective-permute-start.3 = (bf16[128,640]{1,0:T(8,128)(2,1)}, bf16[128,640]{1,0:T(8,128)(2,1)S(1)}, u32[]{:S(2)}, u32[]{:S(2)}) collective-permute-start(bf16[128,640]{1,0:T(8,128)(2,1)} %copy-done.6), channel_id=1, source_target_pairs={{0,1},{1,0},{2,3},{3,2},{4,5},{5,4},{6,7},{7,6},{8,9},{9,8},{10,11... | collective-permute-start | bytes 491528 | tf_op jit(solution)/shard_map/ppermute | solution.py:358
  45.6 8.7 %collective-permute-start.4 = (bf16[128,640]{1,0:T(8,128)(2,1)S(1)}, bf16[128,640]{1,0:T(8,128)(2,1)S(1)}, u32[]{:S(2)}, u32[]{:S(2)}) collective-permute-start(bf16[128,640]{1,0:T(8,128)(2,1)S(1)} %get-tuple-element.41), channel_id=1, source_target_pairs={{0,2},{1,3},{2,0},{3,1},{4,6},{5,7},{6,4},{7,5},{8,10},{9,11},{10,... | collective-permute-start | bytes 491528 | tf_op jit(solution)/shard_map/ppermute | solution.py:358
  45.9 9.1 %collective-permute-start.5 = (bf16[128,640]{1,0:T(8,128)(2,1)S(1)}, bf16[128,640]{1,0:T(8,128)(2,1)S(1)}, u32[]{:S(2)}, u32[]{:S(2)}) collective-permute-start(bf16[128,640]{1,0:T(8,128)(2,1)S(1)} %get-tuple-element.42), channel_id=1, source_target_pairs={{0,3},{1,2},{2,1},{3,0},{4,7},{5,6},{6,5},{7,4},{8,11},{9,10},{10,... | collective-permute-start | bytes 491528 | tf_op jit(solution)/shard_map/ppermute | solution.py:358
  52.1 12.1 %collective-permute-start = (bf16[128,640]{1,0:T(8,128)(2,1)}, bf16[128,640]{1,0:T(8,128)(2,1)S(1)}, u32[]{:S(2)}, u32[]{:S(2)}) collective-permute-start(bf16[128,640]{1,0:T(8,128)(2,1)} %get-tuple-element.33), channel_id=1, source_target_pairs={{0,1},{1,0},{2,3},{3,2},{4,5},{5,4},{6,7},{7,6},{8,9},{9,8},{10,11... | collective-permute-start | bytes 491528 | tf_op jit(solution)/shard_map/ppermute | solution.py:358
  52.3 11.9 %collective-permute-start.1 = (bf16[128,640]{1,0:T(8,128)(2,1)}, bf16[128,640]{1,0:T(8,128)(2,1)}, u32[]{:S(2)}, u32[]{:S(2)}) collective-permute-start(bf16[128,640]{1,0:T(8,128)(2,1)} %get-tuple-element.34), channel_id=1, source_target_pairs={{0,2},{1,3},{2,0},{3,1},{4,6},{5,7},{6,4},{7,5},{8,10},{9,11},{10,... | collective-permute-start | bytes 491528 | tf_op jit(solution)/shard_map/ppermute | solution.py:358
  52.6 11.6 %collective-permute-start.2 = (bf16[128,640]{1,0:T(8,128)(2,1)S(1)}, bf16[128,640]{1,0:T(8,128)(2,1)}, u32[]{:S(2)}, u32[]{:S(2)}) collective-permute-start(bf16[128,640]{1,0:T(8,128)(2,1)S(1)} %get-tuple-element.35), channel_id=1, source_target_pairs={{0,3},{1,2},{2,1},{3,0},{4,7},{5,6},{6,5},{7,4},{8,11},{9,10},{10,... | collective-permute-start | bytes 491528 | tf_op jit(solution)/shard_map/ppermute | solution.py:358
  60.4 33.1 %all-to-all-start.1 = ((bf16[128,4,1920]{2,1,0:T(4,128)(2,1)}), bf16[128,4,1920]{2,1,0:T(4,128)(2,1)S(1)}, u32[]{:S(2)}, u32[]{:S(2)}) async-start(bf16[128,4,1920]{2,1,0:T(4,128)(2,1)} %backward.1), calls=%async_computation.1 | async-start | bytes 3932160 | tf_op jit(solution)/shard_map/all_to_all | solution.py:353

commit v4 on v3

--- a/solution.py
+++ b/solution.py
@@ -67,7 +67,26 @@
     return value
 
 
-def pack_kernel(me_ref, table_ref, q_ref, k_ref, v_ref, out_ref, index_ref, in_ref, send_ref, index_sem, in_sem, out_sem):
+def pack_kernel(
+    me_ref,
+    table_ref,
+    q_ref,
+    k_ref,
+    v_ref,
+    cot_ref,
+    out_ref,
+    p0_ref,
+    p1_ref,
+    p2_ref,
+    p3_ref,
+    index_ref,
+    in_ref,
+    send_ref,
+    index_sem,
+    in_sem,
+    out_sem,
+    piece_sem,
+):
     index = pltpu.make_async_copy(table_ref, index_ref, index_sem)
     index.start()
     loads = []
@@ -75,6 +94,12 @@
         load = pltpu.make_async_copy(ref, in_ref.at[array], in_sem.at[array])
         load.start()
         loads.append(load)
+    pieces = []
+    for step, ref in enumerate((p0_ref, p1_ref, p2_ref, p3_ref)):
+        lanes = part_lanes(jnp.bitwise_xor(me_ref[0] % N_SP, step))
+        piece = pltpu.make_async_copy(cot_ref.at[:, lanes], ref, piece_sem.at[step])
+        piece.start()
+        pieces.append(piece)
     index.wait()
     pick = row_picker(index_ref[...], me_ref[0])
     stores = []
@@ -89,6 +114,8 @@
         )
         store.start()
         stores.append(store)
+    for piece in pieces:
+        piece.wait()
     for store in stores:
         store.wait()
 
@@ -107,33 +134,40 @@
         store.wait()
 
 
-def spread_kernel(
+def prepare_kernel(
     me_ref,
     lengths_ref,
     plan_ref,
     bins_ref,
     guide_ref,
     table_ref,
-    cot_ref,
-    p0_ref,
-    p1_ref,
-    p2_ref,
-    p3_ref,
+    d0_ref,
+    d1_ref,
+    d2_ref,
+    d3_ref,
+    grad_ref,
     bias_ref,
     live_ref,
     pick_ref,
     gated_ref,
+    rows_ref,
 ):
     me = me_ref[0]
     group, mine = me // N_SP, me % N_SP
     group_len = sample_of(group, plan_ref, lengths_ref)
     group_bin = sample_of(group, plan_ref, bins_ref)
-    for head in range(HEADS):
-        lanes = pl.ds(head * HD, HD)
-        gated_ref[:, lanes] = (guide_ref[group_bin, head] * cot_ref[:, lanes].astype(F32)).astype(BF)
-    order = onehot(table_ref[pl.ds(me, 1), :] // ROWS == iota((LOADERS, ROWS), 0))
-    for step, ref in enumerate((p0_ref, p1_ref, p2_ref, p3_ref)):
-        ref[...] = dot(order, gated_ref[:, part_lanes(jnp.bitwise_xor(mine, step))]).astype(BF)
+    for step, ref in enumerate((d0_ref, d1_ref, d2_ref, d3_ref)):
+        for head in range(HEADS_DEV):
+            lanes = pl.ds(head * HD, HD)
+            gate = guide_ref[group_bin, mine * HEADS_DEV + head]
+            gated_ref[jnp.bitwise_xor(mine, step), :, lanes] = (gate * ref[:, lanes].astype(F32)).astype(BF)
+    for quarter in range(4):
+        own = table_ref[pl.ds(group * N_SP + quarter, 1), :] // ROWS
+        rows_ref[quarter] = dot(onehot(own == iota((LOADERS, ROWS), 0)), gated_ref[quarter]).astype(BF)
+    order = quarters_first()
+    for half in range(2):
+        rows = rows_ref[:, pl.ds(half * 64, 64), :].reshape(256, PART)
+        grad_ref[pl.ds(half * 256, 256), :] = dot_tn(order, rows).astype(BF)
     pick_ref[...] = row_picker(table_ref[...], me).astype(F32).T.astype(BF)
     row = iota((GROUP, ROWS), 0)
     source = jnp.zeros((GROUP, ROWS), jnp.int32)
@@ -167,7 +201,6 @@
     mine = me_ref[0] % N_SP
     live = live_ref[0:1, :]
     bias = bias_ref[:, 0:1]
-    order = quarters_first()
     for head in range(HEADS_DEV):
         query = recv_ref[:, :, columns(head, 0)].reshape(GROUP, HD)
         key = recv_ref[:, :, columns(head, 1)].reshape(GROUP, HD)
@@ -179,37 +212,15 @@
         weights = raised.astype(BF)
         raised_ref[head] = weights
         inverse_ref[head : head + 1, :] = inverse
-        output = (dot_tn(value, weights) * inverse).astype(BF)
-        for half in range(2):
-            rows = dot_nt(order, output[:, half * 256 : (half + 1) * 256]).astype(BF)
-            out_ref[:, pl.ds(half * 64, 64), pl.ds(head * HD, HD)] = rows.reshape(4, 64, HD)
+        output = dot_tn(value, weights) * inverse
+        out_ref[:, pl.ds(head * HD, HD)] = output.T.astype(BF)
     inverse_ref[HEADS_DEV:, :] = jnp.zeros((8 - HEADS_DEV, GROUP), F32)
     for step, ref in enumerate((o0_ref, o1_ref, o2_ref, o3_ref)):
-        ref[...] = out_ref[jnp.bitwise_xor(mine, step)]
-
-
-def backward_kernel(
-    me_ref,
-    recv_ref,
-    raised_ref,
-    inverse_ref,
-    d0_ref,
-    d1_ref,
-    d2_ref,
-    d3_ref,
-    out_ref,
-    cot_ref,
-    grad_ref,
-    ret_ref,
-    out_sem,
-):
-    mine = me_ref[0] % N_SP
-    for step, ref in enumerate((d0_ref, d1_ref, d2_ref, d3_ref)):
-        cot_ref[jnp.bitwise_xor(mine, step)] = ref[...]
-    order = quarters_first()
-    for half in range(2):
-        rows = cot_ref[:, pl.ds(half * 64, 64), :].reshape(256, PART)
-        grad_ref[pl.ds(half * 256, 256), :] = dot_tn(order, rows).astype(BF)
+        quarter = onehot(iota((ROWS, GROUP), 1) == 4 * iota((ROWS, GROUP), 0) + jnp.bitwise_xor(mine, step))
+        ref[...] = dot(quarter, out_ref[...]).astype(BF)
+
+
+def backward_kernel(recv_ref, raised_ref, inverse_ref, grad_ref, out_ref, ret_ref, out_sem):
     inverse_columns = inverse_ref[...].T
     stores = []
     for head in range(HEADS_DEV):
@@ -252,12 +263,12 @@
     return pltpu.with_memory_space_constraint(array, pltpu.HBM)
 
 
-def pack(me, table, queries, keys, values):
-    chunks = pl.pallas_call(
+def pack(me, table, queries, keys, values, cotangent):
+    chunks, *pieces = pl.pallas_call(
         pack_kernel,
-        out_shape=pltpu.HBM((N_DP, N_SP, 4, CHUNK), BF),
-        in_specs=[SMEM] + [HBM] * 4,
-        out_specs=HBM,
+        out_shape=(pltpu.HBM((N_DP, N_SP, 4, CHUNK), BF),) + (PIECE,) * N_SP,
+        in_specs=[SMEM] + [HBM] * 5,
+        out_specs=(HBM,) + (VMEM,) * N_SP,
         scratch_shapes=[
             pltpu.VMEM((LOADERS, ROWS), jnp.int32),
             pltpu.VMEM((3, ROWS, WIDTH), BF),
@@ -265,11 +276,12 @@
             pltpu.SemaphoreType.DMA,
             pltpu.SemaphoreType.DMA((3,)),
             pltpu.SemaphoreType.DMA((3,)),
+            pltpu.SemaphoreType.DMA((N_SP,)),
         ],
         compiler_params=PARAMS,
         name="pack",
-    )(me, in_hbm(table), in_hbm(queries), in_hbm(keys), in_hbm(values))
-    return chunks.reshape(LOADERS, 4, CHUNK)
+    )(me, in_hbm(table), in_hbm(queries), in_hbm(keys), in_hbm(values), in_hbm(cotangent))
+    return chunks.reshape(LOADERS, 4, CHUNK), pieces
 
 
 def unpack(pick, chunks):
@@ -287,21 +299,22 @@
     )(pick, chunks.reshape(N_DP, N_SP, 4, CHUNK))
 
 
-def spread(me, lengths, plan, bins, guide, table, cotangent):
+def prepare(me, lengths, plan, bins, guide, table, pieces):
     return pl.pallas_call(
-        spread_kernel,
-        out_shape=(PIECE,) * N_SP
-        + (
+        prepare_kernel,
+        out_shape=(
+            jax.ShapeDtypeStruct((GROUP, PART), BF),
             jax.ShapeDtypeStruct((GROUP, HD), F32),
             jax.ShapeDtypeStruct((8, GROUP), F32),
             jax.ShapeDtypeStruct((ROWS, LOADERS), BF),
         ),
-        in_specs=[SMEM] * 5 + [VMEM] * 2,
-        out_specs=(VMEM,) * (N_SP + 3),
-        scratch_shapes=[pltpu.VMEM((ROWS, WIDTH), BF)],
-        compiler_params=PARAMS,
-        name="spread",
-    )(me, lengths, plan, bins, guide, table, cotangent)
+        in_specs=[SMEM] * 5 + [VMEM] * (1 + N_SP),
+        out_specs=(VMEM,) * 4,
+        scratch_shapes=[pltpu.VMEM((4, ROWS, PART), BF), pltpu.VMEM((4, ROWS, PART), BF)],
+        compiler_params=PARAMS,
+        cost_estimate=AHEAD,
+        name="prepare",
+    )(me, lengths, plan, bins, guide, table, *pieces)
 
 
 def collect(me, plan, bins, guide, table, pieces):
@@ -326,27 +339,25 @@
         + (PIECE,) * N_SP,
         in_specs=[SMEM] + [VMEM] * 3,
         out_specs=(VMEM,) * (2 + N_SP),
-        scratch_shapes=[pltpu.VMEM((4, ROWS, PART), BF)],
+        scratch_shapes=[pltpu.VMEM((GROUP, PART), BF)],
         compiler_params=PARAMS,
         name="forward",
     )(me, bias, live, chunks)
 
 
-def backward(me, chunks, raised, inverse, pieces):
+def backward(chunks, raised, inverse, grad):
     return pl.pallas_call(
         backward_kernel,
         out_shape=pltpu.HBM((LOADERS, 4, CHUNK), BF),
-        in_specs=[SMEM] + [VMEM] * (3 + N_SP),
+        in_specs=[VMEM] * 4,
         out_specs=HBM,
         scratch_shapes=[
-            pltpu.VMEM((4, ROWS, PART), BF),
-            pltpu.VMEM((GROUP, PART), BF),
             pltpu.VMEM((LOADERS, 4, CHUNK), BF),
             pltpu.SemaphoreType.DMA((HEADS_DEV, 3)),
         ],
         compiler_params=PARAMS,
         name="backward",
-    )(me, chunks, raised, inverse, *pieces)
+    )(chunks, raised, inverse, grad)
 
 
 def exchange(chunks):
@@ -372,15 +383,14 @@
 ):
     me = (lax.axis_index("dp") * N_SP + lax.axis_index("sp")).astype(jnp.int32).reshape(1)
     table = block_source.reshape(LOADERS, ROWS)
-    chunks = exchange(pack(me, table, queries, key_rows, value_rows))
-    *pieces, bias, live, pick = spread(
-        me, lengths, sample_plan, guide_bins, guide_table, table, cotangent
+    packed, pieces = pack(me, table, queries, key_rows, value_rows, cotangent)
+    chunks = exchange(packed)
+    grad, bias, live, pick = prepare(
+        me, lengths, sample_plan, guide_bins, guide_table, table, swap_pieces(pieces)
     )
-    chunks, pieces = lax.optimization_barrier((chunks, pieces))
-    grad_pieces = swap_pieces(pieces)
     raised, inverse, *outs = forward(me, bias, live, chunks)
     out_pieces = swap_pieces(outs)
-    grads = backward(me, chunks, raised, inverse, grad_pieces)
+    grads = backward(chunks, raised, inverse, grad)
     back = exchange(grads)
     attn_out = collect(me, sample_plan, guide_bins, guide_table, table, out_pieces)
     return attn_out, *unpack(pick, back)

time: 95.4 us -> 93.8 us (0.983)
  waiting for transfers between devices: 54.9 us -> 52.9 us
    all_to_all x2, starting transfers between devices: 15.3 us -> 13.9 us  [exchange(): lax.all_to_all(chunks, ('dp', 'sp'), split_axis=0, concat_axis=0, tiled=T...]
    all_to_all x2, waiting for transfers between devices: 54.1 us -> 52.9 us  [exchange(): lax.all_to_all(chunks, ('dp', 'sp'), split_axis=0, concat_axis=0, tiled=T...]
    ppermute x6, starting transfers between devices: 4.66 us -> 5.74 us  [swap_pieces(): lax.ppermute(pieces[step], 'sp', [(i, i ^ step) for i in range(N_SP)])]
  transfers between devices with their start and end apart: 8 -> 8, of which waited for: 3 -> 2; matrix products, arithmetic and copies ran while one was open for 0% -> 0% of each run, Pallas kernels for 15% -> 10%
where the time goes in v4:
time: 93.8 us; the launch traced here: 93.4 us
  waiting for transfers between devices  52.9 us (56%)
  starting transfers between devices  19.7 us (21%)
  Pallas kernels  18.5 us (20%)
  local copies, waits for them, and re-layouts  1.59 us (2%)
    all_to_all x2, waiting for transfers between devices, exchange(): lax.all_to_all(chunks, ('dp', 'sp'), split_axis=0, concat_axis=0, tiled=T...  52.9 us
    all_to_all x2, starting transfers between devices, exchange(): lax.all_to_all(chunks, ('dp', 'sp'), split_axis=0, concat_axis=0, tiled=T...  13.9 us
    ppermute x6, starting transfers between devices, swap_pieces(): lax.ppermute(pieces[step], 'sp', [(i, i ^ step) for i in range(N_SP)])  5.74 us
    pallas_call x1, Pallas kernels, backward(): pl.pallas_call(backward_kernel, out_shape=pltpu.HBM((LOADERS, 4, CHUNK),...  5.42 us
    pallas_call x1, Pallas kernels, forward(): pl.pallas_call(forward_kernel, out_shape=(jax.ShapeDtypeStruct((HEADS_DEV...  4.08 us
    pallas_call x1, Pallas kernels, pack(): pl.pallas_call(pack_kernel, out_shape=(pltpu.HBM((N_DP, N_SP, 4, CHUNK),...  3.49 us
    pallas_call x1, Pallas kernels, collect(): pl.pallas_call(collect_kernel, out_shape=WHOLE, in_specs=[SMEM] * 4 + [VM...  2.38 us
  transfers between devices with their start and end apart: 8, of which 2 were waited for; matrix products, arithmetic and copies ran while one was open for 0% of the time, Pallas kernels for 10%

profile of v4, /device:TPU:1, one launch (start us, length us, event | category | flops | bytes accessed | tf_op | source)
XLA Modules:
  0.0 93.4 jit_solution(17888364830050014941)
XLA Ops:
  0.6 3.5 %pack.1 = (bf16[32,4,4,1920]{3,2,1,0:T(4,128)(2,1)}, bf16[128,640]{1,0:T(8,128)(2,1)S(1)}, bf16[128,640]{1,0:T(8,128)(2,1)S(1)}, bf16[128,640]{1,0:T(8,128)(2,1)S(1)}, bf16[128,640]{1,0:T(8,128)(2,1)S(1)}) custom-call(s32[1]{0:T(128)} %bitcast.me_ref, s32[128,128]{1,0:T(8,128)} %bitcast.5, bf16[128,2560]{1,0:T(8,128)(2,1)} %q_ref.1, ...), custom_call_target="tpu_custom_call" | custom-call | tf_op jit(solution)/shard_map/pack/pallas_call | solution.py:267
  4.1 1.5 %collective-permute-start = (bf16[128,640]{1,0:T(8,128)(2,1)S(1)}, bf16[128,640]{1,0:T(8,128)(2,1)S(1)}, u32[]{:S(2)}, u32[]{:S(2)}) collective-permute-start(bf16[128,640]{1,0:T(8,128)(2,1)S(1)} %get-tuple-element.23), channel_id=1, source_target_pairs={{0,1},{1,0},{2,3},{3,2},{4,5},{5,4},{6,7},{7,6},{8,9},{9,8},{10,11... | collective-permute-start | bytes 491528 | tf_op jit(solution)/shard_map/ppermute | solution.py:369
  5.6 1.3 %collective-permute-start.1 = (bf16[128,640]{1,0:T(8,128)(2,1)S(1)}, bf16[128,640]{1,0:T(8,128)(2,1)S(1)}, u32[]{:S(2)}, u32[]{:S(2)}) collective-permute-start(bf16[128,640]{1,0:T(8,128)(2,1)S(1)} %get-tuple-element.24), channel_id=1, source_target_pairs={{0,2},{1,3},{2,0},{3,1},{4,6},{5,7},{6,4},{7,5},{8,10},{9,11},{10,... | collective-permute-start | bytes 491528 | tf_op jit(solution)/shard_map/ppermute | solution.py:369
  6.9 0.4 collective-permute-start.2
  7.4 0.0 copy-start.6
  7.4 10.2 %all-to-all-start = ((bf16[128,4,1920]{2,1,0:T(4,128)(2,1)}), bf16[128,4,1920]{2,1,0:T(4,128)(2,1)S(1)}, u32[]{:S(2)}, u32[]{:S(2)}) async-start(bf16[128,4,1920]{2,1,0:T(4,128)(2,1)} %bitcast.8), calls=%async_computation | async-start | bytes 3932160 | tf_op jit(solution)/shard_map/all_to_all | solution.py:364
  17.6 0.0 collective-permute-done.d1_ref
  17.6 0.0 collective-permute-done.2.d3_ref
  17.7 0.0 copy-start.1
  17.7 0.7 copy-done.1
  18.4 0.0 copy-start.2
  18.4 0.9 copy-done.2
  19.3 1.5 %prepare.1 = (bf16[512,640]{1,0:T(8,128)(2,1)S(1)}, f32[512,128]{1,0:T(8,128)S(1)}, f32[8,512]{1,0:T(8,128)S(1)}, bf16[128,128]{1,0:T(8,128)(2,1)S(1)}) custom-call(s32[1]{0:T(128)} %bitcast.me_ref, s32[32]{0:T(128)S(1)} %copy-done.4, s32[32]{0:T(128)S(1)} %copy-done.5, s32[32]{0:T(128)S(1)} %copy-done.6, f32[8,20]{1,0:T(8,128)S(1)} %copy-done.3, ...), custom_call_target="tpu_custom_call" | custom-call | flops 60000002048 | bytes 200000000 | tf_op jit(solution)/shard_map/prepare/pallas_call | solution.py:303
  20.8 26.0 %all-to-all-done.recv_ref = bf16[128,4,1920]{2,1,0:T(4,128)(2,1)S(1)} async-done(((bf16[128,4,1920]{2,1,0:T(4,128)(2,1)}), bf16[128,4,1920]{2,1,0:T(4,128)(2,1)S(1)}, u32[]{:S(2)}, u32[]{:S(2)}) %all-to-all-start) | async-done | bytes 1966112 | tf_op jit(solution)/shard_map/all_to_all | solution.py:364
  46.8 4.1 %forward.1 = (bf16[5,512,512]{2,1,0:T(8,128)(2,1)S(1)}, f32[8,512]{1,0:T(8,128)S(1)}, bf16[128,640]{1,0:T(8,128)(2,1)S(1)}, bf16[128,640]{1,0:T(8,128)(2,1)}, bf...) custom-call(s32[1]{0:T(128)} %bitcast.me_ref, f32[512,128]{1,0:T(8,128)S(1)} %get-tuple-element.26.bias_ref, ...), custom_call_target="tpu_custom_call" | custom-call | tf_op jit(solution)/shard_map/forward/pallas_call | solution.py:333
  50.9 0.9 collective-permute-start.3
  51.8 0.3 collective-permute-start.4
  52.1 1.3 %collective-permute-start.5 = (bf16[128,640]{1,0:T(8,128)(2,1)S(1)}, bf16[128,640]{1,0:T(8,128)(2,1)}, u32[]{:S(2)}, u32[]{:S(2)}) collective-permute-start(bf16[128,640]{1,0:T(8,128)(2,1)S(1)} %get-tuple-element.32), channel_id=1, source_target_pairs={{0,3},{1,2},{2,1},{3,0},{4,7},{5,6},{6,5},{7,4},{8,11},{9,10},{10,... | collective-permute-start | bytes 491528 | tf_op jit(solution)/shard_map/ppermute | solution.py:369
  53.4 5.4 %backward.1 = bf16[128,4,1920]{2,1,0:T(4,128)(2,1)} custom-call(bf16[128,4,1920]{2,1,0:T(4,128)(2,1)S(1)} %all-to-all-done.recv_ref, bf16[5,512,512]{2,1,0:T(8,128)(2,1)S(1)} %get-tuple-element.34.raised_ref, f32[8,512]{1,0:T(8,128)S(1)} %get-tuple-element.35.inverse_ref, bf16[512,640]{1,0:T(8,128)(2,1)S(1)} %get-tuple-element.36.grad_ref), custom_call_target="tpu_custom_call" | custom-call | tf_op jit(solution)/shard_map/backward/pallas_call | solution.py:349
  58.8 3.7 %all-to-all-start.1 = ((bf16[128,4,1920]{2,1,0:T(4,128)(2,1)}), bf16[128,4,1920]{2,1,0:T(4,128)(2,1)S(1)}, u32[]{:S(2)}, u32[]{:S(2)}) async-start(bf16[128,4,1920]{2,1,0:T(4,128)(2,1)} %backward.1), calls=%async_computation.1 | async-start | bytes 3932160 | tf_op jit(solution)/shard_map/all_to_all | solution.py:364
  62.5 0.0 collective-permute-done.3.i1_ref
  62.5 2.4 %collect.1 = bf16[128,2560]{1,0:T(8,128)(2,1)} custom-call(s32[1]{0:T(128)} %bitcast.me_ref, s32[32]{0:T(128)S(1)} %copy-done.5, s32[32]{0:T(128)S(1)} %copy-done.6, f32[8,20]{1,0:T(8,128)S(1)} %copy-done.3, s32[128,128]{1,0:T(8,128)S(1)} %bitcast.7, bf16[128,640]{1,0:T(8,128)(2,1)S(1)} %get-tuple-element.29.i0_ref, ...), custom_call_target="tpu_custom_call" | custom-call | flops 60000002048 | bytes 200000000 | tf_op jit(solution)/shard_map/collect/pallas_call | solution.py:321
  64.9 26.9 %all-to-all-done.1 = bf16[128,4,1920]{2,1,0:T(4,128)(2,1)S(1)} async-done(((bf16[128,4,1920]{2,1,0:T(4,128)(2,1)}), bf16[128,4,1920]{2,1,0:T(4,128)(2,1)S(1)}, u32[]{:S(2)}, u32[]{:S(2)}) %all-to-all-start.1) | async-done | bytes 1966112 | tf_op jit(solution)/shard_map/all_to_all | solution.py:364
  91.8 1.6 %unpack.1 = (bf16[128,2560]{1,0:T(8,128)(2,1)}, bf16[128,2560]{1,0:T(8,128)(2,1)}, bf16[128,2560]{1,0:T(8,128)(2,1)}) custom-call(bf16[128,128]{1,0:T(8,128)(2,1)S(1)} %get-tuple-element.33.pick_ref, bf16[32,4,4,1920]{3,2,1,0:T(4,128)(2,1)S(1)} %bitcast.4), custom_call_target="tpu_custom_call" | custom-call | tf_op jit(solution)/shard_map/unpack/pallas_call | solution.py:288
  (12 shorter events, 0.0 us)
Async XLA Ops:
  4.1 13.5 %collective-permute-start = (bf16[128,640]{1,0:T(8,128)(2,1)S(1)}, bf16[128,640]{1,0:T(8,128)(2,1)S(1)}, u32[]{:S(2)}, u32[]{:S(2)}) collective-permute-start(bf16[128,640]{1,0:T(8,128)(2,1)S(1)} %get-tuple-element.23), channel_id=1, source_target_pairs={{0,1},{1,0},{2,3},{3,2},{4,5},{5,4},{6,7},{7,6},{8,9},{9,8},{10,11... | collective-permute-start | bytes 491528 | tf_op jit(solution)/shard_map/ppermute | solution.py:369
  5.6 12.0 %collective-permute-start.1 = (bf16[128,640]{1,0:T(8,128)(2,1)S(1)}, bf16[128,640]{1,0:T(8,128)(2,1)S(1)}, u32[]{:S(2)}, u32[]{:S(2)}) collective-permute-start(bf16[128,640]{1,0:T(8,128)(2,1)S(1)} %get-tuple-element.24), channel_id=1, source_target_pairs={{0,2},{1,3},{2,0},{3,1},{4,6},{5,7},{6,4},{7,5},{8,10},{9,11},{10,... | collective-permute-start | bytes 491528 | tf_op jit(solution)/shard_map/ppermute | solution.py:369
  6.9 10.7 %collective-permute-start.2 = (bf16[128,640]{1,0:T(8,128)(2,1)S(1)}, bf16[128,640]{1,0:T(8,128)(2,1)S(1)}, u32[]{:S(2)}, u32[]{:S(2)}) collective-permute-start(bf16[128,640]{1,0:T(8,128)(2,1)S(1)} %get-tuple-element.25), channel_id=1, source_target_pairs={{0,3},{1,2},{2,1},{3,0},{4,7},{5,6},{6,5},{7,4},{8,11},{9,10},{10,... | collective-permute-start | bytes 491528 | tf_op jit(solution)/shard_map/ppermute | solution.py:369
  7.4 11.0 %copy-start = (s32[16384]{0:T(1024)S(1)}, s32[16384]{0:T(1024)}, u32[]{:S(2)}) copy-start(s32[16384]{0:T(1024)} %param.17) | copy-start | bytes 196612
  7.4 11.0 %copy-start.3 = (f32[8,20]{1,0:T(8,128)S(1)}, f32[8,20]{1,0:T(8,128)}, u32[]{:S(2)}) copy-start(f32[8,20]{1,0:T(8,128)} %guide_ref.3) | copy-start | bytes 1924
  7.4 11.0 %copy-start.4 = (s32[32]{0:T(128)S(1)}, s32[32]{0:T(128)}, u32[]{:S(2)}) copy-start(s32[32]{0:T(128)} %lengths_ref.1) | copy-start | bytes 388
  7.4 11.0 %copy-start.5 = (s32[32]{0:T(128)S(1)}, s32[32]{0:T(128)}, u32[]{:S(2)}) copy-start(s32[32]{0:T(128)} %plan_ref.3) | copy-start | bytes 388
  7.4 11.0 %copy-start.6 = (s32[32]{0:T(128)S(1)}, s32[32]{0:T(128)}, u32[]{:S(2)}) copy-start(s32[32]{0:T(128)} %bins_ref.3) | copy-start | bytes 388
  7.4 39.4 %all-to-all-start = ((bf16[128,4,1920]{2,1,0:T(4,128)(2,1)}), bf16[128,4,1920]{2,1,0:T(4,128)(2,1)S(1)}, u32[]{:S(2)}, u32[]{:S(2)}) async-start(bf16[128,4,1920]{2,1,0:T(4,128)(2,1)} %bitcast.8), calls=%async_computation | async-start | bytes 3932160 | tf_op jit(solution)/shard_map/all_to_all | solution.py:364
  17.7 0.7 copy-start.1
  18.4 0.9 copy-start.2
  50.9 11.6 %collective-permute-start.3 = (bf16[128,640]{1,0:T(8,128)(2,1)}, bf16[128,640]{1,0:T(8,128)(2,1)S(1)}, u32[]{:S(2)}, u32[]{:S(2)}) collective-permute-start(bf16[128,640]{1,0:T(8,128)(2,1)} %get-tuple-element.30), channel_id=1, source_target_pairs={{0,1},{1,0},{2,3},{3,2},{4,5},{5,4},{6,7},{7,6},{8,9},{9,8},{10,11... | collective-permute-start | bytes 491528 | tf_op jit(solution)/shard_map/ppermute | solution.py:369
  51.8 10.8 %collective-permute-start.4 = (bf16[128,640]{1,0:T(8,128)(2,1)S(1)}, bf16[128,640]{1,0:T(8,128)(2,1)}, u32[]{:S(2)}, u32[]{:S(2)}) collective-permute-start(bf16[128,640]{1,0:T(8,128)(2,1)S(1)} %get-tuple-element.31), channel_id=1, source_target_pairs={{0,2},{1,3},{2,0},{3,1},{4,6},{5,7},{6,4},{7,5},{8,10},{9,11},{10,... | collective-permute-start | bytes 491528 | tf_op jit(solution)/shard_map/ppermute | solution.py:369
  52.1 10.5 %collective-permute-start.5 = (bf16[128,640]{1,0:T(8,128)(2,1)S(1)}, bf16[128,640]{1,0:T(8,128)(2,1)}, u32[]{:S(2)}, u32[]{:S(2)}) collective-permute-start(bf16[128,640]{1,0:T(8,128)(2,1)S(1)} %get-tuple-element.32), channel_id=1, source_target_pairs={{0,3},{1,2},{2,1},{3,0},{4,7},{5,6},{6,5},{7,4},{8,11},{9,10},{10,... | collective-permute-start | bytes 491528 | tf_op jit(solution)/shard_map/ppermute | solution.py:369
  58.8 33.0 %all-to-all-start.1 = ((bf16[128,4,1920]{2,1,0:T(4,128)(2,1)}), bf16[128,4,1920]{2,1,0:T(4,128)(2,1)S(1)}, u32[]{:S(2)}, u32[]{:S(2)}) async-start(bf16[128,4,1920]{2,1,0:T(4,128)(2,1)} %backward.1), calls=%async_computation.1 | async-start | bytes 3932160 | tf_op jit(solution)/shard_map/all_to_all | solution.py:364

commit v5 on v4

v5 whole, which is shorter than its diff:
```python
import jax
import jax.numpy as jnp
from jax import lax
from jax.experimental import pallas as pl
from jax.experimental.pallas import tpu as pltpu
from jax.sharding import PartitionSpec as P

HEADS = 20
HD = 128
N_DP = 32
N_SP = 4
LOADERS = N_DP * N_SP
ROWS = 128
GROUP = 512
HEADS_DEV = HEADS // N_SP
WIDTH = HEADS * HD
PART = HEADS_DEV * HD
CHUNK = 3 * PART
SCALE = HD ** (-0.5)
LOG2E = 1.4426950408889634
BF = jnp.bfloat16
F32 = jnp.float32


def dot(a, b):
    return jnp.dot(a, b, preferred_element_type=F32)


def dot_nt(a, b):
    return lax.dot_general(a, b, (((1,), (1,)), ((), ())), preferred_element_type=F32)


def dot_tn(a, b):
    return lax.dot_general(a, b, (((0,), (0,)), ((), ())), preferred_element_type=F32)


def iota(shape, dim):
    return lax.broadcasted_iota(jnp.int32, shape, dim)


def onehot(hit):
    return jnp.where(hit, 1.0, 0.0).astype(BF)


def row_picker(table, me):
    slot = jnp.sum(jnp.where(table // ROWS == me, table % ROWS, 0), axis=1, keepdims=True)
    return onehot(slot == iota((LOADERS, ROWS), 1))


def quarters_first():
    row, col = iota((256, 256), 0), iota((256, 256), 1)
    return onehot(col == (row % 64) * 4 + row // 64)


def columns(head, array):
    return pl.ds((array * HEADS_DEV + head) * HD, HD)


def part_lanes(index):
    return pl.ds(pl.multiple_of(index * PART, HD), PART)


def sample_of(group, plan_ref, value_ref):
    value = jnp.int32(0)
    for sample in range(N_DP):
        value = jnp.where(plan_ref[sample] == group, value_ref[sample], value)
    return value


def pack_kernel(
    me_ref,
    table_ref,
    q_ref,
    k_ref,
    v_ref,
    cot_ref,
    out_ref,
    near_ref,
    far_ref,
    index_ref,
    in_ref,
    send_ref,
    stage_ref,
    index_sem,
    in_sem,
    out_sem,
    piece_sem,
    near_sem,
):
    index = pltpu.make_async_copy(table_ref, index_ref, index_sem)
    index.start()
    loads = []
    for array, ref in enumerate((q_ref, k_ref, v_ref)):
        load = pltpu.make_async_copy(ref, in_ref.at[array], in_sem.at[array])
        load.start()
        loads.append(load)
    pieces = []
    for step, ref in ((1, stage_ref), (2, far_ref.at[0]), (3, far_ref.at[1])):
        lanes = part_lanes(jnp.bitwise_xor(me_ref[0] % N_SP, step))
        piece = pltpu.make_async_copy(cot_ref.at[:, lanes], ref, piece_sem.at[step - 1])
        piece.start()
        pieces.append(piece)
    index.wait()
    pick = row_picker(index_ref[...], me_ref[0])
    stores = []
    for array in range(3):
        loads[array].wait()
        if array == 2:
            pieces[0].wait()
            near = pltpu.make_async_copy(stage_ref, near_ref, near_sem)
            near.start()
            stores.append(near)
        lanes = pl.ds(array * PART, PART)
        for part in range(N_SP):
            rows = dot(pick, in_ref[array, :, pl.ds(part * PART, PART)]).astype(BF)
            send_ref[:, part, :, lanes] = rows.reshape(N_DP, 4, PART)
            if part % 2 == 1:
                parts = pl.ds(part - 1, 2)
                store = pltpu.make_async_copy(
                    send_ref.at[:, parts, :, lanes], out_ref.at[:, parts, :, lanes], out_sem.at[array, part // 2]
                )
                store.start()
                stores.append(store)
    for piece in pieces[1:]:
        piece.wait()
    for store in stores:
        store.wait()


def unpack_kernel(pick_ref, recv_ref, q_ref, k_ref, v_ref, out_ref, out_sem):
    pick = pick_ref[...]
    stores = []
    for array, ref in enumerate((q_ref, k_ref, v_ref)):
        for part in range(N_SP):
            rows = recv_ref[:, part, :, pl.ds(array * PART, PART)].reshape(ROWS, PART)
            out_ref[array, :, pl.ds(part * PART, PART)] = dot(pick, rows).astype(BF)
            if part % 2 == 1:
                lanes = pl.ds((part - 1) * PART, 2 * PART)
                store = pltpu.make_async_copy(
                    out_ref.at[array, :, lanes], ref.at[:, lanes], out_sem.at[array, part // 2]
                )
                store.start()
                stores.append(store)
    for store in stores:
        store.wait()


def prepare_kernel(
    me_ref,
    lengths_ref,
    plan_ref,
    bins_ref,
    guide_ref,
    table_ref,
    cot_ref,
    near_ref,
    far_ref,
    relay_ref,
    grad_ref,
    turned_ref,
    bias_ref,
    live_ref,
    pick_ref,
    own_ref,
    gated_ref,
    rows_ref,
    own_sem,
):
    me = me_ref[0]
    group, mine = me // N_SP, me % N_SP
    own_load = pltpu.make_async_copy(cot_ref.at[:, part_lanes(mine)], own_ref, own_sem)
    own_load.start()
    group_len = sample_of(group, plan_ref, lengths_ref)
    group_bin = sample_of(group, plan_ref, bins_ref)
    own_load.wait()
    for step, ref in enumerate((own_ref, near_ref, far_ref.at[0], relay_ref.at[1])):
        for head in range(HEADS_DEV):
            lanes = pl.ds(head * HD, HD)
            gate = guide_ref[group_bin, mine * HEADS_DEV + head]
            gated_ref[jnp.bitwise_xor(mine, step), :, lanes] = (gate * ref[:, lanes].astype(F32)).astype(BF)
    for quarter in range(4):
        own = table_ref[pl.ds(group * N_SP + quarter, 1), :] // ROWS
        rows_ref[quarter] = dot(onehot(own == iota((LOADERS, ROWS), 0)), gated_ref[quarter]).astype(BF)
    order = quarters_first()
    for half in range(2):
        rows = rows_ref[:, pl.ds(half * 64, 64), :].reshape(256, PART)
        grad = dot_tn(order, rows)
        grad_ref[pl.ds(half * 256, 256), :] = grad.astype(BF)
        for head in range(HEADS_DEV):
            lanes = slice(head * HD, (head + 1) * HD)
            turned_ref[lanes, pl.ds(half * 256, 256)] = grad[:, lanes].T.astype(BF)
    pick_ref[...] = row_picker(table_ref[...], me).astype(F32).T.astype(BF)
    row = iota((GROUP, ROWS), 0)
    source = jnp.zeros((GROUP, ROWS), jnp.int32)
    for quarter in range(4):
        own = table_ref[pl.ds(group * N_SP + quarter, 1), :] // ROWS
        source = jnp.where(row % 4 == quarter, own, source)
    place = onehot(source == row // 4)
    count = iota((ROWS, HD), 0).astype(F32).astype(BF)
    place_col = dot(place, count) + (ROWS * (row % 4)).astype(F32)
    bias_ref[...] = jnp.where(place_col < group_len.astype(F32), 0.0, -1e30)
    lane = iota((8, GROUP), 1)
    place_row = dot_nt(iota((8, ROWS), 1).astype(F32).astype(BF), place) + (ROWS * (lane % 4)).astype(F32)
    live_ref[...] = jnp.where(place_row < group_len.astype(F32), 1.0, 0.0)


def collect_kernel(me_ref, plan_ref, bins_ref, guide_ref, table_ref, i0_ref, i1_ref, far_ref, relay_ref, out_ref):
    me = me_ref[0]
    group, mine = me // N_SP, me % N_SP
    group_bin = sample_of(group, plan_ref, bins_ref)
    order = onehot(table_ref[pl.ds(me, 1), :] // ROWS == iota((LOADERS, ROWS), 0)).astype(F32).T.astype(BF)
    for step, ref in enumerate((i0_ref, i1_ref, far_ref.at[0], relay_ref.at[1])):
        out_ref[:, part_lanes(jnp.bitwise_xor(mine, step))] = dot(order, ref[...]).astype(BF)
    for head in range(HEADS):
        lanes = pl.ds(head * HD, HD)
        out_ref[:, lanes] = (guide_ref[group_bin, head] * out_ref[:, lanes].astype(F32)).astype(BF)


def forward_kernel(
    me_ref,
    bias_ref,
    live_ref,
    turned_ref,
    recv_ref,
    raised_ref,
    stats_ref,
    own_ref,
    near_ref,
    far_ref,
    out_ref,
    piece_ref,
    piece_sem,
):
    mine = me_ref[0] % N_SP
    live = live_ref[0:1, :]
    bias = bias_ref[:, 0:1]

    def item(head, array):
        return recv_ref[:, :, columns(head, array)].reshape(GROUP, HD)

    def score(head):
        return dot_nt(item(head, 1), item(head, 0)) + bias

    def attend(head, weights, inverse):
        output = dot_tn(item(head, 2), weights) * inverse
        turned = turned_ref[pl.ds(head * HD, HD), :].astype(F32)
        stats_ref[8 + head : 9 + head, :] = jnp.sum(output * turned, axis=0, keepdims=True)
        out_ref[:, pl.ds(head * HD, HD)] = output.T.astype(BF)

    following = score(0)
    earlier = None
    for head in range(HEADS_DEV):
        scores = following
        if head + 1 < HEADS_DEV:
            following = score(head + 1)
        top = jnp.max(scores, axis=0, keepdims=True)
        raised = jnp.exp2((scores - top) * (SCALE * LOG2E))
        inverse = live / jnp.sum(raised, axis=0, keepdims=True)
        weights = raised.astype(BF)
        raised_ref[head] = weights
        stats_ref[head : head + 1, :] = inverse
        if earlier is not None:
            attend(*earlier)
        earlier = (head, weights, inverse)
    attend(*earlier)
    stats_ref[HEADS_DEV:8, :] = jnp.zeros((8 - HEADS_DEV, GROUP), F32)
    stores = []
    for step, ref in ((2, far_ref.at[0]), (3, far_ref.at[1]), (1, near_ref), (0, own_ref)):
        quarter = onehot(iota((ROWS, GROUP), 1) == 4 * iota((ROWS, GROUP), 0) + jnp.bitwise_xor(mine, step))
        piece_ref[step] = dot(quarter, out_ref[...]).astype(BF)
        store = pltpu.make_async_copy(piece_ref.at[step], ref, piece_sem.at[step])
        store.start()
        stores.append(store)
    for store in stores:
        store.wait()


def backward_kernel(recv_ref, raised_ref, stats_ref, grad_ref, out_ref, ret_ref, out_sem):
    inverse_columns = stats_ref[0:8, :].T
    halves = [(head, half) for head in range(HEADS_DEV) for half in range(2)]
    stores = []

    def item(head, array, half=None):
        loaders = pl.ds(0, LOADERS) if half is None else pl.ds(half * 64, 64)
        return recv_ref[loaders, :, columns(head, array)].reshape(-1, HD)

    def attended(head, half):
        return dot_nt(item(head, 2), grad_ref[pl.ds(half * 256, 256), pl.ds(head * HD, HD)])

    ahead = [attended(*halves[0]), attended(*halves[1])]
    for index, (head, half) in enumerate(halves):
        grad_attend = ahead.pop(0)
        if index + 2 < len(halves):
            ahead.append(attended(*halves[index + 2]))
        rows = slice(half * 256, (half + 1) * 256)
        weights = raised_ref[head, :, rows]
        inverse = stats_ref[head : head + 1, rows]
        row_dot = stats_ref[8 + head : 9 + head, rows]
        grad_scores = (weights.astype(F32) * (grad_attend - row_dot)).astype(BF)
        column = inverse_columns[rows, head : head + 1]
        query = (item(head, 0, half).astype(F32) * (column * SCALE)).astype(BF)
        grad = (grad_ref[rows, pl.ds(head * HD, HD)].astype(F32) * column).astype(BF)
        grad_query = (dot_tn(item(head, 1), grad_scores) * (inverse * SCALE)).T.astype(BF)
        ret_ref[pl.ds(half * 64, 64), :, columns(head, 0)] = grad_query.reshape(64, 4, HD)
        if half == 0:
            grad_key, grad_value = dot(grad_scores, query), dot(weights, grad)
            continue
        grad_key += dot(grad_scores, query)
        grad_value += dot(weights, grad)
        ret_ref[:, :, columns(head, 1)] = grad_key.astype(BF).reshape(LOADERS, 4, HD)
        ret_ref[:, :, columns(head, 2)] = grad_value.astype(BF).reshape(LOADERS, 4, HD)
        for array in range(3):
            lanes = columns(head, array)
            store = pltpu.make_async_copy(
                ret_ref.at[:, :, lanes], out_ref.at[:, :, lanes], out_sem.at[head, array]
            )
            store.start()
            stores.append(store)
    for store in stores:
        store.wait()


SMEM = pl.BlockSpec(memory_space=pltpu.SMEM)
VMEM = pl.BlockSpec(memory_space=pltpu.VMEM)
HBM = pl.BlockSpec(memory_space=pltpu.HBM)
PARAMS = pltpu.CompilerParams(vmem_limit_bytes=24 * 1024 * 1024)
AHEAD = pl.CostEstimate(flops=15_000_000_000, bytes_accessed=50_000_000, transcendentals=0)
PIECES = jax.ShapeDtypeStruct((2, ROWS, PART), BF)
WHOLE = jax.ShapeDtypeStruct((ROWS, WIDTH), BF)


def in_hbm(array):
    return pltpu.with_memory_space_constraint(array, pltpu.HBM)


def pack(me, table, queries, keys, values, cotangent):
    chunks, *pieces = pl.pallas_call(
        pack_kernel,
        out_shape=(pltpu.HBM((N_DP, N_SP, 4, CHUNK), BF), pltpu.HBM((ROWS, PART), BF), PIECES),
        in_specs=[SMEM] + [HBM] * 5,
        out_specs=(HBM, HBM, VMEM),
        scratch_shapes=[
            pltpu.VMEM((LOADERS, ROWS), jnp.int32),
            pltpu.VMEM((3, ROWS, WIDTH), BF),
            pltpu.VMEM((N_DP, N_SP, 4, CHUNK), BF),
            pltpu.VMEM((ROWS, PART), BF),
            pltpu.SemaphoreType.DMA,
            pltpu.SemaphoreType.DMA((3,)),
            pltpu.SemaphoreType.DMA((3, 2)),
            pltpu.SemaphoreType.DMA((N_SP - 1,)),
            pltpu.SemaphoreType.DMA,
        ],
        compiler_params=PARAMS,
        name="pack",
    )(me, in_hbm(table), in_hbm(queries), in_hbm(keys), in_hbm(values), in_hbm(cotangent))
    return chunks.reshape(LOADERS, 4, CHUNK), pieces


def unpack(pick, chunks):
    return pl.pallas_call(
        unpack_kernel,
        out_shape=(pltpu.HBM((ROWS, WIDTH), BF),) * 3,
        in_specs=[VMEM] * 2,
        out_specs=(HBM,) * 3,
        scratch_shapes=[
            pltpu.VMEM((3, ROWS, WIDTH), BF),
            pltpu.SemaphoreType.DMA((3, 2)),
        ],
        compiler_params=PARAMS,
        name="unpack",
    )(pick, chunks.reshape(N_DP, N_SP, 4, CHUNK))


def prepare(me, lengths, plan, bins, guide, table, cotangent, pieces):
    return pl.pallas_call(
        prepare_kernel,
        out_shape=(
            jax.ShapeDtypeStruct((GROUP, PART), BF),
            jax.ShapeDtypeStruct((PART, GROUP), BF),
            jax.ShapeDtypeStruct((GROUP, HD), F32),
            jax.ShapeDtypeStruct((8, GROUP), F32),
            jax.ShapeDtypeStruct((ROWS, LOADERS), BF),
        ),
        in_specs=[SMEM] * 5 + [VMEM, HBM] + [VMEM] * 3,
        out_specs=(VMEM,) * 5,
        scratch_shapes=[
            pltpu.VMEM((ROWS, PART), BF),
            pltpu.VMEM((4, ROWS, PART), BF),
            pltpu.VMEM((4, ROWS, PART), BF),
            pltpu.SemaphoreType.DMA,
        ],
        compiler_params=PARAMS,
        cost_estimate=AHEAD,
        name="prepare",
    )(me, lengths, plan, bins, guide, table, in_hbm(cotangent), *pieces)


def collect(me, plan, bins, guide, table, pieces):
    return pl.pallas_call(
        collect_kernel,
        out_shape=WHOLE,
        in_specs=[SMEM] * 4 + [VMEM] * (1 + N_SP),
        out_specs=VMEM,
        compiler_params=PARAMS,
        cost_estimate=AHEAD,
        name="collect",
    )(me, plan, bins, guide, table, *pieces)


def forward(me, bias, live, turned, chunks):
    return pl.pallas_call(
        forward_kernel,
        out_shape=(
            jax.ShapeDtypeStruct((HEADS_DEV, GROUP, GROUP), BF),
            jax.ShapeDtypeStruct((16, GROUP), F32),
            pltpu.HBM((ROWS, PART), BF),
            pltpu.HBM((ROWS, PART), BF),
            pltpu.HBM((2, ROWS, PART), BF),
        ),
        in_specs=[SMEM] + [VMEM] * 4,
        out_specs=(VMEM, VMEM, HBM, HBM, HBM),
        scratch_shapes=[
            pltpu.VMEM((GROUP, PART), BF),
            pltpu.VMEM((N_SP, ROWS, PART), BF),
            pltpu.SemaphoreType.DMA((N_SP,)),
        ],
        compiler_params=PARAMS,
        name="forward",
    )(me, bias, live, turned, chunks)


def backward(chunks, raised, stats, grad):
    return pl.pallas_call(
        backward_kernel,
        out_shape=pltpu.HBM((LOADERS, 4, CHUNK), BF),
        in_specs=[VMEM] * 4,
        out_specs=HBM,
        scratch_shapes=[
            pltpu.VMEM((LOADERS, 4, CHUNK), BF),
            pltpu.SemaphoreType.DMA((HEADS_DEV, 3)),
        ],
        compiler_params=PARAMS,
        name="backward",
    )(chunks, raised, stats, grad)


def exchange(chunks):
    return lax.all_to_all(chunks, ("dp", "sp"), split_axis=0, concat_axis=0, tiled=True)


def swap(piece, step):
    return lax.ppermute(piece, "sp", [(i, i ^ step) for i in range(N_SP)])


def swap_pieces(near, far):
    far = swap(far, 2)
    return swap(near, 1), far, swap(far, 1)


def per_device(
    queries,
    key_rows,
    value_rows,
    cotangent,
    lengths,
    sample_plan,
    guide_bins,
    guide_table,
    block_source,
):
    me = (lax.axis_index("dp") * N_SP + lax.axis_index("sp")).astype(jnp.int32).reshape(1)
    table = block_source.reshape(LOADERS, ROWS)
    packed, pieces = pack(me, table, queries, key_rows, value_rows, cotangent)
    chunks = exchange(packed)
    grad, turned, bias, live, pick = prepare(
        me, lengths, sample_plan, guide_bins, guide_table, table, cotangent, swap_pieces(*pieces)
    )
    raised, stats, own, *outs = forward(me, bias, live, turned, chunks)
    out_pieces = own, *swap_pieces(*outs)
    grads = backward(chunks, raised, stats, grad)
    back = exchange(grads)
    attn_out = collect(me, sample_plan, guide_bins, guide_table, table, out_pieces)
    return attn_out, *unpack(pick, back)


def solution(mesh):
    rows = P(("dp", "sp"), None)
    return jax.shard_map(
        per_device,
        mesh=mesh,
        in_specs=(rows,) * 4 + (P(),) * 5,
        out_specs=(rows,) * 4,
        check_vma=False,
    )
```

time: 93.8 us -> 91.3 us (0.973)
  waiting for transfers between devices: 52.9 us -> 45.5 us
  local copies, waits for them, and re-layouts: 1.59 us -> 5.83 us
    all_to_all x2, waiting for transfers between devices: 52.9 us -> 42.8 us  [exchange(): lax.all_to_all(chunks, ('dp', 'sp'), split_axis=0, concat_axis=0, tiled=T...]
    unnamed x14 -> x32, local copies, waits for them, and re-layouts: 1.59 us -> 5.83 us
    ppermute x6, waiting for transfers between devices: 0.02 us -> 2.78 us  [swap(): return lax.ppermute(piece, 'sp', [(i, i ^ step) for i in range(N_SP)])]
    all_to_all x2, starting transfers between devices: 13.9 us -> 16 us  [exchange(): lax.all_to_all(chunks, ('dp', 'sp'), split_axis=0, concat_axis=0, tiled=T...]
    ppermute x6, starting transfers between devices: 5.74 us -> 4.62 us  [swap(): return lax.ppermute(piece, 'sp', [(i, i ^ step) for i in range(N_SP)])]
    pallas_call x1, Pallas kernels: 5.42 us -> 4.36 us  [backward(): pl.pallas_call(backward_kernel, out_shape=pltpu.HBM((LOADERS, 4, CHUNK),...]
    pallas_call x1, Pallas kernels: 1.53 us -> 2.55 us  [prepare(): pl.pallas_call(prepare_kernel, out_shape=(jax.ShapeDtypeStruct((GROUP, PA...]
  transfers between devices with their start and end apart: 8 -> 8, of which waited for: 2 -> 4; matrix products, arithmetic and copies ran while one was open for 0% -> 0% of each run, Pallas kernels for 10% -> 10%
where the time goes in v5:
time: 91.3 us; the launch traced here: 90.9 us
  waiting for transfers between devices  45.5 us (50%)
  starting transfers between devices  20.6 us (23%)
  Pallas kernels  18.1 us (20%)
  local copies, waits for them, and re-layouts  5.83 us (6%)
    all_to_all x2, waiting for transfers between devices, exchange(): lax.all_to_all(chunks, ('dp', 'sp'), split_axis=0, concat_axis=0, tiled=T...  42.8 us
    all_to_all x2, starting transfers between devices, exchange(): lax.all_to_all(chunks, ('dp', 'sp'), split_axis=0, concat_axis=0, tiled=T...  16 us
    unnamed x32, local copies, waits for them, and re-layouts  5.83 us
    ppermute x6, starting transfers between devices, swap(): return lax.ppermute(piece, 'sp', [(i, i ^ step) for i in range(N_SP)])  4.62 us
    pallas_call x1, Pallas kernels, backward(): pl.pallas_call(backward_kernel, out_shape=pltpu.HBM((LOADERS, 4, CHUNK),...  4.36 us
    pallas_call x1, Pallas kernels, forward(): pl.pallas_call(forward_kernel, out_shape=(jax.ShapeDtypeStruct((HEADS_DEV...  3.89 us
    pallas_call x1, Pallas kernels, pack(): pl.pallas_call(pack_kernel, out_shape=(pltpu.HBM((N_DP, N_SP, 4, CHUNK),...  3.8 us
    ppermute x6, waiting for transfers between devices, swap(): return lax.ppermute(piece, 'sp', [(i, i ^ step) for i in range(N_SP)])  2.78 us
  transfers between devices with their start and end apart: 8, of which 4 were waited for; matrix products, arithmetic and copies ran while one was open for 0% of the time, Pallas kernels for 10%

profile of v5, /device:TPU:1, one launch (start us, length us, event | category | flops | bytes accessed | tf_op | source)
XLA Modules:
  0.0 90.9 jit_solution(6710343186131661341)
XLA Ops:
  0.6 3.8 %pack.1 = (bf16[32,4,4,1920]{3,2,1,0:T(4,128)(2,1)}, bf16[128,640]{1,0:T(8,128)(2,1)}, bf16[2,128,640]{2,1,0:T(8,128)(2,1)S(1)}) custom-call(s32[1]{0:T(128)} %bitcast.me_ref, s32[128,128]{1,0:T(8,128)} %bitcast.5, bf16[128,2560]{1,0:T(8,128)(2,1)} %q_ref.1, bf16[128,2560]{1,0:T(8,128)(2,1)} %k_ref.1, bf16[128,2560]{1,0:T(8,128)(2,1)} %v_ref.1, ...), custom_call_target="tpu_custom_call" | custom-call | tf_op jit(solution)/shard_map/pack/pallas_call | solution.py:337
  4.4 2.1 %collective-permute-start.1 = (bf16[2,128,640]{2,1,0:T(8,128)(2,1)S(1)}, bf16[2,128,640]{2,1,0:T(8,128)(2,1)S(1)}, u32[]{:S(2)}, u32[]{:S(2)}) collective-permute-start(bf16[2,128,640]{2,1,0:T(8,128)(2,1)S(1)} %get-tuple-element.21), channel_id=1, source_target_pairs={{0,2},{1,3},{2,0},{3,1},{4,6},{5,7},{6,4},{7,5},{8,10},{9,11},{10,... | collective-permute-start | bytes 983048 | tf_op jit(solution)/shard_map/ppermute | solution.py:452
  6.6 10.7 %all-to-all-start = ((bf16[128,4,1920]{2,1,0:T(4,128)(2,1)}), bf16[128,4,1920]{2,1,0:T(4,128)(2,1)S(1)}, u32[]{:S(2)}, u32[]{:S(2)}) async-start(bf16[128,4,1920]{2,1,0:T(4,128)(2,1)} %bitcast.8), calls=%async_computation | async-start | bytes 3932160 | tf_op jit(solution)/shard_map/all_to_all | solution.py:448
  17.2 1.1 %collective-permute-start.2 = (bf16[2,128,640]{2,1,0:T(8,128)(2,1)S(1)}, bf16[2,128,640]{2,1,0:T(8,128)(2,1)S(1)}, u32[]{:S(2)}, u32[]{:S(2)}) collective-permute-start(bf16[2,128,640]{2,1,0:T(8,128)(2,1)S(1)} %collective-permute-done.1.far_ref), channel_id=1, source_target_pairs={{0,1},{1,0},{2,3},{3,2},{4,5},{5,4},{6,7},{7,6},{8,9},{9,8},{10,11... | collective-permute-start | bytes 983048 | tf_op jit(solution)/shard_map/ppermute | solution.py:452
  18.4 0.7 copy-done.4
  19.1 1.4 %collective-permute-done.near_ref = bf16[128,640]{1,0:T(8,128)(2,1)S(1)} collective-permute-done((bf16[128,640]{1,0:T(8,128)(2,1)S(1)}, bf16[128,640]{1,0:T(8,128)(2,1)S(1)}, u32[]{:S(2)}, u32[]{:S(2)}) %collective-permute-start) | collective-permute-done | bytes 163872 | tf_op jit(solution)/shard_map/ppermute | solution.py:452
  20.5 0.8 copy-done
  21.4 1.0 %copy-done.5 = bf16[2,128,640]{2,1,0:T(8,128)(2,1)S(1)} copy-done((bf16[2,128,640]{2,1,0:T(8,128)(2,1)S(1)}, bf16[2,128,640]{2,1,0:T(8,128)(2,1)}, u32[]{:S(2)}) %copy-start.5) | copy-done | bytes 327704
  22.3 0.7 copy-done.7
  23.0 0.7 copy-done.9
  23.7 0.7 copy-done.10
  24.3 0.7 copy-done.12
  25.0 2.5 %prepare.1 = (bf16[512,640]{1,0:T(8,128)(2,1)S(1)}, bf16[640,512]{1,0:T(8,128)(2,1)S(1)}, f32[512,128]{1,0:T(8,128)S(1)}, f32[8,512]{1,0:T(8,128)S(1)}, bf16[128,128]{1,0:T(8,128)(2,1)S(1)}) custom-call(s32[1]{0:T(128)} %bitcast.me_ref, s32[32]{0:T(128)S(1)} %copy-done.9, s32[32]{0:T(128)S(1)} %copy-done.10, s32[32]{0:T(128)S(1)} %copy-done.12, ...), custom_call_target="tpu_custom_call" | custom-call | flops 15000000512 | bytes 50000000 | tf_op jit(solution)/shard_map/prepare/pallas_call | solution.py:375
  27.6 0.6 copy-done.2
  28.1 18.2 %all-to-all-done.recv_ref = bf16[128,4,1920]{2,1,0:T(4,128)(2,1)S(1)} async-done(((bf16[128,4,1920]{2,1,0:T(4,128)(2,1)}), bf16[128,4,1920]{2,1,0:T(4,128)(2,1)S(1)}, u32[]{:S(2)}, u32[]{:S(2)}) %all-to-all-start) | async-done | bytes 1966112 | tf_op jit(solution)/shard_map/all_to_all | solution.py:448
  46.4 3.9 %forward.1 = (bf16[5,512,512]{2,1,0:T(8,128)(2,1)S(1)}, f32[16,512]{1,0:T(8,128)S(1)}, bf16[128,640]{1,0:T(8,128)(2,1)}, bf16[128,640]{1,0:T(8,128)(2,1)}, bf16[2,128,640]{2,1,0:T(8,128)(2,1)}) custom-call(s32[1]{0:T(128)} %bitcast.me_ref, f32[512,128]{1,0:T(8,128)S(1)} %get-tuple-element.22.bias_ref, f32[8,512]{1,0:T(8,128)S(1)} %get-tuple-element.23.live_ref, ...), custom_call_target="tpu_custom_call" | custom-call | tf_op jit(solution)/shard_map/forward/pallas_call | solution.py:411
  50.4 4.4 %backward.1 = bf16[128,4,1920]{2,1,0:T(4,128)(2,1)} custom-call(bf16[128,4,1920]{2,1,0:T(4,128)(2,1)S(1)} %all-to-all-done.recv_ref, bf16[5,512,512]{2,1,0:T(8,128)(2,1)S(1)} %get-tuple-element.30.raised_ref, f32[16,512]{1,0:T(8,128)S(1)} %get-tuple-element.31.stats_ref, bf16[512,640]{1,0:T(8,128)(2,1)S(1)} %get-tuple-element.32.grad_ref), custom_call_target="tpu_custom_call" | custom-call | tf_op jit(solution)/shard_map/backward/pallas_call | solution.py:433
  54.8 5.3 %all-to-all-start.1 = ((bf16[128,4,1920]{2,1,0:T(4,128)(2,1)}), bf16[128,4,1920]{2,1,0:T(4,128)(2,1)S(1)}, u32[]{:S(2)}, u32[]{:S(2)}) async-start(bf16[128,4,1920]{2,1,0:T(4,128)(2,1)} %backward.1), calls=%async_computation.1 | async-start | bytes 3932160 | tf_op jit(solution)/shard_map/all_to_all | solution.py:448
  60.2 1.1 %collective-permute-start.5 = (bf16[2,128,640]{2,1,0:T(8,128)(2,1)S(1)}, bf16[2,128,640]{2,1,0:T(8,128)(2,1)S(1)}, u32[]{:S(2)}, u32[]{:S(2)}) collective-permute-start(bf16[2,128,640]{2,1,0:T(8,128)(2,1)S(1)} %collective-permute-done.4.far_ref), channel_id=1, source_target_pairs={{0,1},{1,0},{2,3},{3,2},{4,5},{5,4},{6,7},{7,6},{8,9},{9,8},{10,11... | collective-permute-start | bytes 983048 | tf_op jit(solution)/shard_map/ppermute | solution.py:452
  61.3 0.1 collective-permute-start.3
  61.4 1.4 %collective-permute-done.3.i1_ref = bf16[128,640]{1,0:T(8,128)(2,1)S(1)} collective-permute-done((bf16[128,640]{1,0:T(8,128)(2,1)S(1)}, bf16[128,640]{1,0:T(8,128)(2,1)S(1)}, u32[]{:S(2)}, u32[]{:S(2)}) %collective-permute-start.3) | collective-permute-done | bytes 163872 | tf_op jit(solution)/shard_map/ppermute | solution.py:452
  62.9 2.0 %collect.1 = bf16[128,2560]{1,0:T(8,128)(2,1)} custom-call(s32[1]{0:T(128)} %bitcast.me_ref, s32[32]{0:T(128)S(1)} %copy-done.11, s32[32]{0:T(128)S(1)} %copy-done.13, f32[8,20]{1,0:T(8,128)S(1)} %copy-done.8, s32[128,128]{1,0:T(8,128)S(1)} %bitcast.7, bf16[128,640]{1,0:T(8,128)(2,1)S(1)} %copy-done.6, bf16[128,640]{1,0:T(8,128)(2,1)S(1)} %collective-permute-done.3.i1_ref, ...), custom_call_target="tpu_custom_call" | custom-call | flops 15000000512 | bytes 50000000 | tf_op jit(solution)/shard_map/collect/pallas_call | solution.py:399
  64.8 24.5 %all-to-all-done.1 = bf16[128,4,1920]{2,1,0:T(4,128)(2,1)S(1)} async-done(((bf16[128,4,1920]{2,1,0:T(4,128)(2,1)}), bf16[128,4,1920]{2,1,0:T(4,128)(2,1)S(1)}, u32[]{:S(2)}, u32[]{:S(2)}) %all-to-all-start.1) | async-done | bytes 1966112 | tf_op jit(solution)/shard_map/all_to_all | solution.py:448
  89.3 1.6 %unpack.1 = (bf16[128,2560]{1,0:T(8,128)(2,1)}, bf16[128,2560]{1,0:T(8,128)(2,1)}, bf16[128,2560]{1,0:T(8,128)(2,1)}) custom-call(bf16[128,128]{1,0:T(8,128)(2,1)S(1)} %copy-done.3, bf16[32,4,4,1920]{3,2,1,0:T(4,128)(2,1)S(1)} %bitcast.4), custom_call_target="tpu_custom_call" | custom-call | tf_op jit(solution)/shard_map/unpack/pallas_call | solution.py:360
  (30 shorter events, 0.2 us)
Async XLA Ops:
  4.4 12.8 %collective-permute-start.1 = (bf16[2,128,640]{2,1,0:T(8,128)(2,1)S(1)}, bf16[2,128,640]{2,1,0:T(8,128)(2,1)S(1)}, u32[]{:S(2)}, u32[]{:S(2)}) collective-permute-start(bf16[2,128,640]{2,1,0:T(8,128)(2,1)S(1)} %get-tuple-element.21), channel_id=1, source_target_pairs={{0,2},{1,3},{2,0},{3,1},{4,6},{5,7},{6,4},{7,5},{8,10},{9,11},{10,... | collective-permute-start | bytes 983048 | tf_op jit(solution)/shard_map/ppermute | solution.py:452
  6.6 12.5 %copy-start.15 = (bf16[128,640]{1,0:T(8,128)(2,1)S(1)}, bf16[128,640]{1,0:T(8,128)(2,1)}, u32[]{:S(2)}) copy-start(bf16[128,640]{1,0:T(8,128)(2,1)} %get-tuple-element.20) | copy-start | bytes 491524
  6.6 39.8 %all-to-all-start = ((bf16[128,4,1920]{2,1,0:T(4,128)(2,1)}), bf16[128,4,1920]{2,1,0:T(4,128)(2,1)S(1)}, u32[]{:S(2)}, u32[]{:S(2)}) async-start(bf16[128,4,1920]{2,1,0:T(4,128)(2,1)} %bitcast.8), calls=%async_computation | async-start | bytes 3932160 | tf_op jit(solution)/shard_map/all_to_all | solution.py:448
  17.2 3.3 %collective-permute-start.2 = (bf16[2,128,640]{2,1,0:T(8,128)(2,1)S(1)}, bf16[2,128,640]{2,1,0:T(8,128)(2,1)S(1)}, u32[]{:S(2)}, u32[]{:S(2)}) collective-permute-start(bf16[2,128,640]{2,1,0:T(8,128)(2,1)S(1)} %collective-permute-done.1.far_ref), channel_id=1, source_target_pairs={{0,1},{1,0},{2,3},{3,2},{4,5},{5,4},{6,7},{7,6},{8,9},{9,8},{10,11... | collective-permute-start | bytes 983048 | tf_op jit(solution)/shard_map/ppermute | solution.py:452
  18.4 0.7 copy-start.4
  19.1 1.4 %collective-permute-start = (bf16[128,640]{1,0:T(8,128)(2,1)S(1)}, bf16[128,640]{1,0:T(8,128)(2,1)S(1)}, u32[]{:S(2)}, u32[]{:S(2)}) collective-permute-start(bf16[128,640]{1,0:T(8,128)(2,1)S(1)} %copy-done.15), channel_id=1, source_target_pairs={{0,1},{1,0},{2,3},{3,2},{4,5},{5,4},{6,7},{7,6},{8,9},{9,8},{10,11... | collective-permute-start | bytes 491528 | tf_op jit(solution)/shard_map/ppermute | solution.py:452
  20.5 0.8 copy-start
  21.4 1.0 %copy-start.5 = (bf16[2,128,640]{2,1,0:T(8,128)(2,1)S(1)}, bf16[2,128,640]{2,1,0:T(8,128)(2,1)}, u32[]{:S(2)}) copy-start(bf16[2,128,640]{2,1,0:T(8,128)(2,1)} %copy-done.4) | copy-start | bytes 983044
  22.3 0.7 copy-start.7
  23.0 0.7 copy-start.9
  23.7 0.7 copy-start.10
  24.3 0.7 copy-start.12
  27.5 0.6 copy-start.2
  50.3 9.9 %collective-permute-start.4 = (bf16[2,128,640]{2,1,0:T(8,128)(2,1)}, bf16[2,128,640]{2,1,0:T(8,128)(2,1)S(1)}, u32[]{:S(2)}, u32[]{:S(2)}) collective-permute-start(bf16[2,128,640]{2,1,0:T(8,128)(2,1)} %get-tuple-element.28), channel_id=1, source_target_pairs={{0,2},{1,3},{2,0},{3,1},{4,6},{5,7},{6,4},{7,5},{8,10},{9,11},{10,... | collective-permute-start | bytes 983048 | tf_op jit(solution)/shard_map/ppermute | solution.py:452
  54.8 6.6 %copy-start.14 = (bf16[128,640]{1,0:T(8,128)(2,1)S(1)}, bf16[128,640]{1,0:T(8,128)(2,1)}, u32[]{:S(2)}) copy-start(bf16[128,640]{1,0:T(8,128)(2,1)} %get-tuple-element.27) | copy-start | bytes 491524
  54.8 8.1 %copy-start.1 = (s32[16384]{0:T(1024)S(1)}, s32[16384]{0:T(1024)}, u32[]{:S(2)}) copy-start(s32[16384]{0:T(1024)} %param.17) | copy-start | bytes 196612
  54.8 8.1 %copy-start.6 = (bf16[128,640]{1,0:T(8,128)(2,1)S(1)}, bf16[128,640]{1,0:T(8,128)(2,1)}, u32[]{:S(2)}) copy-start(bf16[128,640]{1,0:T(8,128)(2,1)} %get-tuple-element.26.i0_ref) | copy-start | bytes 491524
  54.8 8.0 %copy-start.8 = (f32[8,20]{1,0:T(8,128)S(1)}, f32[8,20]{1,0:T(8,128)}, u32[]{:S(2)}) copy-start(f32[8,20]{1,0:T(8,128)} %guide_ref.3) | copy-start | bytes 1924
  54.8 8.0 %copy-start.11 = (s32[32]{0:T(128)S(1)}, s32[32]{0:T(128)}, u32[]{:S(2)}) copy-start(s32[32]{0:T(128)} %plan_ref.3) | copy-start | bytes 388
  54.8 8.0 %copy-start.13 = (s32[32]{0:T(128)S(1)}, s32[32]{0:T(128)}, u32[]{:S(2)}) copy-start(s32[32]{0:T(128)} %bins_ref.3) | copy-start | bytes 388
  54.8 34.5 %all-to-all-start.1 = ((bf16[128,4,1920]{2,1,0:T(4,128)(2,1)}), bf16[128,4,1920]{2,1,0:T(4,128)(2,1)S(1)}, u32[]{:S(2)}, u32[]{:S(2)}) async-start(bf16[128,4,1920]{2,1,0:T(4,128)(2,1)} %backward.1), calls=%async_computation.1 | async-start | bytes 3932160 | tf_op jit(solution)/shard_map/all_to_all | solution.py:448
  60.2 2.6 %collective-permute-start.5 = (bf16[2,128,640]{2,1,0:T(8,128)(2,1)S(1)}, bf16[2,128,640]{2,1,0:T(8,128)(2,1)S(1)}, u32[]{:S(2)}, u32[]{:S(2)}) collective-permute-start(bf16[2,128,640]{2,1,0:T(8,128)(2,1)S(1)} %collective-permute-done.4.far_ref), channel_id=1, source_target_pairs={{0,1},{1,0},{2,3},{3,2},{4,5},{5,4},{6,7},{7,6},{8,9},{9,8},{10,11... | collective-permute-start | bytes 983048 | tf_op jit(solution)/shard_map/ppermute | solution.py:452
  61.3 1.5 %collective-permute-start.3 = (bf16[128,640]{1,0:T(8,128)(2,1)S(1)}, bf16[128,640]{1,0:T(8,128)(2,1)S(1)}, u32[]{:S(2)}, u32[]{:S(2)}) collective-permute-start(bf16[128,640]{1,0:T(8,128)(2,1)S(1)} %copy-done.14), channel_id=1, source_target_pairs={{0,1},{1,0},{2,3},{3,2},{4,5},{5,4},{6,7},{7,6},{8,9},{9,8},{10,11... | collective-permute-start | bytes 491528 | tf_op jit(solution)/shard_map/ppermute | solution.py:452
  62.9 26.5 %copy-start.3 = (bf16[128,128]{1,0:T(8,128)(2,1)S(1)}, bf16[128,128]{1,0:T(8,128)(2,1)}, u32[]{:S(2)}) copy-start(bf16[128,128]{1,0:T(8,128)(2,1)} %copy-done.2) | copy-start | bytes 98308

commit v6 on v5

--- a/solution.py
+++ b/solution.py
@@ -42,8 +42,12 @@
     return jnp.where(hit, 1.0, 0.0).astype(BF)
 
 
+def owner(source):
+    return lax.shift_right_logical(source, 7)
+
+
 def row_picker(table, me):
-    slot = jnp.sum(jnp.where(table // ROWS == me, table % ROWS, 0), axis=1, keepdims=True)
+    slot = jnp.sum(jnp.where(owner(table) == me, table & (ROWS - 1), 0), axis=1, keepdims=True)
     return onehot(slot == iota((LOADERS, ROWS), 1))
 
 
@@ -114,13 +118,11 @@
         for part in range(N_SP):
             rows = dot(pick, in_ref[array, :, pl.ds(part * PART, PART)]).astype(BF)
             send_ref[:, part, :, lanes] = rows.reshape(N_DP, 4, PART)
-            if part % 2 == 1:
-                parts = pl.ds(part - 1, 2)
-                store = pltpu.make_async_copy(
-                    send_ref.at[:, parts, :, lanes], out_ref.at[:, parts, :, lanes], out_sem.at[array, part // 2]
-                )
-                store.start()
-                stores.append(store)
+        store = pltpu.make_async_copy(
+            send_ref.at[:, :, :, lanes], out_ref.at[:, :, :, lanes], out_sem.at[array]
+        )
+        store.start()
+        stores.append(store)
     for piece in pieces[1:]:
         piece.wait()
     for store in stores:
@@ -179,7 +181,7 @@
             gate = guide_ref[group_bin, mine * HEADS_DEV + head]
             gated_ref[jnp.bitwise_xor(mine, step), :, lanes] = (gate * ref[:, lanes].astype(F32)).astype(BF)
     for quarter in range(4):
-        own = table_ref[pl.ds(group * N_SP + quarter, 1), :] // ROWS
+        own = owner(table_ref[pl.ds(group * N_SP + quarter, 1), :])
         rows_ref[quarter] = dot(onehot(own == iota((LOADERS, ROWS), 0)), gated_ref[quarter]).astype(BF)
     order = quarters_first()
     for half in range(2):
@@ -193,7 +195,7 @@
     row = iota((GROUP, ROWS), 0)
     source = jnp.zeros((GROUP, ROWS), jnp.int32)
     for quarter in range(4):
-        own = table_ref[pl.ds(group * N_SP + quarter, 1), :] // ROWS
+        own = owner(table_ref[pl.ds(group * N_SP + quarter, 1), :])
         source = jnp.where(row % 4 == quarter, own, source)
     place = onehot(source == row // 4)
     count = iota((ROWS, HD), 0).astype(F32).astype(BF)
@@ -208,7 +210,7 @@
     me = me_ref[0]
     group, mine = me // N_SP, me % N_SP
     group_bin = sample_of(group, plan_ref, bins_ref)
-    order = onehot(table_ref[pl.ds(me, 1), :] // ROWS == iota((LOADERS, ROWS), 0)).astype(F32).T.astype(BF)
+    order = onehot(owner(table_ref[pl.ds(me, 1), :]) == iota((LOADERS, ROWS), 0)).astype(F32).T.astype(BF)
     for step, ref in enumerate((i0_ref, i1_ref, far_ref.at[0], relay_ref.at[1])):
         out_ref[:, part_lanes(jnp.bitwise_xor(mine, step))] = dot(order, ref[...]).astype(BF)
     for head in range(HEADS):
@@ -216,20 +218,24 @@
         out_ref[:, lanes] = (guide_ref[group_bin, head] * out_ref[:, lanes].astype(F32)).astype(BF)
 
 
-def forward_kernel(
+def attend_kernel(
     me_ref,
     bias_ref,
     live_ref,
+    grad_ref,
     turned_ref,
     recv_ref,
-    raised_ref,
-    stats_ref,
+    out_ref,
     own_ref,
     near_ref,
     far_ref,
-    out_ref,
+    rows_ref,
     piece_ref,
+    raised_ref,
+    stats_ref,
+    ret_ref,
     piece_sem,
+    out_sem,
 ):
     mine = me_ref[0] % N_SP
     live = live_ref[0:1, :]
@@ -245,7 +251,7 @@
         output = dot_tn(item(head, 2), weights) * inverse
         turned = turned_ref[pl.ds(head * HD, HD), :].astype(F32)
         stats_ref[8 + head : 9 + head, :] = jnp.sum(output * turned, axis=0, keepdims=True)
-        out_ref[:, pl.ds(head * HD, HD)] = output.T.astype(BF)
+        rows_ref[:, pl.ds(head * HD, HD)] = output.T.astype(BF)
 
     following = score(0)
     earlier = None
@@ -267,25 +273,18 @@
     stores = []
     for step, ref in ((2, far_ref.at[0]), (3, far_ref.at[1]), (1, near_ref), (0, own_ref)):
         quarter = onehot(iota((ROWS, GROUP), 1) == 4 * iota((ROWS, GROUP), 0) + jnp.bitwise_xor(mine, step))
-        piece_ref[step] = dot(quarter, out_ref[...]).astype(BF)
+        piece_ref[step] = dot(quarter, rows_ref[...]).astype(BF)
         store = pltpu.make_async_copy(piece_ref.at[step], ref, piece_sem.at[step])
         store.start()
         stores.append(store)
-    for store in stores:
-        store.wait()
-
-
-def backward_kernel(recv_ref, raised_ref, stats_ref, grad_ref, out_ref, ret_ref, out_sem):
     inverse_columns = stats_ref[0:8, :].T
     halves = [(head, half) for head in range(HEADS_DEV) for half in range(2)]
-    stores = []
-
-    def item(head, array, half=None):
+    def part_item(head, array, half=None):
         loaders = pl.ds(0, LOADERS) if half is None else pl.ds(half * 64, 64)
         return recv_ref[loaders, :, columns(head, array)].reshape(-1, HD)
 
     def attended(head, half):
-        return dot_nt(item(head, 2), grad_ref[pl.ds(half * 256, 256), pl.ds(head * HD, HD)])
+        return dot_nt(part_item(head, 2), grad_ref[pl.ds(half * 256, 256), pl.ds(head * HD, HD)])
 
     ahead = [attended(*halves[0]), attended(*halves[1])]
     for index, (head, half) in enumerate(halves):
@@ -298,9 +297,9 @@
         row_dot = stats_ref[8 + head : 9 + head, rows]
         grad_scores = (weights.astype(F32) * (grad_attend - row_dot)).astype(BF)
         column = inverse_columns[rows, head : head + 1]
-        query = (item(head, 0, half).astype(F32) * (column * SCALE)).astype(BF)
+        query = (part_item(head, 0, half).astype(F32) * (column * SCALE)).astype(BF)
         grad = (grad_ref[rows, pl.ds(head * HD, HD)].astype(F32) * column).astype(BF)
-        grad_query = (dot_tn(item(head, 1), grad_scores) * (inverse * SCALE)).T.astype(BF)
+        grad_query = (dot_tn(part_item(head, 1), grad_scores) * (inverse * SCALE)).T.astype(BF)
         ret_ref[pl.ds(half * 64, 64), :, columns(head, 0)] = grad_query.reshape(64, 4, HD)
         if half == 0:
             grad_key, grad_value = dot(grad_scores, query), dot(weights, grad)
@@ -346,7 +345,7 @@
             pltpu.VMEM((ROWS, PART), BF),
             pltpu.SemaphoreType.DMA,
             pltpu.SemaphoreType.DMA((3,)),
-            pltpu.SemaphoreType.DMA((3, 2)),
+            pltpu.SemaphoreType.DMA((3,)),
             pltpu.SemaphoreType.DMA((N_SP - 1,)),
             pltpu.SemaphoreType.DMA,
         ],
@@ -407,41 +406,29 @@
     )(me, plan, bins, guide, table, *pieces)
 
 
-def forward(me, bias, live, turned, chunks):
+def attend(me, bias, live, grad, turned, chunks):
     return pl.pallas_call(
-        forward_kernel,
+        attend_kernel,
         out_shape=(
-            jax.ShapeDtypeStruct((HEADS_DEV, GROUP, GROUP), BF),
-            jax.ShapeDtypeStruct((16, GROUP), F32),
+            pltpu.HBM((LOADERS, 4, CHUNK), BF),
             pltpu.HBM((ROWS, PART), BF),
             pltpu.HBM((ROWS, PART), BF),
             pltpu.HBM((2, ROWS, PART), BF),
         ),
-        in_specs=[SMEM] + [VMEM] * 4,
-        out_specs=(VMEM, VMEM, HBM, HBM, HBM),
+        in_specs=[SMEM] + [VMEM] * 5,
+        out_specs=(HBM,) * 4,
         scratch_shapes=[
             pltpu.VMEM((GROUP, PART), BF),
             pltpu.VMEM((N_SP, ROWS, PART), BF),
+            pltpu.VMEM((HEADS_DEV, GROUP, GROUP), BF),
+            pltpu.VMEM((16, GROUP), F32),
+            pltpu.VMEM((LOADERS, 4, CHUNK), BF),
             pltpu.SemaphoreType.DMA((N_SP,)),
-        ],
-        compiler_params=PARAMS,
-        name="forward",
-    )(me, bias, live, turned, chunks)
-
-
-def backward(chunks, raised, stats, grad):
-    return pl.pallas_call(
-        backward_kernel,
-        out_shape=pltpu.HBM((LOADERS, 4, CHUNK), BF),
-        in_specs=[VMEM] * 4,
-        out_specs=HBM,
-        scratch_shapes=[
-            pltpu.VMEM((LOADERS, 4, CHUNK), BF),
             pltpu.SemaphoreType.DMA((HEADS_DEV, 3)),
         ],
         compiler_params=PARAMS,
-        name="backward",
-    )(chunks, raised, stats, grad)
+        name="attend",
+    )(me, bias, live, grad, turned, chunks)
 
 
 def exchange(chunks):
@@ -475,9 +462,8 @@
     grad, turned, bias, live, pick = prepare(
         me, lengths, sample_plan, guide_bins, guide_table, table, cotangent, swap_pieces(*pieces)
     )
-    raised, stats, own, *outs = forward(me, bias, live, turned, chunks)
+    grads, own, *outs = attend(me, bias, live, grad, turned, chunks)
     out_pieces = own, *swap_pieces(*outs)
-    grads = backward(chunks, raised, stats, grad)
     back = exchange(grads)
     attn_out = collect(me, sample_plan, guide_bins, guide_table, table, out_pieces)
     return attn_out, *unpack(pick, back)

time: 91.3 us -> 89.6 us (0.981)
  starting transfers between devices: 20.6 us -> 22.5 us
  waiting for transfers between devices: 45.5 us -> 43.6 us
  Pallas kernels: 18.1 us -> 16.4 us
    all_to_all x2, waiting for transfers between devices: 42.8 us -> 37.6 us  [exchange(): lax.all_to_all(chunks, ('dp', 'sp'), split_axis=0, concat_axis=0, tiled=T...]
    ppermute x6, waiting for transfers between devices: 2.78 us -> 6.02 us  [swap(): return lax.ppermute(piece, 'sp', [(i, i ^ step) for i in range(N_SP)])]
    ppermute x6, starting transfers between devices: 4.62 us -> 6.56 us  [swap(): return lax.ppermute(piece, 'sp', [(i, i ^ step) for i in range(N_SP)])]
    pallas_call x2 -> x1, Pallas kernels: 8.25 us -> 6.87 us  [attend(): pl.pallas_call(attend_kernel, out_shape=(pltpu.HBM((LOADERS, 4, CHUNK), B...]
  transfers between devices with their start and end apart: 8 -> 8, of which waited for: 4 -> 5; matrix products, arithmetic and copies ran while one was open for 0% -> 0% of each run, Pallas kernels for 10% -> 5%
where the time goes in v6:
time: 89.6 us; the launch traced here: 89.1 us
  waiting for transfers between devices  43.6 us (49%)
  starting transfers between devices  22.5 us (25%)
  Pallas kernels  16.4 us (18%)
  local copies, waits for them, and re-layouts  5.83 us (7%)
    all_to_all x2, waiting for transfers between devices, exchange(): lax.all_to_all(chunks, ('dp', 'sp'), split_axis=0, concat_axis=0, tiled=T...  37.6 us
    all_to_all x2, starting transfers between devices, exchange(): lax.all_to_all(chunks, ('dp', 'sp'), split_axis=0, concat_axis=0, tiled=T...  16 us
    pallas_call x1, Pallas kernels, attend(): pl.pallas_call(attend_kernel, out_shape=(pltpu.HBM((LOADERS, 4, CHUNK), B...  6.87 us
    ppermute x6, starting transfers between devices, swap(): return lax.ppermute(piece, 'sp', [(i, i ^ step) for i in range(N_SP)])  6.56 us
    ppermute x6, waiting for transfers between devices, swap(): return lax.ppermute(piece, 'sp', [(i, i ^ step) for i in range(N_SP)])  6.02 us
    unnamed x32, local copies, waits for them, and re-layouts  5.83 us
    pallas_call x1, Pallas kernels, pack(): pl.pallas_call(pack_kernel, out_shape=(pltpu.HBM((N_DP, N_SP, 4, CHUNK),...  3.47 us
    pallas_call x1, Pallas kernels, prepare(): pl.pallas_call(prepare_kernel, out_shape=(jax.ShapeDtypeStruct((GROUP, PA...  2.53 us
  transfers between devices with their start and end apart: 8, of which 5 were waited for; matrix products, arithmetic and copies ran while one was open for 0% of the time, Pallas kernels for 5%

profile of v6, /device:TPU:1, one launch (start us, length us, event | category | flops | bytes accessed | tf_op | source)
XLA Modules:
  0.0 89.1 jit_solution(1675408872543609492)
XLA Ops:
  0.6 3.5 %pack.1 = (bf16[32,4,4,1920]{3,2,1,0:T(4,128)(2,1)}, bf16[128,640]{1,0:T(8,128)(2,1)}, bf16[2,128,640]{2,1,0:T(8,128)(2,1)S(1)}) custom-call(s32[1]{0:T(128)} %bitcast.me_ref, s32[128,128]{1,0:T(8,128)} %bitcast.5, bf16[128,2560]{1,0:T(8,128)(2,1)} %q_ref.1, bf16[128,2560]{1,0:T(8,128)(2,1)} %k_ref.1, bf16[128,2560]{1,0:T(8,128)(2,1)} %v_ref.1, ...), custom_call_target="tpu_custom_call" | custom-call | tf_op jit(solution)/shard_map/pack/pallas_call | solution.py:336
  4.1 2.1 %collective-permute-start.1 = (bf16[2,128,640]{2,1,0:T(8,128)(2,1)S(1)}, bf16[2,128,640]{2,1,0:T(8,128)(2,1)S(1)}, u32[]{:S(2)}, u32[]{:S(2)}) collective-permute-start(bf16[2,128,640]{2,1,0:T(8,128)(2,1)S(1)} %get-tuple-element.20), channel_id=1, source_target_pairs={{0,2},{1,3},{2,0},{3,1},{4,6},{5,7},{6,4},{7,5},{8,10},{9,11},{10,... | collective-permute-start | bytes 983048 | tf_op jit(solution)/shard_map/ppermute | solution.py:439
  6.2 10.6 %all-to-all-start = ((bf16[128,4,1920]{2,1,0:T(4,128)(2,1)}), bf16[128,4,1920]{2,1,0:T(4,128)(2,1)S(1)}, u32[]{:S(2)}, u32[]{:S(2)}) async-start(bf16[128,4,1920]{2,1,0:T(4,128)(2,1)} %bitcast.8), calls=%async_computation | async-start | bytes 3932160 | tf_op jit(solution)/shard_map/all_to_all | solution.py:435
  16.9 1.1 %collective-permute-start.2 = (bf16[2,128,640]{2,1,0:T(8,128)(2,1)S(1)}, bf16[2,128,640]{2,1,0:T(8,128)(2,1)S(1)}, u32[]{:S(2)}, u32[]{:S(2)}) collective-permute-start(bf16[2,128,640]{2,1,0:T(8,128)(2,1)S(1)} %collective-permute-done.1.far_ref), channel_id=1, source_target_pairs={{0,1},{1,0},{2,3},{3,2},{4,5},{5,4},{6,7},{7,6},{8,9},{9,8},{10,11... | collective-permute-start | bytes 983048 | tf_op jit(solution)/shard_map/ppermute | solution.py:439
  18.1 0.7 copy-done.4
  18.8 1.4 %collective-permute-done.near_ref = bf16[128,640]{1,0:T(8,128)(2,1)S(1)} collective-permute-done((bf16[128,640]{1,0:T(8,128)(2,1)S(1)}, bf16[128,640]{1,0:T(8,128)(2,1)S(1)}, u32[]{:S(2)}, u32[]{:S(2)}) %collective-permute-start) | collective-permute-done | bytes 163872 | tf_op jit(solution)/shard_map/ppermute | solution.py:439
  20.2 0.8 copy-done
  21.0 1.0 %copy-done.5 = bf16[2,128,640]{2,1,0:T(8,128)(2,1)S(1)} copy-done((bf16[2,128,640]{2,1,0:T(8,128)(2,1)S(1)}, bf16[2,128,640]{2,1,0:T(8,128)(2,1)}, u32[]{:S(2)}) %copy-start.5) | copy-done | bytes 327704
  22.0 0.7 copy-done.7
  22.7 0.7 copy-done.9
  23.3 0.7 copy-done.10
  24.0 0.7 copy-done.12
  24.6 2.5 %prepare.1 = (bf16[512,640]{1,0:T(8,128)(2,1)S(1)}, bf16[640,512]{1,0:T(8,128)(2,1)S(1)}, f32[512,128]{1,0:T(8,128)S(1)}, f32[8,512]{1,0:T(8,128)S(1)}, bf16[128,128]{1,0:T(8,128)(2,1)S(1)}) custom-call(s32[1]{0:T(128)} %bitcast.me_ref, s32[32]{0:T(128)S(1)} %copy-done.9, s32[32]{0:T(128)S(1)} %copy-done.10, s32[32]{0:T(128)S(1)} %copy-done.12, ...), custom_call_target="tpu_custom_call" | custom-call | flops 15000000512 | bytes 50000000 | tf_op jit(solution)/shard_map/prepare/pallas_call | solution.py:374
  27.2 0.6 copy-done.2
  27.8 18.3 %all-to-all-done.recv_ref = bf16[128,4,1920]{2,1,0:T(4,128)(2,1)S(1)} async-done(((bf16[128,4,1920]{2,1,0:T(4,128)(2,1)}), bf16[128,4,1920]{2,1,0:T(4,128)(2,1)S(1)}, u32[]{:S(2)}, u32[]{:S(2)}) %all-to-all-start) | async-done | bytes 1966112 | tf_op jit(solution)/shard_map/all_to_all | solution.py:435
  46.1 6.9 %attend.1 = (bf16[128,4,1920]{2,1,0:T(4,128)(2,1)}, bf16[128,640]{1,0:T(8,128)(2,1)}, bf16[128,640]{1,0:T(8,128)(2,1)}, bf16[2,128,640]{2,1,0:T(8,128)(2,1)}) custom-call(s32[1]{0:T(128)} %bitcast.me_ref, f32[512,128]{1,0:T(8,128)S(1)} %get-tuple-element.21.bias_ref, f32[8,512]{1,0:T(8,128)S(1)} %get-tuple-element.22.live_ref, ...), custom_call_target="tpu_custom_call" | custom-call | tf_op jit(solution)/shard_map/attend/pallas_call | solution.py:410
  52.9 0.1 collective-permute-start.4
  53.1 5.3 %all-to-all-start.1 = ((bf16[128,4,1920]{2,1,0:T(4,128)(2,1)}), bf16[128,4,1920]{2,1,0:T(4,128)(2,1)S(1)}, u32[]{:S(2)}, u32[]{:S(2)}) async-start(bf16[128,4,1920]{2,1,0:T(4,128)(2,1)} %get-tuple-element.30), calls=%async_computation.1 | async-start | bytes 3932160 | tf_op jit(solution)/shard_map/all_to_all | solution.py:435
  58.4 3.1 %collective-permute-done.4.far_ref = bf16[2,128,640]{2,1,0:T(8,128)(2,1)S(1)} collective-permute-done((bf16[2,128,640]{2,1,0:T(8,128)(2,1)}, bf16[2,128,640]{2,1,0:T(8,128)(2,1)S(1)}, u32[]{:S(2)}, u32[]{:S(2)}) %collective-permute-start.4) | collective-permute-done | bytes 327712 | tf_op jit(solution)/shard_map/ppermute | solution.py:439
  61.6 3.2 %collective-permute-start.5 = (bf16[2,128,640]{2,1,0:T(8,128)(2,1)S(1)}, bf16[2,128,640]{2,1,0:T(8,128)(2,1)S(1)}, u32[]{:S(2)}, u32[]{:S(2)}) collective-permute-start(bf16[2,128,640]{2,1,0:T(8,128)(2,1)S(1)} %collective-permute-done.4.far_ref), channel_id=1, source_target_pairs={{0,1},{1,0},{2,3},{3,2},{4,5},{5,4},{6,7},{7,6},{8,9},{9,8},{10,11... | collective-permute-start | bytes 983048 | tf_op jit(solution)/shard_map/ppermute | solution.py:439
  64.8 1.5 %collective-permute-done.3.i1_ref = bf16[128,640]{1,0:T(8,128)(2,1)S(1)} collective-permute-done((bf16[128,640]{1,0:T(8,128)(2,1)S(1)}, bf16[128,640]{1,0:T(8,128)(2,1)S(1)}, u32[]{:S(2)}, u32[]{:S(2)}) %collective-permute-start.3) | collective-permute-done | bytes 163872 | tf_op jit(solution)/shard_map/ppermute | solution.py:439
  66.3 2.0 %collect.1 = bf16[128,2560]{1,0:T(8,128)(2,1)} custom-call(s32[1]{0:T(128)} %bitcast.me_ref, s32[32]{0:T(128)S(1)} %copy-done.11, s32[32]{0:T(128)S(1)} %copy-done.13, f32[8,20]{1,0:T(8,128)S(1)} %copy-done.8, s32[128,128]{1,0:T(8,128)S(1)} %bitcast.7, bf16[128,640]{1,0:T(8,128)(2,1)S(1)} %copy-done.6, bf16[128,640]{1,0:T(8,128)(2,1)S(1)} %collective-permute-done.3.i1_ref, ...), custom_call_target="tpu_custom_call" | custom-call | flops 15000000512 | bytes 50000000 | tf_op jit(solution)/shard_map/collect/pallas_call | solution.py:398
  68.2 19.3 %all-to-all-done.1 = bf16[128,4,1920]{2,1,0:T(4,128)(2,1)S(1)} async-done(((bf16[128,4,1920]{2,1,0:T(4,128)(2,1)}), bf16[128,4,1920]{2,1,0:T(4,128)(2,1)S(1)}, u32[]{:S(2)}, u32[]{:S(2)}) %all-to-all-start.1) | async-done | bytes 1966112 | tf_op jit(solution)/shard_map/all_to_all | solution.py:435
  87.6 1.6 %unpack.1 = (bf16[128,2560]{1,0:T(8,128)(2,1)}, bf16[128,2560]{1,0:T(8,128)(2,1)}, bf16[128,2560]{1,0:T(8,128)(2,1)}) custom-call(bf16[128,128]{1,0:T(8,128)(2,1)S(1)} %copy-done.3, bf16[32,4,4,1920]{3,2,1,0:T(4,128)(2,1)S(1)} %bitcast.4), custom_call_target="tpu_custom_call" | custom-call | tf_op jit(solution)/shard_map/unpack/pallas_call | solution.py:359
  (29 shorter events, 0.1 us)
Async XLA Ops:
  4.1 12.8 %collective-permute-start.1 = (bf16[2,128,640]{2,1,0:T(8,128)(2,1)S(1)}, bf16[2,128,640]{2,1,0:T(8,128)(2,1)S(1)}, u32[]{:S(2)}, u32[]{:S(2)}) collective-permute-start(bf16[2,128,640]{2,1,0:T(8,128)(2,1)S(1)} %get-tuple-element.20), channel_id=1, source_target_pairs={{0,2},{1,3},{2,0},{3,1},{4,6},{5,7},{6,4},{7,5},{8,10},{9,11},{10,... | collective-permute-start | bytes 983048 | tf_op jit(solution)/shard_map/ppermute | solution.py:439
  6.2 12.5 %copy-start.15 = (bf16[128,640]{1,0:T(8,128)(2,1)S(1)}, bf16[128,640]{1,0:T(8,128)(2,1)}, u32[]{:S(2)}) copy-start(bf16[128,640]{1,0:T(8,128)(2,1)} %get-tuple-element.19) | copy-start | bytes 491524
  6.2 39.8 %all-to-all-start = ((bf16[128,4,1920]{2,1,0:T(4,128)(2,1)}), bf16[128,4,1920]{2,1,0:T(4,128)(2,1)S(1)}, u32[]{:S(2)}, u32[]{:S(2)}) async-start(bf16[128,4,1920]{2,1,0:T(4,128)(2,1)} %bitcast.8), calls=%async_computation | async-start | bytes 3932160 | tf_op jit(solution)/shard_map/all_to_all | solution.py:435
  16.9 3.3 %collective-permute-start.2 = (bf16[2,128,640]{2,1,0:T(8,128)(2,1)S(1)}, bf16[2,128,640]{2,1,0:T(8,128)(2,1)S(1)}, u32[]{:S(2)}, u32[]{:S(2)}) collective-permute-start(bf16[2,128,640]{2,1,0:T(8,128)(2,1)S(1)} %collective-permute-done.1.far_ref), channel_id=1, source_target_pairs={{0,1},{1,0},{2,3},{3,2},{4,5},{5,4},{6,7},{7,6},{8,9},{9,8},{10,11... | collective-permute-start | bytes 983048 | tf_op jit(solution)/shard_map/ppermute | solution.py:439
  18.1 0.7 copy-start.4
  18.8 1.4 %collective-permute-start = (bf16[128,640]{1,0:T(8,128)(2,1)S(1)}, bf16[128,640]{1,0:T(8,128)(2,1)S(1)}, u32[]{:S(2)}, u32[]{:S(2)}) collective-permute-start(bf16[128,640]{1,0:T(8,128)(2,1)S(1)} %copy-done.15), channel_id=1, source_target_pairs={{0,1},{1,0},{2,3},{3,2},{4,5},{5,4},{6,7},{7,6},{8,9},{9,8},{10,11... | collective-permute-start | bytes 491528 | tf_op jit(solution)/shard_map/ppermute | solution.py:439
  20.2 0.8 copy-start
  21.0 1.0 %copy-start.5 = (bf16[2,128,640]{2,1,0:T(8,128)(2,1)S(1)}, bf16[2,128,640]{2,1,0:T(8,128)(2,1)}, u32[]{:S(2)}) copy-start(bf16[2,128,640]{2,1,0:T(8,128)(2,1)} %copy-done.4) | copy-start | bytes 983044
  22.0 0.7 copy-start.7
  22.7 0.7 copy-start.9
  23.3 0.7 copy-start.10
  24.0 0.7 copy-start.12
  27.2 0.6 copy-start.2
  52.9 8.6 %collective-permute-start.4 = (bf16[2,128,640]{2,1,0:T(8,128)(2,1)}, bf16[2,128,640]{2,1,0:T(8,128)(2,1)S(1)}, u32[]{:S(2)}, u32[]{:S(2)}) collective-permute-start(bf16[2,128,640]{2,1,0:T(8,128)(2,1)} %get-tuple-element.28), channel_id=1, source_target_pairs={{0,2},{1,3},{2,0},{3,1},{4,6},{5,7},{6,4},{7,5},{8,10},{9,11},{10,... | collective-permute-start | bytes 983048 | tf_op jit(solution)/shard_map/ppermute | solution.py:439
  53.0 11.7 %copy-start.14 = (bf16[128,640]{1,0:T(8,128)(2,1)S(1)}, bf16[128,640]{1,0:T(8,128)(2,1)}, u32[]{:S(2)}) copy-start(bf16[128,640]{1,0:T(8,128)(2,1)} %get-tuple-element.27) | copy-start | bytes 491524
  53.0 13.2 %copy-start.1 = (s32[16384]{0:T(1024)S(1)}, s32[16384]{0:T(1024)}, u32[]{:S(2)}) copy-start(s32[16384]{0:T(1024)} %param.17) | copy-start | bytes 196612
  53.1 13.2 %copy-start.6 = (bf16[128,640]{1,0:T(8,128)(2,1)S(1)}, bf16[128,640]{1,0:T(8,128)(2,1)}, u32[]{:S(2)}) copy-start(bf16[128,640]{1,0:T(8,128)(2,1)} %get-tuple-element.26.i0_ref) | copy-start | bytes 491524
  53.1 13.2 %copy-start.8 = (f32[8,20]{1,0:T(8,128)S(1)}, f32[8,20]{1,0:T(8,128)}, u32[]{:S(2)}) copy-start(f32[8,20]{1,0:T(8,128)} %guide_ref.3) | copy-start | bytes 1924
  53.1 13.2 %copy-start.11 = (s32[32]{0:T(128)S(1)}, s32[32]{0:T(128)}, u32[]{:S(2)}) copy-start(s32[32]{0:T(128)} %plan_ref.3) | copy-start | bytes 388
  53.1 13.2 %copy-start.13 = (s32[32]{0:T(128)S(1)}, s32[32]{0:T(128)}, u32[]{:S(2)}) copy-start(s32[32]{0:T(128)} %bins_ref.3) | copy-start | bytes 388
  53.1 34.5 %all-to-all-start.1 = ((bf16[128,4,1920]{2,1,0:T(4,128)(2,1)}), bf16[128,4,1920]{2,1,0:T(4,128)(2,1)S(1)}, u32[]{:S(2)}, u32[]{:S(2)}) async-start(bf16[128,4,1920]{2,1,0:T(4,128)(2,1)} %get-tuple-element.30), calls=%async_computation.1 | async-start | bytes 3932160 | tf_op jit(solution)/shard_map/all_to_all | solution.py:435
  61.6 4.7 %collective-permute-start.5 = (bf16[2,128,640]{2,1,0:T(8,128)(2,1)S(1)}, bf16[2,128,640]{2,1,0:T(8,128)(2,1)S(1)}, u32[]{:S(2)}, u32[]{:S(2)}) collective-permute-start(bf16[2,128,640]{2,1,0:T(8,128)(2,1)S(1)} %collective-permute-done.4.far_ref), channel_id=1, source_target_pairs={{0,1},{1,0},{2,3},{3,2},{4,5},{5,4},{6,7},{7,6},{8,9},{9,8},{10,11... | collective-permute-start | bytes 983048 | tf_op jit(solution)/shard_map/ppermute | solution.py:439
  64.7 1.5 %collective-permute-start.3 = (bf16[128,640]{1,0:T(8,128)(2,1)S(1)}, bf16[128,640]{1,0:T(8,128)(2,1)S(1)}, u32[]{:S(2)}, u32[]{:S(2)}) collective-permute-start(bf16[128,640]{1,0:T(8,128)(2,1)S(1)} %copy-done.14), channel_id=1, source_target_pairs={{0,1},{1,0},{2,3},{3,2},{4,5},{5,4},{6,7},{7,6},{8,9},{9,8},{10,11... | collective-permute-start | bytes 491528 | tf_op jit(solution)/shard_map/ppermute | solution.py:439
  66.3 21.3 %copy-start.3 = (bf16[128,128]{1,0:T(8,128)(2,1)S(1)}, bf16[128,128]{1,0:T(8,128)(2,1)}, u32[]{:S(2)}) copy-start(bf16[128,128]{1,0:T(8,128)(2,1)} %copy-done.2) | copy-start | bytes 98308

commit v7 on v6

--- a/solution.py
+++ b/solution.py
@@ -102,7 +102,7 @@
     for step, ref in ((1, stage_ref), (2, far_ref.at[0]), (3, far_ref.at[1])):
         lanes = part_lanes(jnp.bitwise_xor(me_ref[0] % N_SP, step))
         piece = pltpu.make_async_copy(cot_ref.at[:, lanes], ref, piece_sem.at[step - 1])
-        piece.start()
+        piece.start(priority=1)
         pieces.append(piece)
     index.wait()
     pick = row_picker(index_ref[...], me_ref[0])
@@ -121,7 +121,7 @@
         store = pltpu.make_async_copy(
             send_ref.at[:, :, :, lanes], out_ref.at[:, :, :, lanes], out_sem.at[array]
         )
-        store.start()
+        store.start(priority=1)
         stores.append(store)
     for piece in pieces[1:]:
         piece.wait()

time: 89.6 us -> 89.5 us (level)
  no operation moved by 1% of the time
where the time goes in v7:
time: 89.5 us; the launch traced here: 89 us
  waiting for transfers between devices  43.6 us (49%)
  starting transfers between devices  22.5 us (25%)
  Pallas kernels  16.3 us (18%)
  local copies, waits for them, and re-layouts  5.83 us (7%)
    all_to_all x2, waiting for transfers between devices, exchange(): lax.all_to_all(chunks, ('dp', 'sp'), split_axis=0, concat_axis=0, tiled=T...  37.6 us
    all_to_all x2, starting transfers between devices, exchange(): lax.all_to_all(chunks, ('dp', 'sp'), split_axis=0, concat_axis=0, tiled=T...  15.9 us
    pallas_call x1, Pallas kernels, attend(): pl.pallas_call(attend_kernel, out_shape=(pltpu.HBM((LOADERS, 4, CHUNK), B...  6.88 us
    ppermute x6, starting transfers between devices, swap(): return lax.ppermute(piece, 'sp', [(i, i ^ step) for i in range(N_SP)])  6.54 us
    ppermute x6, waiting for transfers between devices, swap(): return lax.ppermute(piece, 'sp', [(i, i ^ step) for i in range(N_SP)])  6.03 us
    unnamed x32, local copies, waits for them, and re-layouts  5.83 us
    pallas_call x1, Pallas kernels, pack(): pl.pallas_call(pack_kernel, out_shape=(pltpu.HBM((N_DP, N_SP, 4, CHUNK),...  3.37 us
    pallas_call x1, Pallas kernels, prepare(): pl.pallas_call(prepare_kernel, out_shape=(jax.ShapeDtypeStruct((GROUP, PA...  2.53 us
  transfers between devices with their start and end apart: 8, of which 5 were waited for; matrix products, arithmetic and copies ran while one was open for 0% of the time, Pallas kernels for 5%

profile of v7, /device:TPU:1, one launch (start us, length us, event | category | flops | bytes accessed | tf_op | source)
XLA Modules:
  0.0 89.0 jit_solution(1498968595722461348)
XLA Ops:
  0.6 3.4 %pack.1 = (bf16[32,4,4,1920]{3,2,1,0:T(4,128)(2,1)}, bf16[128,640]{1,0:T(8,128)(2,1)}, bf16[2,128,640]{2,1,0:T(8,128)(2,1)S(1)}) custom-call(s32[1]{0:T(128)} %bitcast.me_ref, s32[128,128]{1,0:T(8,128)} %bitcast.5, bf16[128,2560]{1,0:T(8,128)(2,1)} %q_ref.1, bf16[128,2560]{1,0:T(8,128)(2,1)} %k_ref.1, bf16[128,2560]{1,0:T(8,128)(2,1)} %v_ref.1, ...), custom_call_target="tpu_custom_call" | custom-call | tf_op jit(solution)/shard_map/pack/pallas_call | solution.py:336
  4.0 2.1 %collective-permute-start.1 = (bf16[2,128,640]{2,1,0:T(8,128)(2,1)S(1)}, bf16[2,128,640]{2,1,0:T(8,128)(2,1)S(1)}, u32[]{:S(2)}, u32[]{:S(2)}) collective-permute-start(bf16[2,128,640]{2,1,0:T(8,128)(2,1)S(1)} %get-tuple-element.20), channel_id=1, source_target_pairs={{0,2},{1,3},{2,0},{3,1},{4,6},{5,7},{6,4},{7,5},{8,10},{9,11},{10,... | collective-permute-start | bytes 983048 | tf_op jit(solution)/shard_map/ppermute | solution.py:439
  6.1 10.6 %all-to-all-start = ((bf16[128,4,1920]{2,1,0:T(4,128)(2,1)}), bf16[128,4,1920]{2,1,0:T(4,128)(2,1)S(1)}, u32[]{:S(2)}, u32[]{:S(2)}) async-start(bf16[128,4,1920]{2,1,0:T(4,128)(2,1)} %bitcast.8), calls=%async_computation | async-start | bytes 3932160 | tf_op jit(solution)/shard_map/all_to_all | solution.py:435
  16.8 1.1 %collective-permute-start.2 = (bf16[2,128,640]{2,1,0:T(8,128)(2,1)S(1)}, bf16[2,128,640]{2,1,0:T(8,128)(2,1)S(1)}, u32[]{:S(2)}, u32[]{:S(2)}) collective-permute-start(bf16[2,128,640]{2,1,0:T(8,128)(2,1)S(1)} %collective-permute-done.1.far_ref), channel_id=1, source_target_pairs={{0,1},{1,0},{2,3},{3,2},{4,5},{5,4},{6,7},{7,6},{8,9},{9,8},{10,11... | collective-permute-start | bytes 983048 | tf_op jit(solution)/shard_map/ppermute | solution.py:439
  17.9 0.7 copy-done.4
  18.7 1.4 %collective-permute-done.near_ref = bf16[128,640]{1,0:T(8,128)(2,1)S(1)} collective-permute-done((bf16[128,640]{1,0:T(8,128)(2,1)S(1)}, bf16[128,640]{1,0:T(8,128)(2,1)S(1)}, u32[]{:S(2)}, u32[]{:S(2)}) %collective-permute-start) | collective-permute-done | bytes 163872 | tf_op jit(solution)/shard_map/ppermute | solution.py:439
  20.1 0.8 copy-done
  20.9 1.0 %copy-done.5 = bf16[2,128,640]{2,1,0:T(8,128)(2,1)S(1)} copy-done((bf16[2,128,640]{2,1,0:T(8,128)(2,1)S(1)}, bf16[2,128,640]{2,1,0:T(8,128)(2,1)}, u32[]{:S(2)}) %copy-start.5) | copy-done | bytes 327704
  21.9 0.7 copy-done.7
  22.6 0.7 copy-done.9
  23.2 0.7 copy-done.10
  23.9 0.7 copy-done.12
  24.5 2.5 %prepare.1 = (bf16[512,640]{1,0:T(8,128)(2,1)S(1)}, bf16[640,512]{1,0:T(8,128)(2,1)S(1)}, f32[512,128]{1,0:T(8,128)S(1)}, f32[8,512]{1,0:T(8,128)S(1)}, bf16[128,128]{1,0:T(8,128)(2,1)S(1)}) custom-call(s32[1]{0:T(128)} %bitcast.me_ref, s32[32]{0:T(128)S(1)} %copy-done.9, s32[32]{0:T(128)S(1)} %copy-done.10, s32[32]{0:T(128)S(1)} %copy-done.12, ...), custom_call_target="tpu_custom_call" | custom-call | flops 15000000512 | bytes 50000000 | tf_op jit(solution)/shard_map/prepare/pallas_call | solution.py:374
  27.1 0.6 copy-done.2
  27.7 18.3 %all-to-all-done.recv_ref = bf16[128,4,1920]{2,1,0:T(4,128)(2,1)S(1)} async-done(((bf16[128,4,1920]{2,1,0:T(4,128)(2,1)}), bf16[128,4,1920]{2,1,0:T(4,128)(2,1)S(1)}, u32[]{:S(2)}, u32[]{:S(2)}) %all-to-all-start) | async-done | bytes 1966112 | tf_op jit(solution)/shard_map/all_to_all | solution.py:435
  46.0 6.9 %attend.1 = (bf16[128,4,1920]{2,1,0:T(4,128)(2,1)}, bf16[128,640]{1,0:T(8,128)(2,1)}, bf16[128,640]{1,0:T(8,128)(2,1)}, bf16[2,128,640]{2,1,0:T(8,128)(2,1)}) custom-call(s32[1]{0:T(128)} %bitcast.me_ref, f32[512,128]{1,0:T(8,128)S(1)} %get-tuple-element.21.bias_ref, f32[8,512]{1,0:T(8,128)S(1)} %get-tuple-element.22.live_ref, ...), custom_call_target="tpu_custom_call" | custom-call | tf_op jit(solution)/shard_map/attend/pallas_call | solution.py:410
  52.8 0.1 collective-permute-start.4
  53.0 5.3 %all-to-all-start.1 = ((bf16[128,4,1920]{2,1,0:T(4,128)(2,1)}), bf16[128,4,1920]{2,1,0:T(4,128)(2,1)S(1)}, u32[]{:S(2)}, u32[]{:S(2)}) async-start(bf16[128,4,1920]{2,1,0:T(4,128)(2,1)} %get-tuple-element.30), calls=%async_computation.1 | async-start | bytes 3932160 | tf_op jit(solution)/shard_map/all_to_all | solution.py:435
  58.3 3.2 %collective-permute-done.4.far_ref = bf16[2,128,640]{2,1,0:T(8,128)(2,1)S(1)} collective-permute-done((bf16[2,128,640]{2,1,0:T(8,128)(2,1)}, bf16[2,128,640]{2,1,0:T(8,128)(2,1)S(1)}, u32[]{:S(2)}, u32[]{:S(2)}) %collective-permute-start.4) | collective-permute-done | bytes 327712 | tf_op jit(solution)/shard_map/ppermute | solution.py:439
  61.5 3.2 %collective-permute-start.5 = (bf16[2,128,640]{2,1,0:T(8,128)(2,1)S(1)}, bf16[2,128,640]{2,1,0:T(8,128)(2,1)S(1)}, u32[]{:S(2)}, u32[]{:S(2)}) collective-permute-start(bf16[2,128,640]{2,1,0:T(8,128)(2,1)S(1)} %collective-permute-done.4.far_ref), channel_id=1, source_target_pairs={{0,1},{1,0},{2,3},{3,2},{4,5},{5,4},{6,7},{7,6},{8,9},{9,8},{10,11... | collective-permute-start | bytes 983048 | tf_op jit(solution)/shard_map/ppermute | solution.py:439
  64.6 1.5 %collective-permute-done.3.i1_ref = bf16[128,640]{1,0:T(8,128)(2,1)S(1)} collective-permute-done((bf16[128,640]{1,0:T(8,128)(2,1)S(1)}, bf16[128,640]{1,0:T(8,128)(2,1)S(1)}, u32[]{:S(2)}, u32[]{:S(2)}) %collective-permute-start.3) | collective-permute-done | bytes 163872 | tf_op jit(solution)/shard_map/ppermute | solution.py:439
  66.2 2.0 %collect.1 = bf16[128,2560]{1,0:T(8,128)(2,1)} custom-call(s32[1]{0:T(128)} %bitcast.me_ref, s32[32]{0:T(128)S(1)} %copy-done.11, s32[32]{0:T(128)S(1)} %copy-done.13, f32[8,20]{1,0:T(8,128)S(1)} %copy-done.8, s32[128,128]{1,0:T(8,128)S(1)} %bitcast.7, bf16[128,640]{1,0:T(8,128)(2,1)S(1)} %copy-done.6, bf16[128,640]{1,0:T(8,128)(2,1)S(1)} %collective-permute-done.3.i1_ref, ...), custom_call_target="tpu_custom_call" | custom-call | flops 15000000512 | bytes 50000000 | tf_op jit(solution)/shard_map/collect/pallas_call | solution.py:398
  68.1 19.3 %all-to-all-done.1 = bf16[128,4,1920]{2,1,0:T(4,128)(2,1)S(1)} async-done(((bf16[128,4,1920]{2,1,0:T(4,128)(2,1)}), bf16[128,4,1920]{2,1,0:T(4,128)(2,1)S(1)}, u32[]{:S(2)}, u32[]{:S(2)}) %all-to-all-start.1) | async-done | bytes 1966112 | tf_op jit(solution)/shard_map/all_to_all | solution.py:435
  87.5 1.6 %unpack.1 = (bf16[128,2560]{1,0:T(8,128)(2,1)}, bf16[128,2560]{1,0:T(8,128)(2,1)}, bf16[128,2560]{1,0:T(8,128)(2,1)}) custom-call(bf16[128,128]{1,0:T(8,128)(2,1)S(1)} %copy-done.3, bf16[32,4,4,1920]{3,2,1,0:T(4,128)(2,1)S(1)} %bitcast.4), custom_call_target="tpu_custom_call" | custom-call | tf_op jit(solution)/shard_map/unpack/pallas_call | solution.py:359
  (29 shorter events, 0.1 us)
Async XLA Ops:
  4.0 12.8 %collective-permute-start.1 = (bf16[2,128,640]{2,1,0:T(8,128)(2,1)S(1)}, bf16[2,128,640]{2,1,0:T(8,128)(2,1)S(1)}, u32[]{:S(2)}, u32[]{:S(2)}) collective-permute-start(bf16[2,128,640]{2,1,0:T(8,128)(2,1)S(1)} %get-tuple-element.20), channel_id=1, source_target_pairs={{0,2},{1,3},{2,0},{3,1},{4,6},{5,7},{6,4},{7,5},{8,10},{9,11},{10,... | collective-permute-start | bytes 983048 | tf_op jit(solution)/shard_map/ppermute | solution.py:439
  6.1 12.5 %copy-start.15 = (bf16[128,640]{1,0:T(8,128)(2,1)S(1)}, bf16[128,640]{1,0:T(8,128)(2,1)}, u32[]{:S(2)}) copy-start(bf16[128,640]{1,0:T(8,128)(2,1)} %get-tuple-element.19) | copy-start | bytes 491524
  6.1 39.8 %all-to-all-start = ((bf16[128,4,1920]{2,1,0:T(4,128)(2,1)}), bf16[128,4,1920]{2,1,0:T(4,128)(2,1)S(1)}, u32[]{:S(2)}, u32[]{:S(2)}) async-start(bf16[128,4,1920]{2,1,0:T(4,128)(2,1)} %bitcast.8), calls=%async_computation | async-start | bytes 3932160 | tf_op jit(solution)/shard_map/all_to_all | solution.py:435
  16.8 3.3 %collective-permute-start.2 = (bf16[2,128,640]{2,1,0:T(8,128)(2,1)S(1)}, bf16[2,128,640]{2,1,0:T(8,128)(2,1)S(1)}, u32[]{:S(2)}, u32[]{:S(2)}) collective-permute-start(bf16[2,128,640]{2,1,0:T(8,128)(2,1)S(1)} %collective-permute-done.1.far_ref), channel_id=1, source_target_pairs={{0,1},{1,0},{2,3},{3,2},{4,5},{5,4},{6,7},{7,6},{8,9},{9,8},{10,11... | collective-permute-start | bytes 983048 | tf_op jit(solution)/shard_map/ppermute | solution.py:439
  17.9 0.7 copy-start.4
  18.7 1.4 %collective-permute-start = (bf16[128,640]{1,0:T(8,128)(2,1)S(1)}, bf16[128,640]{1,0:T(8,128)(2,1)S(1)}, u32[]{:S(2)}, u32[]{:S(2)}) collective-permute-start(bf16[128,640]{1,0:T(8,128)(2,1)S(1)} %copy-done.15), channel_id=1, source_target_pairs={{0,1},{1,0},{2,3},{3,2},{4,5},{5,4},{6,7},{7,6},{8,9},{9,8},{10,11... | collective-permute-start | bytes 491528 | tf_op jit(solution)/shard_map/ppermute | solution.py:439
  20.1 0.8 copy-start
  20.9 1.0 %copy-start.5 = (bf16[2,128,640]{2,1,0:T(8,128)(2,1)S(1)}, bf16[2,128,640]{2,1,0:T(8,128)(2,1)}, u32[]{:S(2)}) copy-start(bf16[2,128,640]{2,1,0:T(8,128)(2,1)} %copy-done.4) | copy-start | bytes 983044
  21.9 0.7 copy-start.7
  22.6 0.7 copy-start.9
  23.2 0.7 copy-start.10
  23.9 0.7 copy-start.12
  27.1 0.6 copy-start.2
  52.8 8.6 %collective-permute-start.4 = (bf16[2,128,640]{2,1,0:T(8,128)(2,1)}, bf16[2,128,640]{2,1,0:T(8,128)(2,1)S(1)}, u32[]{:S(2)}, u32[]{:S(2)}) collective-permute-start(bf16[2,128,640]{2,1,0:T(8,128)(2,1)} %get-tuple-element.28), channel_id=1, source_target_pairs={{0,2},{1,3},{2,0},{3,1},{4,6},{5,7},{6,4},{7,5},{8,10},{9,11},{10,... | collective-permute-start | bytes 983048 | tf_op jit(solution)/shard_map/ppermute | solution.py:439
  52.9 11.7 %copy-start.14 = (bf16[128,640]{1,0:T(8,128)(2,1)S(1)}, bf16[128,640]{1,0:T(8,128)(2,1)}, u32[]{:S(2)}) copy-start(bf16[128,640]{1,0:T(8,128)(2,1)} %get-tuple-element.27) | copy-start | bytes 491524
  52.9 13.2 %copy-start.1 = (s32[16384]{0:T(1024)S(1)}, s32[16384]{0:T(1024)}, u32[]{:S(2)}) copy-start(s32[16384]{0:T(1024)} %param.17) | copy-start | bytes 196612
  53.0 13.2 %copy-start.6 = (bf16[128,640]{1,0:T(8,128)(2,1)S(1)}, bf16[128,640]{1,0:T(8,128)(2,1)}, u32[]{:S(2)}) copy-start(bf16[128,640]{1,0:T(8,128)(2,1)} %get-tuple-element.26.i0_ref) | copy-start | bytes 491524
  53.0 13.2 %copy-start.8 = (f32[8,20]{1,0:T(8,128)S(1)}, f32[8,20]{1,0:T(8,128)}, u32[]{:S(2)}) copy-start(f32[8,20]{1,0:T(8,128)} %guide_ref.3) | copy-start | bytes 1924
  53.0 13.2 %copy-start.11 = (s32[32]{0:T(128)S(1)}, s32[32]{0:T(128)}, u32[]{:S(2)}) copy-start(s32[32]{0:T(128)} %plan_ref.3) | copy-start | bytes 388
  53.0 13.2 %copy-start.13 = (s32[32]{0:T(128)S(1)}, s32[32]{0:T(128)}, u32[]{:S(2)}) copy-start(s32[32]{0:T(128)} %bins_ref.3) | copy-start | bytes 388
  53.0 34.5 %all-to-all-start.1 = ((bf16[128,4,1920]{2,1,0:T(4,128)(2,1)}), bf16[128,4,1920]{2,1,0:T(4,128)(2,1)S(1)}, u32[]{:S(2)}, u32[]{:S(2)}) async-start(bf16[128,4,1920]{2,1,0:T(4,128)(2,1)} %get-tuple-element.30), calls=%async_computation.1 | async-start | bytes 3932160 | tf_op jit(solution)/shard_map/all_to_all | solution.py:435
  61.5 4.7 %collective-permute-start.5 = (bf16[2,128,640]{2,1,0:T(8,128)(2,1)S(1)}, bf16[2,128,640]{2,1,0:T(8,128)(2,1)S(1)}, u32[]{:S(2)}, u32[]{:S(2)}) collective-permute-start(bf16[2,128,640]{2,1,0:T(8,128)(2,1)S(1)} %collective-permute-done.4.far_ref), channel_id=1, source_target_pairs={{0,1},{1,0},{2,3},{3,2},{4,5},{5,4},{6,7},{7,6},{8,9},{9,8},{10,11... | collective-permute-start | bytes 983048 | tf_op jit(solution)/shard_map/ppermute | solution.py:439
  64.6 1.5 %collective-permute-start.3 = (bf16[128,640]{1,0:T(8,128)(2,1)S(1)}, bf16[128,640]{1,0:T(8,128)(2,1)S(1)}, u32[]{:S(2)}, u32[]{:S(2)}) collective-permute-start(bf16[128,640]{1,0:T(8,128)(2,1)S(1)} %copy-done.14), channel_id=1, source_target_pairs={{0,1},{1,0},{2,3},{3,2},{4,5},{5,4},{6,7},{7,6},{8,9},{9,8},{10,11... | collective-permute-start | bytes 491528 | tf_op jit(solution)/shard_map/ppermute | solution.py:439
  66.2 21.3 %copy-start.3 = (bf16[128,128]{1,0:T(8,128)(2,1)S(1)}, bf16[128,128]{1,0:T(8,128)(2,1)}, u32[]{:S(2)}) copy-start(bf16[128,128]{1,0:T(8,128)(2,1)} %copy-done.2) | copy-start | bytes 98308

commit v8 on v7

--- a/solution.py
+++ b/solution.py
@@ -79,17 +79,14 @@
     v_ref,
     cot_ref,
     out_ref,
-    near_ref,
     far_ref,
     index_ref,
     in_ref,
     send_ref,
-    stage_ref,
     index_sem,
     in_sem,
     out_sem,
     piece_sem,
-    near_sem,
 ):
     index = pltpu.make_async_copy(table_ref, index_ref, index_sem)
     index.start()
@@ -99,9 +96,9 @@
         load.start()
         loads.append(load)
     pieces = []
-    for step, ref in ((1, stage_ref), (2, far_ref.at[0]), (3, far_ref.at[1])):
+    for step in (2, 3):
         lanes = part_lanes(jnp.bitwise_xor(me_ref[0] % N_SP, step))
-        piece = pltpu.make_async_copy(cot_ref.at[:, lanes], ref, piece_sem.at[step - 1])
+        piece = pltpu.make_async_copy(cot_ref.at[:, lanes], far_ref.at[step - 2], piece_sem.at[step - 2])
         piece.start(priority=1)
         pieces.append(piece)
     index.wait()
@@ -109,11 +106,6 @@
     stores = []
     for array in range(3):
         loads[array].wait()
-        if array == 2:
-            pieces[0].wait()
-            near = pltpu.make_async_copy(stage_ref, near_ref, near_sem)
-            near.start()
-            stores.append(near)
         lanes = pl.ds(array * PART, PART)
         for part in range(N_SP):
             rows = dot(pick, in_ref[array, :, pl.ds(part * PART, PART)]).astype(BF)
@@ -123,7 +115,7 @@
         )
         store.start(priority=1)
         stores.append(store)
-    for piece in pieces[1:]:
+    for piece in pieces:
         piece.wait()
     for store in stores:
         store.wait()
@@ -333,26 +325,24 @@
 
 
 def pack(me, table, queries, keys, values, cotangent):
-    chunks, *pieces = pl.pallas_call(
+    chunks, far = pl.pallas_call(
         pack_kernel,
-        out_shape=(pltpu.HBM((N_DP, N_SP, 4, CHUNK), BF), pltpu.HBM((ROWS, PART), BF), PIECES),
+        out_shape=(pltpu.HBM((N_DP, N_SP, 4, CHUNK), BF), PIECES),
         in_specs=[SMEM] + [HBM] * 5,
-        out_specs=(HBM, HBM, VMEM),
+        out_specs=(HBM, VMEM),
         scratch_shapes=[
             pltpu.VMEM((LOADERS, ROWS), jnp.int32),
             pltpu.VMEM((3, ROWS, WIDTH), BF),
             pltpu.VMEM((N_DP, N_SP, 4, CHUNK), BF),
-            pltpu.VMEM((ROWS, PART), BF),
             pltpu.SemaphoreType.DMA,
             pltpu.SemaphoreType.DMA((3,)),
             pltpu.SemaphoreType.DMA((3,)),
-            pltpu.SemaphoreType.DMA((N_SP - 1,)),
-            pltpu.SemaphoreType.DMA,
+            pltpu.SemaphoreType.DMA((2,)),
         ],
         compiler_params=PARAMS,
         name="pack",
     )(me, in_hbm(table), in_hbm(queries), in_hbm(keys), in_hbm(values), in_hbm(cotangent))
-    return chunks.reshape(LOADERS, 4, CHUNK), pieces
+    return chunks.reshape(LOADERS, 4, CHUNK), far
 
 
 def unpack(pick, chunks):
@@ -457,10 +447,11 @@
 ):
     me = (lax.axis_index("dp") * N_SP + lax.axis_index("sp")).astype(jnp.int32).reshape(1)
     table = block_source.reshape(LOADERS, ROWS)
-    packed, pieces = pack(me, table, queries, key_rows, value_rows, cotangent)
+    packed, far = pack(me, table, queries, key_rows, value_rows, cotangent)
     chunks = exchange(packed)
+    near = lax.dynamic_slice_in_dim(cotangent, jnp.bitwise_xor(lax.axis_index("sp"), 1) * PART, PART, axis=1)
     grad, turned, bias, live, pick = prepare(
-        me, lengths, sample_plan, guide_bins, guide_table, table, cotangent, swap_pieces(*pieces)
+        me, lengths, sample_plan, guide_bins, guide_table, table, cotangent, swap_pieces(near, far)
     )
     grads, own, *outs = attend(me, bias, live, grad, turned, chunks)
     out_pieces = own, *swap_pieces(*outs)

time: 89.5 us -> 89.5 us (level)
  waiting for transfers between devices: 43.6 us -> 41.6 us
  local copies, waits for them, and re-layouts: 5.83 us -> 7.74 us
    all_to_all x2, waiting for transfers between devices: 37.6 us -> 35.6 us  [exchange(): lax.all_to_all(chunks, ('dp', 'sp'), split_axis=0, concat_axis=0, tiled=T...]
    unnamed x32 -> x34, local copies, waits for them, and re-layouts: 5.83 us -> 6.81 us
    dynamic_slice x0 -> x1, local copies, waits for them, and re-layouts: none -> 0.93 us  [per_device(): lax.dynamic_slice_in_dim(cotangent, jnp.bitwise_xor(lax.axis_index('sp'),...]
  transfers between devices with their start and end apart: 8 -> 8, of which waited for: 5 -> 5; matrix products, arithmetic and copies ran while one was open for 0% -> 1% of each run, Pallas kernels for 5% -> 5%
where the time goes in v8:
time: 89.5 us; the launch traced here: 89 us
  waiting for transfers between devices  41.6 us (46%)
  starting transfers between devices  22.7 us (25%)
  Pallas kernels  16.2 us (18%)
  local copies, waits for them, and re-layouts  7.74 us (9%)
    all_to_all x2, waiting for transfers between devices, exchange(): lax.all_to_all(chunks, ('dp', 'sp'), split_axis=0, concat_axis=0, tiled=T...  35.6 us
    all_to_all x2, starting transfers between devices, exchange(): lax.all_to_all(chunks, ('dp', 'sp'), split_axis=0, concat_axis=0, tiled=T...  16 us
    pallas_call x1, Pallas kernels, attend(): pl.pallas_call(attend_kernel, out_shape=(pltpu.HBM((LOADERS, 4, CHUNK), B...  6.88 us
    unnamed x34, local copies, waits for them, and re-layouts  6.81 us
    ppermute x6, starting transfers between devices, swap(): return lax.ppermute(piece, 'sp', [(i, i ^ step) for i in range(N_SP)])  6.71 us
    ppermute x6, waiting for transfers between devices, swap(): return lax.ppermute(piece, 'sp', [(i, i ^ step) for i in range(N_SP)])  5.97 us
    pallas_call x1, Pallas kernels, pack(): pl.pallas_call(pack_kernel, out_shape=(pltpu.HBM((N_DP, N_SP, 4, CHUNK),...  3.3 us
    pallas_call x1, Pallas kernels, prepare(): pl.pallas_call(prepare_kernel, out_shape=(jax.ShapeDtypeStruct((GROUP, PA...  2.53 us
  transfers between devices with their start and end apart: 8, of which 5 were waited for; matrix products, arithmetic and copies ran while one was open for 1% of the time, Pallas kernels for 5%

profile of v8, /device:TPU:1, one launch (start us, length us, event | category | flops | bytes accessed | tf_op | source)
XLA Modules:
  0.0 89.0 jit_solution(14438531855388435499)
XLA Ops:
  0.6 3.3 %pack.1 = (bf16[32,4,4,1920]{3,2,1,0:T(4,128)(2,1)}, bf16[2,128,640]{2,1,0:T(8,128)(2,1)S(1)}) custom-call(s32[1]{0:T(128)} %bitcast.me_ref, s32[128,128]{1,0:T(8,128)} %bitcast.5, bf16[128,2560]{1,0:T(8,128)(2,1)} %q_ref.1, bf16[128,2560]{1,0:T(8,128)(2,1)} %k_ref.1, bf16[128,2560]{1,0:T(8,128)(2,1)} %v_ref.1, bf16[128,2560]{1,0:T(8,128)(2,1)} %cot_ref.3), custom_call_target="tpu_custom_call" | custom-call | tf_op jit(solution)/shard_map/pack/pallas_call | solution.py:328
  3.9 2.1 %collective-permute-start.1 = (bf16[2,128,640]{2,1,0:T(8,128)(2,1)S(1)}, bf16[2,128,640]{2,1,0:T(8,128)(2,1)S(1)}, u32[]{:S(2)}, u32[]{:S(2)}) collective-permute-start(bf16[2,128,640]{2,1,0:T(8,128)(2,1)S(1)} %get-tuple-element.18), channel_id=1, source_target_pairs={{0,2},{1,3},{2,0},{3,1},{4,6},{5,7},{6,4},{7,5},{8,10},{9,11},{10,... | collective-permute-start | bytes 983048 | tf_op jit(solution)/shard_map/ppermute | solution.py:429
  6.1 10.7 %all-to-all-start = ((bf16[128,4,1920]{2,1,0:T(4,128)(2,1)}), bf16[128,4,1920]{2,1,0:T(4,128)(2,1)S(1)}, u32[]{:S(2)}, u32[]{:S(2)}) async-start(bf16[128,4,1920]{2,1,0:T(4,128)(2,1)} %bitcast.8), calls=%async_computation | async-start | bytes 3932160 | tf_op jit(solution)/shard_map/all_to_all | solution.py:425
  16.7 1.1 %collective-permute-start.2 = (bf16[2,128,640]{2,1,0:T(8,128)(2,1)S(1)}, bf16[2,128,640]{2,1,0:T(8,128)(2,1)S(1)}, u32[]{:S(2)}, u32[]{:S(2)}) collective-permute-start(bf16[2,128,640]{2,1,0:T(8,128)(2,1)S(1)} %collective-permute-done.1.far_ref), channel_id=1, source_target_pairs={{0,1},{1,0},{2,3},{3,2},{4,5},{5,4},{6,7},{7,6},{8,9},{9,8},{10,11... | collective-permute-start | bytes 983048 | tf_op jit(solution)/shard_map/ppermute | solution.py:429
  17.9 0.9 %constant_dynamic-slice_fusion = bf16[128,640]{1,0:T(8,128)(2,1)S(1)} fusion(bf16[128,2560]{1,0:T(8,128)(2,1)} %cot_ref.3, s32[]{:T(128)S(6)} %select_n.3), kind=kLoop, calls=%fused_computation | loop fusion | bytes 327684 | tf_op jit(solution)/shard_map/dynamic_slice | solution.py:452
  18.9 1.4 %collective-permute-done.near_ref = bf16[128,640]{1,0:T(8,128)(2,1)S(1)} collective-permute-done((bf16[128,640]{1,0:T(8,128)(2,1)S(1)}, bf16[128,640]{1,0:T(8,128)(2,1)S(1)}, u32[]{:S(2)}, u32[]{:S(2)}) %collective-permute-start) | collective-permute-done | bytes 163872 | tf_op jit(solution)/shard_map/ppermute | solution.py:429
  20.3 0.7 copy-done.6
  21.0 0.8 copy-done
  21.9 1.0 %copy-done.5 = bf16[2,128,640]{2,1,0:T(8,128)(2,1)S(1)} copy-done((bf16[2,128,640]{2,1,0:T(8,128)(2,1)S(1)}, bf16[2,128,640]{2,1,0:T(8,128)(2,1)}, u32[]{:S(2)}) %copy-start.5) | copy-done | bytes 327704
  22.9 1.0 %copy-done.7 = bf16[2,128,640]{2,1,0:T(8,128)(2,1)S(1)} copy-done((bf16[2,128,640]{2,1,0:T(8,128)(2,1)S(1)}, bf16[2,128,640]{2,1,0:T(8,128)(2,1)}, u32[]{:S(2)}) %copy-start.7) | copy-done | bytes 327704
  23.8 0.7 copy-done.9
  24.5 0.7 copy-done.11
  25.2 0.7 copy-done.12
  25.8 0.7 copy-done.14
  26.5 2.5 %prepare.1 = (bf16[512,640]{1,0:T(8,128)(2,1)S(1)}, bf16[640,512]{1,0:T(8,128)(2,1)S(1)}, f32[512,128]{1,0:T(8,128)S(1)}, f32[8,512]{1,0:T(8,128)S(1)}, bf16[128,128]{1,0:T(8,128)(2,1)S(1)}) custom-call(s32[1]{0:T(128)} %bitcast.me_ref, s32[32]{0:T(128)S(1)} %copy-done.11, s32[32]{0:T(128)S(1)} %copy-done.12, s32[32]{0:T(128)S(1)} %copy-done.14, ...), custom_call_target="tpu_custom_call" | custom-call | flops 15000000512 | bytes 50000000 | tf_op jit(solution)/shard_map/prepare/pallas_call | solution.py:364
  29.6 16.3 %all-to-all-done.recv_ref = bf16[128,4,1920]{2,1,0:T(4,128)(2,1)S(1)} async-done(((bf16[128,4,1920]{2,1,0:T(4,128)(2,1)}), bf16[128,4,1920]{2,1,0:T(4,128)(2,1)S(1)}, u32[]{:S(2)}, u32[]{:S(2)}) %all-to-all-start) | async-done | bytes 1966112 | tf_op jit(solution)/shard_map/all_to_all | solution.py:425
  45.9 6.9 %attend.1 = (bf16[128,4,1920]{2,1,0:T(4,128)(2,1)}, bf16[128,640]{1,0:T(8,128)(2,1)}, bf16[128,640]{1,0:T(8,128)(2,1)}, bf16[2,128,640]{2,1,0:T(8,128)(2,1)}) custom-call(s32[1]{0:T(128)} %bitcast.me_ref, f32[512,128]{1,0:T(8,128)S(1)} %get-tuple-element.19.bias_ref, f32[8,512]{1,0:T(8,128)S(1)} %get-tuple-element.20.live_ref, ...), custom_call_target="tpu_custom_call" | custom-call | tf_op jit(solution)/shard_map/attend/pallas_call | solution.py:400
  52.9 5.3 %all-to-all-start.1 = ((bf16[128,4,1920]{2,1,0:T(4,128)(2,1)}), bf16[128,4,1920]{2,1,0:T(4,128)(2,1)S(1)}, u32[]{:S(2)}, u32[]{:S(2)}) async-start(bf16[128,4,1920]{2,1,0:T(4,128)(2,1)} %get-tuple-element.28), calls=%async_computation.1 | async-start | bytes 3932160 | tf_op jit(solution)/shard_map/all_to_all | solution.py:425
  58.3 3.1 %collective-permute-done.4.far_ref = bf16[2,128,640]{2,1,0:T(8,128)(2,1)S(1)} collective-permute-done((bf16[2,128,640]{2,1,0:T(8,128)(2,1)}, bf16[2,128,640]{2,1,0:T(8,128)(2,1)S(1)}, u32[]{:S(2)}, u32[]{:S(2)}) %collective-permute-start.4) | collective-permute-done | bytes 327712 | tf_op jit(solution)/shard_map/ppermute | solution.py:429
  61.4 3.2 %collective-permute-start.5 = (bf16[2,128,640]{2,1,0:T(8,128)(2,1)S(1)}, bf16[2,128,640]{2,1,0:T(8,128)(2,1)S(1)}, u32[]{:S(2)}, u32[]{:S(2)}) collective-permute-start(bf16[2,128,640]{2,1,0:T(8,128)(2,1)S(1)} %collective-permute-done.4.far_ref), channel_id=1, source_target_pairs={{0,1},{1,0},{2,3},{3,2},{4,5},{5,4},{6,7},{7,6},{8,9},{9,8},{10,11... | collective-permute-start | bytes 983048 | tf_op jit(solution)/shard_map/ppermute | solution.py:429
  64.6 1.5 %collective-permute-done.3.i1_ref = bf16[128,640]{1,0:T(8,128)(2,1)S(1)} collective-permute-done((bf16[128,640]{1,0:T(8,128)(2,1)S(1)}, bf16[128,640]{1,0:T(8,128)(2,1)S(1)}, u32[]{:S(2)}, u32[]{:S(2)}) %collective-permute-start.3) | collective-permute-done | bytes 163872 | tf_op jit(solution)/shard_map/ppermute | solution.py:429
  66.1 2.0 %collect.1 = bf16[128,2560]{1,0:T(8,128)(2,1)} custom-call(s32[1]{0:T(128)} %bitcast.me_ref, s32[32]{0:T(128)S(1)} %copy-done.13, s32[32]{0:T(128)S(1)} %copy-done.15, f32[8,20]{1,0:T(8,128)S(1)} %copy-done.10, s32[128,128]{1,0:T(8,128)S(1)} %bitcast.7, bf16[128,640]{1,0:T(8,128)(2,1)S(1)} %copy-done.8, bf16[128,640]{1,0:T(8,128)(2,1)S(1)} %collective-permute-done.3.i1_ref, ...), custom_call_target="tpu_custom_call" | custom-call | flops 15000000512 | bytes 50000000 | tf_op jit(solution)/shard_map/collect/pallas_call | solution.py:388
  68.1 19.3 %all-to-all-done.1 = bf16[128,4,1920]{2,1,0:T(4,128)(2,1)S(1)} async-done(((bf16[128,4,1920]{2,1,0:T(4,128)(2,1)}), bf16[128,4,1920]{2,1,0:T(4,128)(2,1)S(1)}, u32[]{:S(2)}, u32[]{:S(2)}) %all-to-all-start.1) | async-done | bytes 1966112 | tf_op jit(solution)/shard_map/all_to_all | solution.py:425
  87.4 1.6 %unpack.1 = (bf16[128,2560]{1,0:T(8,128)(2,1)}, bf16[128,2560]{1,0:T(8,128)(2,1)}, bf16[128,2560]{1,0:T(8,128)(2,1)}) custom-call(bf16[128,128]{1,0:T(8,128)(2,1)S(1)} %copy-done.3, bf16[32,4,4,1920]{3,2,1,0:T(4,128)(2,1)S(1)} %bitcast.4), custom_call_target="tpu_custom_call" | custom-call | tf_op jit(solution)/shard_map/unpack/pallas_call | solution.py:349
  (32 shorter events, 0.9 us)
Async XLA Ops:
  3.9 12.8 %collective-permute-start.1 = (bf16[2,128,640]{2,1,0:T(8,128)(2,1)S(1)}, bf16[2,128,640]{2,1,0:T(8,128)(2,1)S(1)}, u32[]{:S(2)}, u32[]{:S(2)}) collective-permute-start(bf16[2,128,640]{2,1,0:T(8,128)(2,1)S(1)} %get-tuple-element.18), channel_id=1, source_target_pairs={{0,2},{1,3},{2,0},{3,1},{4,6},{5,7},{6,4},{7,5},{8,10},{9,11},{10,... | collective-permute-start | bytes 983048 | tf_op jit(solution)/shard_map/ppermute | solution.py:429
  6.1 39.8 %all-to-all-start = ((bf16[128,4,1920]{2,1,0:T(4,128)(2,1)}), bf16[128,4,1920]{2,1,0:T(4,128)(2,1)S(1)}, u32[]{:S(2)}, u32[]{:S(2)}) async-start(bf16[128,4,1920]{2,1,0:T(4,128)(2,1)} %bitcast.8), calls=%async_computation | async-start | bytes 3932160 | tf_op jit(solution)/shard_map/all_to_all | solution.py:425
  16.7 3.6 %copy-start.4 = (bf16[2,128,640]{2,1,0:T(8,128)(2,1)}, bf16[2,128,640]{2,1,0:T(8,128)(2,1)S(1)}, u32[]{:S(2)}) copy-start(bf16[2,128,640]{2,1,0:T(8,128)(2,1)S(1)} %collective-permute-done.1.far_ref) | copy-start | bytes 983044
  16.7 3.6 %collective-permute-start.2 = (bf16[2,128,640]{2,1,0:T(8,128)(2,1)S(1)}, bf16[2,128,640]{2,1,0:T(8,128)(2,1)S(1)}, u32[]{:S(2)}, u32[]{:S(2)}) collective-permute-start(bf16[2,128,640]{2,1,0:T(8,128)(2,1)S(1)} %collective-permute-done.1.far_ref), channel_id=1, source_target_pairs={{0,1},{1,0},{2,3},{3,2},{4,5},{5,4},{6,7},{7,6},{8,9},{9,8},{10,11... | collective-permute-start | bytes 983048 | tf_op jit(solution)/shard_map/ppermute | solution.py:429
  18.8 1.5 %collective-permute-start = (bf16[128,640]{1,0:T(8,128)(2,1)S(1)}, bf16[128,640]{1,0:T(8,128)(2,1)S(1)}, u32[]{:S(2)}, u32[]{:S(2)}) collective-permute-start(bf16[128,640]{1,0:T(8,128)(2,1)S(1)} %constant_dynamic-slice_fusion), channel_id=1, source_target_pairs={{0,1},{1,0},{2,3},{3,2},{4,5},{5,4},{6,7},{7,6},{8,9},{9,8},{10,11... | collective-permute-start | bytes 491528 | tf_op jit(solution)/shard_map/ppermute | solution.py:429
  20.3 0.7 copy-start.6
  21.0 0.8 copy-start
  21.9 1.0 %copy-start.5 = (bf16[2,128,640]{2,1,0:T(8,128)(2,1)S(1)}, bf16[2,128,640]{2,1,0:T(8,128)(2,1)}, u32[]{:S(2)}) copy-start(bf16[2,128,640]{2,1,0:T(8,128)(2,1)} %copy-done.4) | copy-start | bytes 983044
  22.8 1.0 %copy-start.7 = (bf16[2,128,640]{2,1,0:T(8,128)(2,1)S(1)}, bf16[2,128,640]{2,1,0:T(8,128)(2,1)}, u32[]{:S(2)}) copy-start(bf16[2,128,640]{2,1,0:T(8,128)(2,1)} %copy-done.6) | copy-start | bytes 983044
  23.8 0.7 copy-start.9
  24.5 0.7 copy-start.11
  25.2 0.7 copy-start.12
  25.8 0.7 copy-start.14
  52.8 8.6 %collective-permute-start.4 = (bf16[2,128,640]{2,1,0:T(8,128)(2,1)}, bf16[2,128,640]{2,1,0:T(8,128)(2,1)S(1)}, u32[]{:S(2)}, u32[]{:S(2)}) collective-permute-start(bf16[2,128,640]{2,1,0:T(8,128)(2,1)} %get-tuple-element.26), channel_id=1, source_target_pairs={{0,2},{1,3},{2,0},{3,1},{4,6},{5,7},{6,4},{7,5},{8,10},{9,11},{10,... | collective-permute-start | bytes 983048 | tf_op jit(solution)/shard_map/ppermute | solution.py:429
  52.9 11.7 %copy-start.16 = (bf16[128,640]{1,0:T(8,128)(2,1)S(1)}, bf16[128,640]{1,0:T(8,128)(2,1)}, u32[]{:S(2)}) copy-start(bf16[128,640]{1,0:T(8,128)(2,1)} %get-tuple-element.25) | copy-start | bytes 491524
  52.9 13.2 %copy-start.1 = (s32[16384]{0:T(1024)S(1)}, s32[16384]{0:T(1024)}, u32[]{:S(2)}) copy-start(s32[16384]{0:T(1024)} %param.17) | copy-start | bytes 196612
  52.9 13.2 %copy-start.8 = (bf16[128,640]{1,0:T(8,128)(2,1)S(1)}, bf16[128,640]{1,0:T(8,128)(2,1)}, u32[]{:S(2)}) copy-start(bf16[128,640]{1,0:T(8,128)(2,1)} %get-tuple-element.24.i0_ref) | copy-start | bytes 491524
  52.9 13.2 %copy-start.10 = (f32[8,20]{1,0:T(8,128)S(1)}, f32[8,20]{1,0:T(8,128)}, u32[]{:S(2)}) copy-start(f32[8,20]{1,0:T(8,128)} %guide_ref.3) | copy-start | bytes 1924
  52.9 13.2 %copy-start.13 = (s32[32]{0:T(128)S(1)}, s32[32]{0:T(128)}, u32[]{:S(2)}) copy-start(s32[32]{0:T(128)} %plan_ref.3) | copy-start | bytes 388
  52.9 13.2 %copy-start.15 = (s32[32]{0:T(128)S(1)}, s32[32]{0:T(128)}, u32[]{:S(2)}) copy-start(s32[32]{0:T(128)} %bins_ref.3) | copy-start | bytes 388
  52.9 34.5 %all-to-all-start.1 = ((bf16[128,4,1920]{2,1,0:T(4,128)(2,1)}), bf16[128,4,1920]{2,1,0:T(4,128)(2,1)S(1)}, u32[]{:S(2)}, u32[]{:S(2)}) async-start(bf16[128,4,1920]{2,1,0:T(4,128)(2,1)} %get-tuple-element.28), calls=%async_computation.1 | async-start | bytes 3932160 | tf_op jit(solution)/shard_map/all_to_all | solution.py:425
  61.4 4.7 %collective-permute-start.5 = (bf16[2,128,640]{2,1,0:T(8,128)(2,1)S(1)}, bf16[2,128,640]{2,1,0:T(8,128)(2,1)S(1)}, u32[]{:S(2)}, u32[]{:S(2)}) collective-permute-start(bf16[2,128,640]{2,1,0:T(8,128)(2,1)S(1)} %collective-permute-done.4.far_ref), channel_id=1, source_target_pairs={{0,1},{1,0},{2,3},{3,2},{4,5},{5,4},{6,7},{7,6},{8,9},{9,8},{10,11... | collective-permute-start | bytes 983048 | tf_op jit(solution)/shard_map/ppermute | solution.py:429
  64.6 1.5 %collective-permute-start.3 = (bf16[128,640]{1,0:T(8,128)(2,1)S(1)}, bf16[128,640]{1,0:T(8,128)(2,1)S(1)}, u32[]{:S(2)}, u32[]{:S(2)}) collective-permute-start(bf16[128,640]{1,0:T(8,128)(2,1)S(1)} %copy-done.16), channel_id=1, source_target_pairs={{0,1},{1,0},{2,3},{3,2},{4,5},{5,4},{6,7},{7,6},{8,9},{9,8},{10,11... | collective-permute-start | bytes 491528 | tf_op jit(solution)/shard_map/ppermute | solution.py:429
  66.1 21.3 %copy-start.3 = (bf16[128,128]{1,0:T(8,128)(2,1)S(1)}, bf16[128,128]{1,0:T(8,128)(2,1)}, u32[]{:S(2)}) copy-start(bf16[128,128]{1,0:T(8,128)(2,1)} %copy-done.2) | copy-start | bytes 98308
  (1 other events, 0.6 us)

commit v9 on v8

--- a/solution.py
+++ b/solution.py
@@ -128,13 +128,10 @@
         for part in range(N_SP):
             rows = recv_ref[:, part, :, pl.ds(array * PART, PART)].reshape(ROWS, PART)
             out_ref[array, :, pl.ds(part * PART, PART)] = dot(pick, rows).astype(BF)
-            if part % 2 == 1:
-                lanes = pl.ds((part - 1) * PART, 2 * PART)
-                store = pltpu.make_async_copy(
-                    out_ref.at[array, :, lanes], ref.at[:, lanes], out_sem.at[array, part // 2]
-                )
-                store.start()
-                stores.append(store)
+            lanes = pl.ds(part * PART, PART)
+            store = pltpu.make_async_copy(out_ref.at[array, :, lanes], ref.at[:, lanes], out_sem.at[array, part])
+            store.start()
+            stores.append(store)
     for store in stores:
         store.wait()
 
@@ -353,7 +350,7 @@
         out_specs=(HBM,) * 3,
         scratch_shapes=[
             pltpu.VMEM((3, ROWS, WIDTH), BF),
-            pltpu.SemaphoreType.DMA((3, 2)),
+            pltpu.SemaphoreType.DMA((3, N_SP)),
         ],
         compiler_params=PARAMS,
         name="unpack",

time: 89.5 us -> 89.5 us (level)
  no operation moved by 1% of the time
where the time goes in v9:
time: 89.5 us; the launch traced here: 89 us
  waiting for transfers between devices  41.6 us (46%)
  starting transfers between devices  22.7 us (25%)
  Pallas kernels  16.2 us (18%)
  local copies, waits for them, and re-layouts  7.74 us (9%)
    all_to_all x2, waiting for transfers between devices, exchange(): lax.all_to_all(chunks, ('dp', 'sp'), split_axis=0, concat_axis=0, tiled=T...  35.6 us
    all_to_all x2, starting transfers between devices, exchange(): lax.all_to_all(chunks, ('dp', 'sp'), split_axis=0, concat_axis=0, tiled=T...  16 us
    pallas_call x1, Pallas kernels, attend(): pl.pallas_call(attend_kernel, out_shape=(pltpu.HBM((LOADERS, 4, CHUNK), B...  6.88 us
    unnamed x34, local copies, waits for them, and re-layouts  6.81 us
    ppermute x6, starting transfers between devices, swap(): return lax.ppermute(piece, 'sp', [(i, i ^ step) for i in range(N_SP)])  6.71 us
    ppermute x6, waiting for transfers between devices, swap(): return lax.ppermute(piece, 'sp', [(i, i ^ step) for i in range(N_SP)])  5.97 us
    pallas_call x1, Pallas kernels, pack(): pl.pallas_call(pack_kernel, out_shape=(pltpu.HBM((N_DP, N_SP, 4, CHUNK),...  3.3 us
    pallas_call x1, Pallas kernels, prepare(): pl.pallas_call(prepare_kernel, out_shape=(jax.ShapeDtypeStruct((GROUP, PA...  2.53 us
  transfers between devices with their start and end apart: 8, of which 5 were waited for; matrix products, arithmetic and copies ran while one was open for 1% of the time, Pallas kernels for 5%

profile of v9, /device:TPU:1, one launch (start us, length us, event | category | flops | bytes accessed | tf_op | source)
XLA Modules:
  0.0 89.0 jit_solution(2620901871061619181)
XLA Ops:
  0.6 3.3 %pack.1 = (bf16[32,4,4,1920]{3,2,1,0:T(4,128)(2,1)}, bf16[2,128,640]{2,1,0:T(8,128)(2,1)S(1)}) custom-call(s32[1]{0:T(128)} %bitcast.me_ref, s32[128,128]{1,0:T(8,128)} %bitcast.5, bf16[128,2560]{1,0:T(8,128)(2,1)} %q_ref.1, bf16[128,2560]{1,0:T(8,128)(2,1)} %k_ref.1, bf16[128,2560]{1,0:T(8,128)(2,1)} %v_ref.1, bf16[128,2560]{1,0:T(8,128)(2,1)} %cot_ref.3), custom_call_target="tpu_custom_call" | custom-call | tf_op jit(solution)/shard_map/pack/pallas_call | solution.py:325
  3.9 2.1 %collective-permute-start.1 = (bf16[2,128,640]{2,1,0:T(8,128)(2,1)S(1)}, bf16[2,128,640]{2,1,0:T(8,128)(2,1)S(1)}, u32[]{:S(2)}, u32[]{:S(2)}) collective-permute-start(bf16[2,128,640]{2,1,0:T(8,128)(2,1)S(1)} %get-tuple-element.18), channel_id=1, source_target_pairs={{0,2},{1,3},{2,0},{3,1},{4,6},{5,7},{6,4},{7,5},{8,10},{9,11},{10,... | collective-permute-start | bytes 983048 | tf_op jit(solution)/shard_map/ppermute | solution.py:426
  6.1 10.7 %all-to-all-start = ((bf16[128,4,1920]{2,1,0:T(4,128)(2,1)}), bf16[128,4,1920]{2,1,0:T(4,128)(2,1)S(1)}, u32[]{:S(2)}, u32[]{:S(2)}) async-start(bf16[128,4,1920]{2,1,0:T(4,128)(2,1)} %bitcast.8), calls=%async_computation | async-start | bytes 3932160 | tf_op jit(solution)/shard_map/all_to_all | solution.py:422
  16.7 1.1 %collective-permute-start.2 = (bf16[2,128,640]{2,1,0:T(8,128)(2,1)S(1)}, bf16[2,128,640]{2,1,0:T(8,128)(2,1)S(1)}, u32[]{:S(2)}, u32[]{:S(2)}) collective-permute-start(bf16[2,128,640]{2,1,0:T(8,128)(2,1)S(1)} %collective-permute-done.1.far_ref), channel_id=1, source_target_pairs={{0,1},{1,0},{2,3},{3,2},{4,5},{5,4},{6,7},{7,6},{8,9},{9,8},{10,11... | collective-permute-start | bytes 983048 | tf_op jit(solution)/shard_map/ppermute | solution.py:426
  17.9 0.9 %constant_dynamic-slice_fusion = bf16[128,640]{1,0:T(8,128)(2,1)S(1)} fusion(bf16[128,2560]{1,0:T(8,128)(2,1)} %cot_ref.3, s32[]{:T(128)S(6)} %select_n.3), kind=kLoop, calls=%fused_computation | loop fusion | bytes 327684 | tf_op jit(solution)/shard_map/dynamic_slice | solution.py:449
  18.9 1.4 %collective-permute-done.near_ref = bf16[128,640]{1,0:T(8,128)(2,1)S(1)} collective-permute-done((bf16[128,640]{1,0:T(8,128)(2,1)S(1)}, bf16[128,640]{1,0:T(8,128)(2,1)S(1)}, u32[]{:S(2)}, u32[]{:S(2)}) %collective-permute-start) | collective-permute-done | bytes 163872 | tf_op jit(solution)/shard_map/ppermute | solution.py:426
  20.3 0.7 copy-done.6
  21.0 0.8 copy-done
  21.9 1.0 %copy-done.5 = bf16[2,128,640]{2,1,0:T(8,128)(2,1)S(1)} copy-done((bf16[2,128,640]{2,1,0:T(8,128)(2,1)S(1)}, bf16[2,128,640]{2,1,0:T(8,128)(2,1)}, u32[]{:S(2)}) %copy-start.5) | copy-done | bytes 327704
  22.9 1.0 %copy-done.7 = bf16[2,128,640]{2,1,0:T(8,128)(2,1)S(1)} copy-done((bf16[2,128,640]{2,1,0:T(8,128)(2,1)S(1)}, bf16[2,128,640]{2,1,0:T(8,128)(2,1)}, u32[]{:S(2)}) %copy-start.7) | copy-done | bytes 327704
  23.8 0.7 copy-done.9
  24.5 0.7 copy-done.11
  25.2 0.7 copy-done.12
  25.8 0.7 copy-done.14
  26.5 2.5 %prepare.1 = (bf16[512,640]{1,0:T(8,128)(2,1)S(1)}, bf16[640,512]{1,0:T(8,128)(2,1)S(1)}, f32[512,128]{1,0:T(8,128)S(1)}, f32[8,512]{1,0:T(8,128)S(1)}, bf16[128,128]{1,0:T(8,128)(2,1)S(1)}) custom-call(s32[1]{0:T(128)} %bitcast.me_ref, s32[32]{0:T(128)S(1)} %copy-done.11, s32[32]{0:T(128)S(1)} %copy-done.12, s32[32]{0:T(128)S(1)} %copy-done.14, ...), custom_call_target="tpu_custom_call" | custom-call | flops 15000000512 | bytes 50000000 | tf_op jit(solution)/shard_map/prepare/pallas_call | solution.py:361
  29.6 16.3 %all-to-all-done.recv_ref = bf16[128,4,1920]{2,1,0:T(4,128)(2,1)S(1)} async-done(((bf16[128,4,1920]{2,1,0:T(4,128)(2,1)}), bf16[128,4,1920]{2,1,0:T(4,128)(2,1)S(1)}, u32[]{:S(2)}, u32[]{:S(2)}) %all-to-all-start) | async-done | bytes 1966112 | tf_op jit(solution)/shard_map/all_to_all | solution.py:422
  45.9 6.9 %attend.1 = (bf16[128,4,1920]{2,1,0:T(4,128)(2,1)}, bf16[128,640]{1,0:T(8,128)(2,1)}, bf16[128,640]{1,0:T(8,128)(2,1)}, bf16[2,128,640]{2,1,0:T(8,128)(2,1)}) custom-call(s32[1]{0:T(128)} %bitcast.me_ref, f32[512,128]{1,0:T(8,128)S(1)} %get-tuple-element.19.bias_ref, f32[8,512]{1,0:T(8,128)S(1)} %get-tuple-element.20.live_ref, ...), custom_call_target="tpu_custom_call" | custom-call | tf_op jit(solution)/shard_map/attend/pallas_call | solution.py:397
  52.9 5.3 %all-to-all-start.1 = ((bf16[128,4,1920]{2,1,0:T(4,128)(2,1)}), bf16[128,4,1920]{2,1,0:T(4,128)(2,1)S(1)}, u32[]{:S(2)}, u32[]{:S(2)}) async-start(bf16[128,4,1920]{2,1,0:T(4,128)(2,1)} %get-tuple-element.28), calls=%async_computation.1 | async-start | bytes 3932160 | tf_op jit(solution)/shard_map/all_to_all | solution.py:422
  58.3 3.1 %collective-permute-done.4.far_ref = bf16[2,128,640]{2,1,0:T(8,128)(2,1)S(1)} collective-permute-done((bf16[2,128,640]{2,1,0:T(8,128)(2,1)}, bf16[2,128,640]{2,1,0:T(8,128)(2,1)S(1)}, u32[]{:S(2)}, u32[]{:S(2)}) %collective-permute-start.4) | collective-permute-done | bytes 327712 | tf_op jit(solution)/shard_map/ppermute | solution.py:426
  61.4 3.2 %collective-permute-start.5 = (bf16[2,128,640]{2,1,0:T(8,128)(2,1)S(1)}, bf16[2,128,640]{2,1,0:T(8,128)(2,1)S(1)}, u32[]{:S(2)}, u32[]{:S(2)}) collective-permute-start(bf16[2,128,640]{2,1,0:T(8,128)(2,1)S(1)} %collective-permute-done.4.far_ref), channel_id=1, source_target_pairs={{0,1},{1,0},{2,3},{3,2},{4,5},{5,4},{6,7},{7,6},{8,9},{9,8},{10,11... | collective-permute-start | bytes 983048 | tf_op jit(solution)/shard_map/ppermute | solution.py:426
  64.6 1.5 %collective-permute-done.3.i1_ref = bf16[128,640]{1,0:T(8,128)(2,1)S(1)} collective-permute-done((bf16[128,640]{1,0:T(8,128)(2,1)S(1)}, bf16[128,640]{1,0:T(8,128)(2,1)S(1)}, u32[]{:S(2)}, u32[]{:S(2)}) %collective-permute-start.3) | collective-permute-done | bytes 163872 | tf_op jit(solution)/shard_map/ppermute | solution.py:426
  66.1 2.0 %collect.1 = bf16[128,2560]{1,0:T(8,128)(2,1)} custom-call(s32[1]{0:T(128)} %bitcast.me_ref, s32[32]{0:T(128)S(1)} %copy-done.13, s32[32]{0:T(128)S(1)} %copy-done.15, f32[8,20]{1,0:T(8,128)S(1)} %copy-done.10, s32[128,128]{1,0:T(8,128)S(1)} %bitcast.7, bf16[128,640]{1,0:T(8,128)(2,1)S(1)} %copy-done.8, bf16[128,640]{1,0:T(8,128)(2,1)S(1)} %collective-permute-done.3.i1_ref, ...), custom_call_target="tpu_custom_call" | custom-call | flops 15000000512 | bytes 50000000 | tf_op jit(solution)/shard_map/collect/pallas_call | solution.py:385
  68.1 19.3 %all-to-all-done.1 = bf16[128,4,1920]{2,1,0:T(4,128)(2,1)S(1)} async-done(((bf16[128,4,1920]{2,1,0:T(4,128)(2,1)}), bf16[128,4,1920]{2,1,0:T(4,128)(2,1)S(1)}, u32[]{:S(2)}, u32[]{:S(2)}) %all-to-all-start.1) | async-done | bytes 1966112 | tf_op jit(solution)/shard_map/all_to_all | solution.py:422
  87.4 1.6 %unpack.1 = (bf16[128,2560]{1,0:T(8,128)(2,1)}, bf16[128,2560]{1,0:T(8,128)(2,1)}, bf16[128,2560]{1,0:T(8,128)(2,1)}) custom-call(bf16[128,128]{1,0:T(8,128)(2,1)S(1)} %copy-done.3, bf16[32,4,4,1920]{3,2,1,0:T(4,128)(2,1)S(1)} %bitcast.4), custom_call_target="tpu_custom_call" | custom-call | tf_op jit(solution)/shard_map/unpack/pallas_call | solution.py:346
  (32 shorter events, 0.9 us)
Async XLA Ops:
  3.9 12.8 %collective-permute-start.1 = (bf16[2,128,640]{2,1,0:T(8,128)(2,1)S(1)}, bf16[2,128,640]{2,1,0:T(8,128)(2,1)S(1)}, u32[]{:S(2)}, u32[]{:S(2)}) collective-permute-start(bf16[2,128,640]{2,1,0:T(8,128)(2,1)S(1)} %get-tuple-element.18), channel_id=1, source_target_pairs={{0,2},{1,3},{2,0},{3,1},{4,6},{5,7},{6,4},{7,5},{8,10},{9,11},{10,... | collective-permute-start | bytes 983048 | tf_op jit(solution)/shard_map/ppermute | solution.py:426
  6.1 39.8 %all-to-all-start = ((bf16[128,4,1920]{2,1,0:T(4,128)(2,1)}), bf16[128,4,1920]{2,1,0:T(4,128)(2,1)S(1)}, u32[]{:S(2)}, u32[]{:S(2)}) async-start(bf16[128,4,1920]{2,1,0:T(4,128)(2,1)} %bitcast.8), calls=%async_computation | async-start | bytes 3932160 | tf_op jit(solution)/shard_map/all_to_all | solution.py:422
  16.7 3.6 %copy-start.4 = (bf16[2,128,640]{2,1,0:T(8,128)(2,1)}, bf16[2,128,640]{2,1,0:T(8,128)(2,1)S(1)}, u32[]{:S(2)}) copy-start(bf16[2,128,640]{2,1,0:T(8,128)(2,1)S(1)} %collective-permute-done.1.far_ref) | copy-start | bytes 983044
  16.7 3.6 %collective-permute-start.2 = (bf16[2,128,640]{2,1,0:T(8,128)(2,1)S(1)}, bf16[2,128,640]{2,1,0:T(8,128)(2,1)S(1)}, u32[]{:S(2)}, u32[]{:S(2)}) collective-permute-start(bf16[2,128,640]{2,1,0:T(8,128)(2,1)S(1)} %collective-permute-done.1.far_ref), channel_id=1, source_target_pairs={{0,1},{1,0},{2,3},{3,2},{4,5},{5,4},{6,7},{7,6},{8,9},{9,8},{10,11... | collective-permute-start | bytes 983048 | tf_op jit(solution)/shard_map/ppermute | solution.py:426
  18.8 1.5 %collective-permute-start = (bf16[128,640]{1,0:T(8,128)(2,1)S(1)}, bf16[128,640]{1,0:T(8,128)(2,1)S(1)}, u32[]{:S(2)}, u32[]{:S(2)}) collective-permute-start(bf16[128,640]{1,0:T(8,128)(2,1)S(1)} %constant_dynamic-slice_fusion), channel_id=1, source_target_pairs={{0,1},{1,0},{2,3},{3,2},{4,5},{5,4},{6,7},{7,6},{8,9},{9,8},{10,11... | collective-permute-start | bytes 491528 | tf_op jit(solution)/shard_map/ppermute | solution.py:426
  20.3 0.7 copy-start.6
  21.0 0.8 copy-start
  21.9 1.0 %copy-start.5 = (bf16[2,128,640]{2,1,0:T(8,128)(2,1)S(1)}, bf16[2,128,640]{2,1,0:T(8,128)(2,1)}, u32[]{:S(2)}) copy-start(bf16[2,128,640]{2,1,0:T(8,128)(2,1)} %copy-done.4) | copy-start | bytes 983044
  22.8 1.0 %copy-start.7 = (bf16[2,128,640]{2,1,0:T(8,128)(2,1)S(1)}, bf16[2,128,640]{2,1,0:T(8,128)(2,1)}, u32[]{:S(2)}) copy-start(bf16[2,128,640]{2,1,0:T(8,128)(2,1)} %copy-done.6) | copy-start | bytes 983044
  23.8 0.7 copy-start.9
  24.5 0.7 copy-start.11
  25.2 0.7 copy-start.12
  25.8 0.7 copy-start.14
  52.8 8.6 %collective-permute-start.4 = (bf16[2,128,640]{2,1,0:T(8,128)(2,1)}, bf16[2,128,640]{2,1,0:T(8,128)(2,1)S(1)}, u32[]{:S(2)}, u32[]{:S(2)}) collective-permute-start(bf16[2,128,640]{2,1,0:T(8,128)(2,1)} %get-tuple-element.26), channel_id=1, source_target_pairs={{0,2},{1,3},{2,0},{3,1},{4,6},{5,7},{6,4},{7,5},{8,10},{9,11},{10,... | collective-permute-start | bytes 983048 | tf_op jit(solution)/shard_map/ppermute | solution.py:426
  52.9 11.7 %copy-start.16 = (bf16[128,640]{1,0:T(8,128)(2,1)S(1)}, bf16[128,640]{1,0:T(8,128)(2,1)}, u32[]{:S(2)}) copy-start(bf16[128,640]{1,0:T(8,128)(2,1)} %get-tuple-element.25) | copy-start | bytes 491524
  52.9 13.2 %copy-start.1 = (s32[16384]{0:T(1024)S(1)}, s32[16384]{0:T(1024)}, u32[]{:S(2)}) copy-start(s32[16384]{0:T(1024)} %param.17) | copy-start | bytes 196612
  52.9 13.2 %copy-start.8 = (bf16[128,640]{1,0:T(8,128)(2,1)S(1)}, bf16[128,640]{1,0:T(8,128)(2,1)}, u32[]{:S(2)}) copy-start(bf16[128,640]{1,0:T(8,128)(2,1)} %get-tuple-element.24.i0_ref) | copy-start | bytes 491524
  52.9 13.2 %copy-start.10 = (f32[8,20]{1,0:T(8,128)S(1)}, f32[8,20]{1,0:T(8,128)}, u32[]{:S(2)}) copy-start(f32[8,20]{1,0:T(8,128)} %guide_ref.3) | copy-start | bytes 1924
  52.9 13.2 %copy-start.13 = (s32[32]{0:T(128)S(1)}, s32[32]{0:T(128)}, u32[]{:S(2)}) copy-start(s32[32]{0:T(128)} %plan_ref.3) | copy-start | bytes 388
  52.9 13.2 %copy-start.15 = (s32[32]{0:T(128)S(1)}, s32[32]{0:T(128)}, u32[]{:S(2)}) copy-start(s32[32]{0:T(128)} %bins_ref.3) | copy-start | bytes 388
  52.9 34.5 %all-to-all-start.1 = ((bf16[128,4,1920]{2,1,0:T(4,128)(2,1)}), bf16[128,4,1920]{2,1,0:T(4,128)(2,1)S(1)}, u32[]{:S(2)}, u32[]{:S(2)}) async-start(bf16[128,4,1920]{2,1,0:T(4,128)(2,1)} %get-tuple-element.28), calls=%async_computation.1 | async-start | bytes 3932160 | tf_op jit(solution)/shard_map/all_to_all | solution.py:422
  61.4 4.7 %collective-permute-start.5 = (bf16[2,128,640]{2,1,0:T(8,128)(2,1)S(1)}, bf16[2,128,640]{2,1,0:T(8,128)(2,1)S(1)}, u32[]{:S(2)}, u32[]{:S(2)}) collective-permute-start(bf16[2,128,640]{2,1,0:T(8,128)(2,1)S(1)} %collective-permute-done.4.far_ref), channel_id=1, source_target_pairs={{0,1},{1,0},{2,3},{3,2},{4,5},{5,4},{6,7},{7,6},{8,9},{9,8},{10,11... | collective-permute-start | bytes 983048 | tf_op jit(solution)/shard_map/ppermute | solution.py:426
  64.6 1.5 %collective-permute-start.3 = (bf16[128,640]{1,0:T(8,128)(2,1)S(1)}, bf16[128,640]{1,0:T(8,128)(2,1)S(1)}, u32[]{:S(2)}, u32[]{:S(2)}) collective-permute-start(bf16[128,640]{1,0:T(8,128)(2,1)S(1)} %copy-done.16), channel_id=1, source_target_pairs={{0,1},{1,0},{2,3},{3,2},{4,5},{5,4},{6,7},{7,6},{8,9},{9,8},{10,11... | collective-permute-start | bytes 491528 | tf_op jit(solution)/shard_map/ppermute | solution.py:426
  66.1 21.3 %copy-start.3 = (bf16[128,128]{1,0:T(8,128)(2,1)S(1)}, bf16[128,128]{1,0:T(8,128)(2,1)}, u32[]{:S(2)}) copy-start(bf16[128,128]{1,0:T(8,128)(2,1)} %copy-done.2) | copy-start | bytes 98308
  (1 other events, 0.6 us)
